TPU v7x, 32 devices: a whole 2x2x4 slice. The times are simulated.
32 devices in a mesh: cell: 16 (over z, x, core), mode: 2 (over y).
Axes of the slice: x: 2, y: 2, z: 4, core: 2. Of those that a mesh axis runs over, the one named last changes fastest.
Arguments:
- pod_modes: bfloat16 [3, 512, 4, 32, 128], P(None, 'mode', None, 'cell'), may hold values from -6 to 6
- slab_map: int32 [4, 32, 128], P(None, 'cell'), may hold values from 0 to 7
- slab_volume: float32 [8], replicated, may hold values from 0.25 to 4
- advect_index: int32 [8], replicated, may hold values from 0 to 511, as said below
- pair_adv: int32 [2048], replicated, may hold values from 0 to 7
- pair_mode: int32 [2048], replicated, may hold values from 0 to 511
- pair_amp: float32 [2048, 1024], replicated, may hold values from -0.2 to 0.2
Outputs:
- convective: float32 [512, 8, 512], P(('mode', 'cell'))
- response: float32 [512, 1024], P(('mode', 'cell'))
Inputs may be any that keep to these rules, and one draw needn't show every extreme that they name: `advect_index`: 8 distinct mode indices.
All inputs are finite; a program needn't handle non-finite values.
Results may differ from a plain program's by a relative error of at most 0.0043.
Values may be sent and summed in bfloat16 or wider, within the bound.
No kernel may reach another device: no remote copies, remote signals or barrier semaphores. Data moves between devices by JAX's collectives and lax.ppermute only.
A program may use at most 128 MiB of HBM per device.

v0:
```python
import jax
import jax.numpy as jnp
from jax import lax
from jax.sharding import PartitionSpec as P


def padded(x, sides, width):
    for axis, dim in sides:
        size, length = (lax.axis_size(axis), x.shape[dim])
        up = [(i, (i + 1) % size) for i in range(size - 1)]
        down = [(j, i) for i, j in up]
        last = lax.slice_in_dim(x, length - width, length, axis=dim)
        first = lax.slice_in_dim(x, 0, width, axis=dim)
        before = lax.ppermute(last, axis, up)
        after = lax.ppermute(first, axis, down)
        x = jnp.concatenate([before, x, after], axis=dim)
    return x


def from_behind(block, axis, distance):
    devices = range(lax.axis_size(axis))
    route = [((i - distance) % len(devices), i) for i in devices]
    return lax.ppermute(block, axis, route)


def gradients(haloed):
    interior = haloed[:, :, :, 1:-1].astype(jnp.float32)
    along_x = 0.5 * (jnp.roll(interior, -1, axis=2) - jnp.roll(interior, 1, axis=2))
    along_y = 0.5 * (
        haloed[:, :, :, 2:].astype(jnp.float32) - haloed[:, :, :, :-2].astype(jnp.float32)
    )
    along_z = 0.5 * (jnp.roll(interior, -1, axis=4) - jnp.roll(interior, 1, axis=4))
    return jnp.stack([along_x, along_y, along_z]).astype(jnp.bfloat16)


def contract(left_factor, grads):
    return jnp.einsum("ijdcxyz,dckxyz->ijk", left_factor, grads, preferred_element_type=jnp.float32)


def owner_rows(partial_value):
    return lax.psum_scatter(partial_value, "cell", scatter_dimension=0, tiled=True)


def shards(pod_modes, slab_map, slab_volume, advect_index, pair_adv, pair_mode, pair_amp):
    mode_block = pod_modes.shape[1]
    planes = pod_modes.shape[2]
    rows_y = pod_modes.shape[3]
    cols_z = pod_modes.shape[4]
    mode_devs = lax.axis_size("mode")
    cell_devs = lax.axis_size("cell")
    mode_count = mode_block * mode_devs
    advect_count = advect_index.shape[0]
    scale_factor = float(planes * rows_y * cell_devs * cols_z) ** (-0.5)
    haloed = padded(pod_modes, (("cell", 3),), 1)
    all_modes = lax.all_gather(pod_modes, "mode", axis=1, tiled=True)
    chosen = jnp.take(all_modes, advect_index, axis=1).astype(jnp.float32)
    levels = slab_volume.shape[0]
    level_ids = lax.broadcasted_iota(jnp.int32, (levels, planes, rows_y, cols_z), 0)
    volume = jnp.sum(
        jnp.where(slab_map[None] == level_ids, slab_volume[:, None, None, None], 0.0), axis=0
    )
    weighted = chosen * volume[None, None]
    left_factor = (
        jnp.transpose(pod_modes, (1, 0, 2, 3, 4))[:, None, None, :].astype(jnp.float32)
        * jnp.transpose(weighted, (1, 0, 2, 3, 4))[None, :, :, None]
    ).astype(jnp.bfloat16)
    local_grads = gradients(haloed)
    own_index = lax.axis_index("mode")
    rows_here = mode_block // cell_devs
    result = jnp.zeros((rows_here, advect_count, mode_count), jnp.float32)

    def place(result, grads_now, step_index):
        source = (own_index - step_index) % mode_devs
        block_rows = owner_rows(contract(left_factor, grads_now))
        return lax.dynamic_update_slice_in_dim(result, block_rows, source * mode_block, 2)

    def advance(step_index, loop_state):
        result, grads_now = loop_state
        result = place(result, grads_now, step_index)
        grads_now = from_behind(grads_now, "mode", 1)
        return (result, grads_now)

    result, grads_now = lax.fori_loop(0, mode_devs - 1, advance, (result, local_grads))
    owned_rows = place(result, grads_now, mode_devs - 1)
    tensor = owned_rows * scale_factor
    flat_rows = tensor.reshape(tensor.shape[0], advect_count * mode_count)
    pair_slot = pair_adv * mode_count + pair_mode
    columns = jnp.take(flat_rows, pair_slot, axis=1)
    response = jnp.dot(
        columns, pair_amp, precision=lax.Precision.HIGHEST, preferred_element_type=jnp.float32
    )
    return (tensor, response)


def solution(mesh):
    in_specs = (P(None, "mode", None, "cell", None), P(None, "cell", None), P(), P(), P(), P(), P())
    out_specs = (P(("mode", "cell"), None, None), P(("mode", "cell"), None))
    return jax.shard_map(shards, mesh=mesh, in_specs=in_specs, out_specs=out_specs, check_vma=False)
```

profile of v0, /device:TPU:0, one launch (start us, length us, event | category | flops | bytes accessed | tf_op | source)
XLA Modules:
  0.0 267.6 jit_solution(10850033636865427567)
XLA Ops:
  7.2 0.0 all-gather.2.cloned.1.call-start
  7.2 4.0 %fusion.28 = (bf16[3,256,4,2,128]{4,1,3,2,0:T(8,128)(2,1)S(1)}, f32[3,256,4,2,128]{4,1,3,2,0:T(8,128)S(1)}, f32[256,3,4,2,128]{4,0,3,2,1:T(8,128)}) fusion(bf16[3,256,4,2,128]{4,3,2,1,0:T(2,128)(2,1)} %param.7), kind=kLoop, calls=%fused_computation.54 | loop fusion | flops 786432 | bytes 9437184 | tf_op args[0]
  11.3 1.1 copy-done
  12.4 1.3 fusion.27
  13.7 1.3 collective-permute-start
  15.0 4.0 %collective-permute-start.1 = (bf16[3,256,4,1,128]{4,1,3,2,0:T(8,128)(2,1)}, bf16[3,256,4,1,128]{4,1,3,2,0:T(8,128)(2,1)}, u32[]{:S(2)}, u32[]{:S(2)}) collective-permute-start(bf16[3,256,4,1,128]{4,1,3,2,0:T(8,128)(2,1)} %get-tuple-element.29), channel_id=1, source_target_pairs={{0,2},{2,4},{4,6},{6,8},{8,10},{10,12},{12,14},{14,16},{16,18},{18... | collective-permute-start | bytes 2359304 | tf_op jit(solution)/shard_map/ppermute | solution.py:14
  19.0 0.0 copy-done.6
  19.0 1.7 copy.74
  20.7 0.0 all-gather.2.cloned.1.call-update
  20.7 0.0 reduce-scatter.3.cloned.1.call-start
  20.8 2.7 slice_bitcast_fusion.2
  23.4 3.8 %fusion.26 = (f32[3,256,4,2,1]{4,1,3,2,0:T(8,128)}, f32[3,256,4,2,1]{4,1,3,2,0:T(8,128)}) fusion(f32[3,256,4,2,128]{4,1,3,2,0:T(8,128)S(1)} %get-tuple-element.31), kind=kLoop, calls=%fused_computation.52 | loop fusion | bytes 98304 | tf_op jit(solution)/shard_map/jit(_roll_static)/slice | solution.py:32
  27.2 1.3 slice_bitcast_fusion.4
  28.5 2.7 %copy.84 = f32[3,256,4,2,1]{1,2,4,3,0:T(4,128)S(1)} copy(f32[3,256,4,2,1]{4,1,3,2,0:T(8,128)} %get-tuple-element.25) | data formatting | bytes 49152 | tf_op jit(solution)/shard_map/jit(_roll_static)/slice | solution.py:32
  31.2 2.2 copy.85
  33.5 2.6 copy.86
  36.1 2.2 copy.87
  38.3 0.0 copy-start.8
  38.3 0.0 copy-start.9
  38.3 1.2 slice_bitcast_fusion
  39.6 0.6 copy-done.2
  40.2 1.0 copy-done.3
  41.1 0.7 copy-done.4
  41.8 0.7 copy-done.5
  42.5 0.1 copy-done.8
  42.6 0.2 copy-done.9
  42.8 2.1 fusion.10
  44.9 0.0 copy-start.7
  45.0 0.0 collective-permute-done
  45.0 0.0 collective-permute-done.1
  45.0 0.0 copy-done.1
  45.0 2.5 fusion.20
  47.5 0.0 copy-start.15
  47.5 0.0 copy-start.13
  47.5 0.0 copy-start.14
  47.5 2.5 pad_maximum_fusion
  50.0 0.0 copy-done.7
  50.0 2.8 %collective-permute-start.2 = (bf16[3,3,256,4,2,128]{5,2,4,3,0,1:T(8,128)(2,1)}, bf16[3,3,256,4,2,128]{5,2,4,3,0,1:T(8,128)(2,1)}, u32[]{:S(2)}, u32[]{:S(2)}) collective-permute-start(bf16[3,3,256,4,2,128]{5,2,4,3,0,1:T(8,128)(2,1)} %pad_maximum_fusion), channel_id=1, source_target_pairs={{1,0},{0,1},{3,2},{2,3},{5,4},{4,5},{7,6},{6,7},{9,8},{8,9},{11,10... | collective-permute-start | bytes 14155784 | tf_op jit(solution)/shard_map/while/body/eval_jaxpr/ppermute | solution.py:23
  52.8 0.0 copy-done.15
  52.8 0.0 copy-done.13
  52.8 0.0 copy-done.14
  52.8 0.1 select_reduce_fusion
  52.9 29.6 %all-gather.2.cloned.1.call-done = bf16[3,512,4,2,128]{4,2,3,1,0:T(4,128)(2,1)} async-done(((bf16[3,256,4,2,128]{4,2,3,1,0:T(4,128)(2,1)}), bf16[3,512,4,2,128]{4,2,3,1,0:T(4,128)(2,1)}) %all-gather.2.cloned.1.call-update) | async-done | bytes 3145744 | tf_op jit(solution)/shard_map/all_gather | solution.py:55
  82.6 2.5 gather_fusion
  85.0 0.1 convert_multiply_fusion
  85.1 0.1 copy.76
  85.2 14.5 %fusion.14 = f32[256,8,256]{2,0,1:T(8,128)} fusion(f32[8,3,4,2,128]{4,3,0,2,1:T(2,128)S(1)} %copy.76, f32[256,3,4,2,128]{4,0,3,2,1:T(8,128)} %get-tuple-element.32, bf16[1,3,256,4,2,128]{5,2,4,3,0,1:T(8,128)(2,1)} %copy-done.7, bf16[1,3,256,4,2,128]{5,2,4,3,0,1:T(8,128)(2,1)S(1)} %fusion.20, bf16[1,3,256,4,2,128]{5,2,4,3,0,1:T(8,128)(2,1)S(1)} %get-tuple-element.33), kind=kOutput, calls=%fused_computation.25 | convolution fusion | flops 9706143744 | bytes 10059776 | tf_op jit(solution)/shard_map/while/body/eval_jaxpr/ijdcxyz,dckxyz->ijk/dot_general | solution.py:37
  99.7 0.0 reduce-scatter.3.cloned.1.call-update
  99.7 0.0 copy-start.11
  99.7 0.0 copy-start.12
  99.7 0.3 reduce-scatter.5.cloned.1.call-start
  100.0 69.5 %collective-permute-done.2 = bf16[3,3,256,4,2,128]{5,2,4,3,0,1:T(8,128)(2,1)} collective-permute-done((bf16[3,3,256,4,2,128]{5,2,4,3,0,1:T(8,128)(2,1)}, bf16[3,3,256,4,2,128]{5,2,4,3,0,1:T(8,128)(2,1)}, u32[]{:S(2)}, u32[]{:S(2)}) %collective-permute-start.2) | collective-permute-done | bytes 4718624 | tf_op jit(solution)/shard_map/while/body/eval_jaxpr/ppermute | solution.py:23
  169.4 15.4 %fusion.17 = f32[256,8,256]{2,0,1:T(8,128)} fusion(bf16[3,3,256,4,2,128]{5,2,4,3,0,1:T(8,128)(2,1)} %collective-permute-done.2, f32[8,3,4,2,128]{4,3,0,2,1:T(2,128)S(1)} %copy.76, f32[256,3,4,2,128]{4,0,3,2,1:T(8,128)} %get-tuple-element.32), kind=kOutput, calls=%fused_computation.26 | convolution fusion | flops 9701425152 | bytes 10059776 | tf_op jit(solution)/shard_map/ijdcxyz,dckxyz->ijk/dot_general | solution.py:37
  184.9 0.0 reduce-scatter.5.cloned.1.call-update
  185.0 0.0 copy-done.11
  185.0 0.0 copy-done.12
  185.0 0.0 reduce-scatter.3.cloned.1.call-done
  185.1 1.0 copy_dynamic-update-slice_fusion.1
  186.0 60.6 %reduce-scatter.5.cloned.1.call-done = f32[16,8,256]{2,0,1:T(8,128)} async-done(((f32[256,8,256]{2,0,1:T(8,128)}), f32[16,8,256]{2,0,1:T(8,128)}) %reduce-scatter.5.cloned.1.call-update) | async-done | bytes 131088 | tf_op jit(solution)/shard_map/reduce_scatter | solution.py:41
  246.7 1.0 copy_dynamic-update-slice_fusion
  247.7 0.0 copy-start.10
  247.7 0.6 copy.91
  248.3 5.5 %gather_fusion.1 = f32[2048,16]{1,0:T(8,128)S(1)} fusion(f32[16,4096]{0,1:T(8,128)S(1)} %bitcast.60, s32[2048]{0:T(1024)S(1)} %broadcast_clamp_fusion), kind=kCustom, calls=%fused_computation.1 | custom fusion | bytes 270336 | tf_op jit(solution)/shard_map/jit(_take)/gather | solution.py:88
  253.8 7.2 %fusion.21 = f32[16,1024]{1,0:T(8,128)} fusion(f32[2048,1024]{1,0:T(8,128)} %param.13, f32[2048,16]{1,0:T(8,128)S(1)} %gather_fusion.1, pred[2048]{0:T(1024)(128)(4,1)S(1)} %compare_and_fusion), kind=kOutput, calls=%fused_computation.30 | convolution fusion | flops 402685952 | bytes 8587264 | tf_op jit(solution)/shard_map/dot_general | solution.py:89
  (15 shorter events, 0.1 us)
Async XLA Ops:
  7.2 75.4 %all-gather.2.cloned.1.call-start = ((), (), s32[]{:S(2)}) async-start(), calls=%async_computation.2 | async-start | bytes 4718592 | tf_op jit(solution)/shard_map/all_gather | solution.py:55
  11.3 1.2 copy-start
  11.3 7.7 %copy-start.6 = (bf16[3,256,4,2,128]{4,3,2,1,0:T(2,128)(2,1)S(1)}, bf16[3,256,4,2,128]{4,3,2,1,0:T(2,128)(2,1)}, u32[]{:S(2)}) copy-start(bf16[3,256,4,2,128]{4,3,2,1,0:T(2,128)(2,1)} %param.7) | copy-start | bytes 4718596
  13.7 31.2 %collective-permute-start = (bf16[3,256,4,1,128]{4,1,3,2,0:T(8,128)(2,1)}, bf16[3,256,4,1,128]{4,1,3,2,0:T(8,128)(2,1)}, u32[]{:S(2)}, u32[]{:S(2)}) collective-permute-start(bf16[3,256,4,1,128]{4,1,3,2,0:T(8,128)(2,1)} %get-tuple-element.28), channel_id=1, source_target_pairs={{2,0},{4,2},{6,4},{8,6},{10,8},{12,10},{14,12},{16,14},{18,16},{20... | collective-permute-start | bytes 2359304 | tf_op jit(solution)/shard_map/ppermute | solution.py:15
  15.0 30.0 %collective-permute-start.1 = (bf16[3,256,4,1,128]{4,1,3,2,0:T(8,128)(2,1)}, bf16[3,256,4,1,128]{4,1,3,2,0:T(8,128)(2,1)}, u32[]{:S(2)}, u32[]{:S(2)}) collective-permute-start(bf16[3,256,4,1,128]{4,1,3,2,0:T(8,128)(2,1)} %get-tuple-element.29), channel_id=1, source_target_pairs={{0,2},{2,4},{4,6},{6,8},{8,10},{10,12},{12,14},{14,16},{16,18},{18... | collective-permute-start | bytes 2359304 | tf_op jit(solution)/shard_map/ppermute | solution.py:14
  20.7 164.3 %reduce-scatter.3.cloned.1.call-start = ((), (), s32[]{:S(2)}) async-start(), calls=%async_computation.3 | async-start | bytes 2228224 | tf_op jit(solution)/shard_map/while/body/eval_jaxpr/reduce_scatter | solution.py:41
  38.3 1.9 copy-start.2
  38.3 2.8 %copy-start.3 = (f32[1,3,256,4,2,1]{5,2,4,3,1,0:T(8,128)S(1)}, f32[1,3,256,4,2,1]{5,2,4,3,1,0:T(8,128)}, u32[]{:S(2)}) copy-start(f32[1,3,256,4,2,1]{5,2,4,3,1,0:T(8,128)} %copy.87) | copy-start | bytes 73732
  38.3 3.5 %copy-start.4 = (f32[1,3,256,3,2,128]{5,2,4,3,0,1:T(8,128)S(1)}, f32[1,3,256,3,2,128]{5,2,4,3,0,1:T(8,128)}, u32[]{:S(2)}) copy-start(f32[1,3,256,3,2,128]{5,2,4,3,0,1:T(8,128)} %get-tuple-element.16) | copy-start | bytes 7077892
  38.3 4.2 %copy-start.5 = (f32[1,3,256,3,2,128]{5,2,4,3,1,0:T(8,128)S(1)}, f32[1,3,256,3,2,128]{5,2,4,3,1,0:T(8,128)}, u32[]{:S(2)}) copy-start(f32[1,3,256,3,2,128]{5,2,4,3,1,0:T(8,128)} %get-tuple-element.17) | copy-start | bytes 7077892
  38.3 4.3 %copy-start.8 = (f32[1,3,256,1,2,128]{5,2,4,3,0,1:T(8,128)S(1)}, f32[1,3,256,1,2,128]{5,2,4,3,0,1:T(8,128)}, u32[]{:S(2)}) copy-start(f32[1,3,256,1,2,128]{5,2,4,3,0,1:T(8,128)} %get-tuple-element.14) | copy-start | bytes 2359300
  38.3 4.5 %copy-start.9 = (f32[1,3,256,1,2,128]{5,2,4,3,1,0:T(8,128)S(1)}, f32[1,3,256,1,2,128]{5,2,4,3,1,0:T(8,128)}, u32[]{:S(2)}) copy-start(f32[1,3,256,1,2,128]{5,2,4,3,1,0:T(8,128)} %get-tuple-element.15) | copy-start | bytes 2359300
  42.8 2.1 copy-start.1
  44.9 5.1 %copy-start.7 = (bf16[1,3,256,4,2,128]{5,2,4,3,0,1:T(8,128)(2,1)}, bf16[1,3,256,4,2,128]{5,2,4,3,0,1:T(8,128)(2,1)S(1)}, u32[]{:S(2)}) copy-start(bf16[1,3,256,4,2,128]{5,2,4,3,0,1:T(8,128)(2,1)S(1)} %get-tuple-element.34) | copy-start | bytes 4718596
  47.5 5.3 %copy-start.15 = (s32[8]{0:T(128)S(1)}, s32[8]{0:T(128)}, u32[]{:S(2)}) copy-start(s32[8]{0:T(128)} %param.10) | copy-start | bytes 100
  47.5 5.3 %copy-start.13 = (s32[4,2,128]{2,1,0:T(2,128)S(1)}, s32[4,2,128]{2,1,0:T(2,128)}, u32[]{:S(2)}) copy-start(s32[4,2,128]{2,1,0:T(2,128)} %param.8) | copy-start | bytes 12292
  47.5 5.3 %copy-start.14 = (f32[8]{0:T(128)S(1)}, f32[8]{0:T(128)}, u32[]{:S(2)}) copy-start(f32[8]{0:T(128)} %param.9) | copy-start | bytes 100
  50.0 119.4 %collective-permute-start.2 = (bf16[3,3,256,4,2,128]{5,2,4,3,0,1:T(8,128)(2,1)}, bf16[3,3,256,4,2,128]{5,2,4,3,0,1:T(8,128)(2,1)}, u32[]{:S(2)}, u32[]{:S(2)}) collective-permute-start(bf16[3,3,256,4,2,128]{5,2,4,3,0,1:T(8,128)(2,1)} %pad_maximum_fusion), channel_id=1, source_target_pairs={{1,0},{0,1},{3,2},{2,3},{5,4},{4,5},{7,6},{6,7},{9,8},{8,9},{11,10... | collective-permute-start | bytes 14155784 | tf_op jit(solution)/shard_map/while/body/eval_jaxpr/ppermute | solution.py:23
  99.7 85.3 %copy-start.11 = (s32[2048]{0:T(1024)S(1)}, s32[2048]{0:T(1024)}, u32[]{:S(2)}) copy-start(s32[2048]{0:T(1024)} %param.12) | copy-start | bytes 24580
  99.7 85.3 %copy-start.12 = (s32[2048]{0:T(1024)S(1)}, s32[2048]{0:T(1024)}, u32[]{:S(2)}) copy-start(s32[2048]{0:T(1024)} %param.11) | copy-start | bytes 24580
  99.7 146.9 %reduce-scatter.5.cloned.1.call-start = ((), (), s32[]{:S(2)}) async-start(), calls=%async_computation.4 | async-start | bytes 2228224 | tf_op jit(solution)/shard_map/reduce_scatter | solution.py:41
  247.7 13.3 %copy-start.10 = (f32[16,8,512]{2,1,0:T(8,128)}, f32[16,8,512]{2,1,0:T(8,128)S(1)}, u32[]{:S(2)}) copy-start(f32[16,8,512]{2,1,0:T(8,128)S(1)} %broadcast_multiply_fusion) | copy-start | bytes 786436
Sparse Core Ops, SparseCore 0:
  20.8 61.6 all-gather.1
  99.8 61.6 reduce-scatter.2
  185.0 61.5 reduce-scatter.4
where the time goes:
time: 268 us
  waiting for transfers between devices  160 us (60%)
  matrix products  37.2 us (14%)
  local copies, waits for them, and re-layouts  36.9 us (14%)
  between operations  14 us (5%)
  other arithmetic  11.3 us (4%)
  starting transfers between devices  8.4 us (3%)
    ppermute x1, waiting for transfers between devices, from_behind(): return lax.ppermute(block, axis, route)  69.5 us
    reduce_scatter x2, waiting for transfers between devices, owner_rows(): lax.psum_scatter(partial_value, 'cell', scatter_dimension=0, tiled=True)  60.6 us
    dot_general x2, matrix products, contract(): jnp.einsum('ijdcxyz,dckxyz->ijk', left_factor, grads, preferred_element_t...  29.9 us
    all_gather x1, waiting for transfers between devices, shards(): all_modes = lax.all_gather(pod_modes, 'mode', axis=1, tiled=True)  29.6 us
    dot_general x1, matrix products, shards(): jnp.dot(columns, pair_amp, precision=lax.Precision.HIGHEST, preferred_ele...  7.23 us
    slice x2, local copies, waits for them, and re-layouts, gradients(): jnp.roll(interior, 1, axis=4)  6.39 us
    unnamed x33, local copies, waits for them, and re-layouts  6.18 us
    gather x1, local copies, waits for them, and re-layouts, shards(): columns = jnp.take(flat_rows, pair_slot, axis=1)  5.47 us
  transfers between devices with their start and end apart: 6, of which 3 were waited for; matrix products, arithmetic and copies ran while one was open for 23% of the time, Pallas kernels for 0%

commit v1 on v0

v1 whole, which is shorter than its diff:
```python
import functools

import jax
import jax.numpy as jnp
from jax import lax
from jax.experimental import pallas as pl
from jax.experimental.pallas import tpu as pltpu
from jax.sharding import PartitionSpec as P

LANES = 128
F32 = jnp.float32
BF16 = jnp.bfloat16


def whole(memory_space=pltpu.VMEM):
    return pl.BlockSpec(memory_space=memory_space)


def params(mib):
    return pltpu.CompilerParams(vmem_limit_bytes=mib * 2**20)


def cost(flops, size):
    return pl.CostEstimate(flops=int(flops), bytes_accessed=int(size), transcendentals=0)


def pack_kernel(planes, rows_y, owners, chunks, base_ref, index_ref, pods_ref, *refs):
    row_refs, own_ref = refs[:rows_y], refs[rows_y]
    chunk_refs = refs[rows_y + 1 : rows_y + 1 + len(chunks)]
    chosen_ref, wide = refs[-2], refs[-1]
    modes, cells = pods_ref.shape[1], pods_ref.shape[2]
    wide[...] = pods_ref[0].astype(F32).reshape(modes * cells, LANES)
    per_owner = modes // owners
    for r in range(rows_y):
        for p in range(planes):
            value = wide[pl.ds(p * rows_y + r, modes, stride=cells), :]
            own = value.astype(BF16)
            at = (r * planes + p) * LANES
            row_refs[r][:, p * LANES : (p + 1) * LANES] = own
            own_ref[:, at : at + LANES] = own
            split = value.reshape(owners, per_owner, LANES)
            for ref, (first, count) in zip(chunk_refs, chunks):
                part = split[:, first : first + count].reshape(owners * count, LANES)
                ref[:, at : at + LANES] = part.astype(BF16)
    for j in range(chosen_ref.shape[1]):
        local = index_ref[j] - base_ref[0]
        inside = jnp.logical_and(local >= 0, local < modes)
        row = jnp.clip(local, 0, modes - 1) * cells
        found = wide[pl.ds(pl.multiple_of(row, cells), cells), :]
        chosen_ref[0, j] = jnp.where(inside, found, 0.0)


def pack(pods, advect_index, base, owners, chunks):
    comps, modes, planes, rows_y, width = pods.shape
    cells = planes * rows_y
    advect_count = advect_index.shape[0]
    flat = pods.reshape(comps, modes, cells, width)
    part = planes * width
    shapes = [((modes, comps * part), (modes, part))] * rows_y
    shapes += [((modes, comps * rows_y * part), (modes, rows_y * part))]
    for _, count in chunks:
        shapes += [((owners * count, comps * rows_y * part), (owners * count, rows_y * part))]
    out_shape = [jax.ShapeDtypeStruct(s, BF16) for s, _ in shapes]
    out_specs = [pl.BlockSpec(b, lambda c: (0, c)) for _, b in shapes]
    out_shape += [jax.ShapeDtypeStruct((comps, advect_count, cells, width), F32)]
    out_specs += [pl.BlockSpec((1, advect_count, cells, width), lambda c: (c, 0, 0, 0))]
    outs = pl.pallas_call(
        functools.partial(pack_kernel, planes, rows_y, owners, chunks),
        grid=(comps,),
        in_specs=[
            whole(pltpu.SMEM),
            whole(pltpu.SMEM),
            pl.BlockSpec((1, modes, cells, width), lambda c: (c, 0, 0, 0)),
        ],
        out_specs=out_specs,
        out_shape=out_shape,
        scratch_shapes=[pltpu.VMEM((modes * cells, width), F32)],
        compiler_params=params(24),
        cost_estimate=cost(0, 4 * pods.size * 2),
        name="pack",
    )(base.reshape(1), advect_index, flat)
    return outs[:rows_y], outs[rows_y], outs[rows_y + 1 : -1], outs[-1]


def advected_kernel(comps, planes, rows_y, volume_ref, map_ref, chosen_ref, *refs):
    row_refs, below_ref, above_ref = refs[:rows_y], refs[rows_y], refs[rows_y + 1]
    out_ref, weighted = refs[-2], refs[-1]
    advect_count = chosen_ref.shape[1]
    slabs = map_ref[...]
    volume = jnp.zeros(slabs.shape, F32)
    for level in range(volume_ref.shape[0]):
        volume = jnp.where(slabs == level, volume_ref[level], volume)
    for d in range(comps):
        for j in range(advect_count):
            weighted[d, j] = chosen_ref[d, j] * volume

    def rounded(x):
        return x.astype(BF16).astype(F32)

    def at(ref, c, p):
        lane = (c * planes + p % planes) * LANES
        return ref[:, lane : lane + LANES].astype(F32)

    for c in range(comps):
        for r in range(rows_y):
            for p in range(planes):
                u = at(row_refs[r], c, p)
                under = at(row_refs[r - 1] if r > 0 else below_ref, c, p)
                over = at(row_refs[r + 1] if r < rows_y - 1 else above_ref, c, p)
                grads = (
                    rounded(0.5 * (at(row_refs[r], c, p + 1) - at(row_refs[r], c, p - 1 + planes))),
                    rounded(0.5 * (over - under)),
                    rounded(0.5 * (pltpu.roll(u, LANES - 1, 1) - pltpu.roll(u, 1, 1))),
                )
                cell = p * rows_y + r
                lane = ((c * rows_y + r) * planes + p) * LANES
                for j in range(advect_count):
                    total = weighted[0, j, cell : cell + 1, :] * grads[0]
                    for d in range(1, comps):
                        total = total + weighted[d, j, cell : cell + 1, :] * grads[d]
                    out_ref[j, :, lane : lane + LANES] = total.astype(BF16)


def advected(rows, below, above, chosen, slab_map, slab_volume):
    comps, advect_count, cells, width = chosen.shape
    rows_y = len(rows)
    planes = cells // rows_y
    modes = rows[0].shape[0]
    tall = 32
    line = pl.BlockSpec((tall, rows[0].shape[1]), lambda b: (b, 0))
    depth = comps * cells * width
    return pl.pallas_call(
        functools.partial(advected_kernel, comps, planes, rows_y),
        grid=(modes // tall,),
        in_specs=[whole(pltpu.SMEM), whole(), whole()] + [line] * (rows_y + 2),
        out_specs=pl.BlockSpec((advect_count, tall, depth), lambda b: (0, b, 0)),
        out_shape=jax.ShapeDtypeStruct((advect_count, modes, depth), BF16),
        scratch_shapes=[pltpu.VMEM((comps, advect_count, cells, width), F32)],
        compiler_params=params(24),
        cost_estimate=cost(5 * advect_count * modes * depth, 2 * advect_count * modes * depth),
        name="advected",
    )(slab_volume, slab_map.reshape(cells, width), chosen, *rows, below, above)


def contract_kernel(left_ref, right_ref, out_ref):
    out_ref[...] = lax.dot_general(
        left_ref[...], right_ref[...], (((1,), (1,)), ((), ())), preferred_element_type=F32
    )


def contract(left, right):
    rows, depth = left.shape
    columns = right.shape[0]
    wide = min(columns, 256)
    return pl.pallas_call(
        contract_kernel,
        grid=(columns // wide,),
        in_specs=[whole(), pl.BlockSpec((wide, depth), lambda j: (j, 0))],
        out_specs=pl.BlockSpec((rows, wide), lambda j: (0, j)),
        out_shape=jax.ShapeDtypeStruct((rows, columns), F32),
        compiler_params=params(24),
        cost_estimate=cost(2 * rows * depth * columns, right.size * 2),
        name="contract",
    )(left, right)


def shifted(block, axis, distance, size, span):
    route = []
    for i in range(lax.axis_size(axis)):
        digit = i // span % size
        route.append((i, i + ((digit + distance) % size - digit) * span))
    return lax.ppermute(block, axis, route)


def stages(count):
    sizes = []
    while count % 4 == 0 and count > 4:
        sizes, count = sizes + [4], count // 4
    if count == 4:
        sizes, count = sizes + [2], 2
    return [count] + sizes[::-1] if count > 1 else sizes[::-1]


def owner_rows(partial):
    size = lax.axis_size("cell")
    own = lax.axis_index("cell")
    span = 1
    value = partial.reshape(size, -1, partial.shape[-1])
    for ways in stages(size):
        digit = own // span % ways
        value = value.reshape(-1, ways, *value.shape[1:])
        kept = lax.dynamic_index_in_dim(value, digit, 1, keepdims=False)
        for s in range(1, ways):
            sent = lax.dynamic_index_in_dim(value, (digit + s) % ways, 1, keepdims=False)
            kept = kept + shifted(sent.astype(BF16), "cell", s, ways, span).astype(F32)
        value = kept
        span *= ways
    return value[0]


def finish_kernel(blocks, advect_count, per_block, scale_factor, slot_ref, flat_ref, amp_ref, tensor_ref, out_ref, columns):
    rows = flat_ref.shape[0]
    step = pl.program_id(0)

    @pl.when(step == 0)
    def _():
        for b in range(blocks):
            for j in range(advect_count):
                at = (b * advect_count + j) * per_block
                tensor_ref[:, j, b * per_block : (b + 1) * per_block] = flat_ref[:, at : at + per_block] * scale_factor

    groups = flat_ref.shape[1] // LANES
    tall = columns.shape[1]
    for g in range(tall // LANES):
        slot = slot_ref[:, g * LANES : (g + 1) * LANES]
        lane = jnp.broadcast_to(slot % LANES, (rows, LANES))
        group = jnp.broadcast_to(slot // LANES, (rows, LANES))
        found = jnp.zeros((rows, LANES), F32)
        for s in range(groups):
            source = flat_ref[:, s * LANES : (s + 1) * LANES]
            found = jnp.where(group == s, jnp.take_along_axis(source, lane, axis=1), found)
        columns[:, g * LANES : (g + 1) * LANES] = found * scale_factor
    term = jnp.dot(columns[...], amp_ref[...], precision=lax.Precision.HIGHEST, preferred_element_type=F32)

    @pl.when(step == 0)
    def _():
        out_ref[...] = term

    @pl.when(step > 0)
    def _():
        out_ref[...] += term


def finish(flat, slot, amp, blocks, advect_count, per_block, scale_factor):
    rows = flat.shape[0]
    pairs, snaps = amp.shape
    tall = 512 if pairs % 512 == 0 else pairs
    return pl.pallas_call(
        functools.partial(finish_kernel, blocks, advect_count, per_block, scale_factor),
        grid=(pairs // tall,),
        in_specs=[
            pl.BlockSpec((1, tall), lambda i: (0, i)),
            whole(),
            pl.BlockSpec((tall, snaps), lambda i: (i, 0)),
        ],
        out_specs=[whole(), whole()],
        out_shape=[
            jax.ShapeDtypeStruct((rows, advect_count, blocks * per_block), F32),
            jax.ShapeDtypeStruct((rows, snaps), F32),
        ],
        scratch_shapes=[pltpu.VMEM((rows, tall), F32)],
        compiler_params=params(32),
        cost_estimate=cost(12 * rows * pairs * snaps, amp.size * 4),
        name="finish",
    )(slot.reshape(1, pairs), flat, amp)


def shards(pod_modes, slab_map, slab_volume, advect_index, pair_adv, pair_mode, pair_amp):
    comps, mode_block, planes, rows_y, width = pod_modes.shape
    mode_devs = lax.axis_size("mode")
    cell_devs = lax.axis_size("cell")
    advect_count = advect_index.shape[0]
    scale_factor = float(planes * rows_y * cell_devs * width) ** (-0.5)
    me = lax.axis_index("mode")
    rows_here = mode_block // cell_devs
    half = rows_here // 2
    chunks = ((0, half), (half, half)) if half % 8 == 0 else ()

    rows, own, parts, chosen = pack(pod_modes, advect_index, me * mode_block, cell_devs, chunks)
    parts = parts or [own]
    picked = chosen.astype(BF16)
    for s in range(1, mode_devs):
        chosen = chosen + shifted(picked, "mode", s, mode_devs, 1).astype(F32)
    arrived = [[shifted(part, "mode", s, mode_devs, 1) for part in parts] for s in range(1, mode_devs)]
    up = [(i, i + 1) for i in range(cell_devs - 1)]
    below = lax.ppermute(rows[-1], "cell", up)
    above = lax.ppermute(rows[0], "cell", [(j, i) for i, j in up])
    right = advected(rows, below, above, chosen, slab_map, slab_volume)
    right = right.reshape(-1, right.shape[-1])

    mine = owner_rows(contract(own, right))
    result = jnp.zeros((mode_devs,) + mine.shape, F32)
    result = lax.dynamic_update_index_in_dim(result, mine, me, 0)
    for s in range(1, mode_devs):
        block = jnp.concatenate([owner_rows(contract(part, right)) for part in arrived[s - 1]], axis=0)
        back = shifted(block, "mode", mode_devs - s, mode_devs, 1)
        result = lax.dynamic_update_index_in_dim(result, back, (me + s) % mode_devs, 0)
    flat = jnp.transpose(result, (1, 0, 2)).reshape(rows_here, -1)
    slot = (pair_mode // mode_block * advect_count + pair_adv) * mode_block + pair_mode % mode_block
    tensor, response = finish(flat, slot, pair_amp, mode_devs, advect_count, mode_block, scale_factor)
    return (tensor, response)


def solution(mesh):
    in_specs = (P(None, "mode", None, "cell", None), P(None, "cell", None), P(), P(), P(), P(), P())
    out_specs = (P(("mode", "cell"), None, None), P(("mode", "cell"), None))
    return jax.shard_map(shards, mesh=mesh, in_specs=in_specs, out_specs=out_specs, check_vma=False)
```

time: 268 us -> 119 us (0.44)
  waiting for transfers between devices: 160 us -> 42.9 us
  matrix products: 37.2 us -> 0 us
  Pallas kernels: 0 us -> 34.2 us
  local copies, waits for them, and re-layouts: 36.9 us -> 8.13 us
  starting transfers between devices: 8.4 us -> 31.5 us
  between operations: 14 us -> 0.98 us
  other arithmetic: 11.3 us -> 0.44 us
    reduce_scatter x2 -> x0, waiting for transfers between devices: 60.6 us -> none  [owner_rows(): lax.psum_scatter(partial_value, 'cell', scatter_dimension=0, tiled=True)]
    dot_general x3 -> x0, matrix products: 37.2 us -> none  [the longest x2 29.9 us: contract(): jnp.einsum('ijdcxyz,dckxyz->ijk', left_factor, grads, preferred_element_t...]
    pallas_call x0 -> x6, Pallas kernels: none -> 34.2 us  [the longest x3 15.4 us: contract(): pl.pallas_call(contract_kernel, grid=(columns // wide,), in_specs=[whole(...]
    all_gather x1 -> x0, waiting for transfers between devices: 29.6 us -> none  [shards(): all_modes = lax.all_gather(pod_modes, 'mode', axis=1, tiled=True)]
    ppermute x3 -> x21, waiting for transfers between devices: 69.5 us -> 42.9 us  [the longest x19 42.9 us: shifted(): return lax.ppermute(block, axis, route)]
    ppermute x3 -> x21, starting transfers between devices: 8.06 us -> 31.5 us  [the longest x19 27 us: shifted(): return lax.ppermute(block, axis, route)]
    slice x4 -> x0, local copies, waits for them, and re-layouts: 10.4 us -> none  [the longest x2 6.39 us: gradients(): jnp.roll(interior, 1, axis=4)]
    concatenate x5 -> x0, local copies, waits for them, and re-layouts: 9.68 us -> none  [the longest x2 4.01 us: gradients(): jnp.roll(interior, 1, axis=2)]
  transfers between devices with their start and end apart: 6 -> 21, of which waited for: 3 -> 8; matrix products, arithmetic and copies ran while one was open for 23% -> 1% of each run, Pallas kernels for 0% -> 21%
where the time goes in v1:
time: 119 us; the launch traced here: 118 us
  waiting for transfers between devices  42.9 us (36%)
  Pallas kernels  34.2 us (29%)
  starting transfers between devices  31.5 us (26%)
  local copies, waits for them, and re-layouts  8.13 us (7%)
    ppermute x19, waiting for transfers between devices, shifted(): return lax.ppermute(block, axis, route)  42.9 us
    ppermute x19, starting transfers between devices, shifted(): return lax.ppermute(block, axis, route)  27 us
    pallas_call x3, Pallas kernels, contract(): pl.pallas_call(contract_kernel, grid=(columns // wide,), in_specs=[whole(...  15.4 us
    pallas_call x1, Pallas kernels, advected(): pl.pallas_call(functools.partial(advected_kernel, comps, planes, rows_y),...  9.27 us
    pallas_call x1, Pallas kernels, finish(): pl.pallas_call(functools.partial(finish_kernel, blocks, advect_count, per...  5.96 us
    unnamed x15, local copies, waits for them, and re-layouts  5.62 us
    pallas_call x1, Pallas kernels, pack(): pl.pallas_call(functools.partial(pack_kernel, planes, rows_y, owners, chu...  3.54 us
    ppermute x1, starting transfers between devices, shards(): below = lax.ppermute(rows[-1], 'cell', up)  3.25 us
  transfers between devices with their start and end apart: 21, of which 8 were waited for; matrix products, arithmetic and copies ran while one was open for 1% of the time, Pallas kernels for 21%

profile of v1, /device:TPU:0, one launch (start us, length us, event | category | flops | bytes accessed | tf_op | source)
XLA Modules:
  0.0 118.2 jit_solution(11361829466737529134)
XLA Ops:
  0.7 1.4 %copy-done.1 = bf16[3,256,4,2,128]{4,3,2,1,0:T(2,128)(2,1)S(1)} copy-done((bf16[3,256,4,2,128]{4,3,2,1,0:T(2,128)(2,1)S(1)}, bf16[3,256,4,2,128]{4,3,2,1,0:T(2,128)(2,1)}, u32[]{:S(2)}) %copy-start.1) | copy-done | bytes 1572888
  2.1 0.7 copy-done.3
  2.7 3.5 %pack.1 = (bf16[256,1536]{1,0:T(8,128)(2,1)}, bf16[256,1536]{1,0:T(8,128)(2,1)}, bf16[256,3072]{1,0:T(8,128)(2,1)S(1)}, bf16[128,3072]{1,0:T(8,128)(2,1)}, bf16[...) custom-call(s32[1]{0:T(128)} %bitcast.1.base_ref, s32[8]{0:T(128)S(1)} %copy-done.3, bf16[3,256,8,128]{3,2,1,0:T(8,128)(2,1)S(1)} %bitcast.68), custom_call_target="tpu_custom_call" | custom-call | bytes 6291456 | tf_op jit(solution)/shard_map/pack/pallas_call | solution.py:67
  6.3 3.2 %collective-permute-start.1 = (bf16[256,1536]{1,0:T(8,128)(2,1)}, bf16[256,1536]{1,0:T(8,128)(2,1)}, u32[]{:S(2)}, u32[]{:S(2)}) collective-permute-start(bf16[256,1536]{1,0:T(8,128)(2,1)} %get-tuple-element.11.refs_1_), channel_id=1, source_target_pairs={{0,2},{2,4},{4,6},{6,8},{8,10},{10,12},{12,14},{14,16},{16,18},{18... | collective-permute-start | bytes 2359304 | tf_op jit(solution)/shard_map/ppermute | solution.py:276
  9.5 1.3 %collective-permute-start.2 = (bf16[256,1536]{1,0:T(8,128)(2,1)}, bf16[256,1536]{1,0:T(8,128)(2,1)}, u32[]{:S(2)}, u32[]{:S(2)}) collective-permute-start(bf16[256,1536]{1,0:T(8,128)(2,1)} %get-tuple-element.10.refs_0_), channel_id=1, source_target_pairs={{2,0},{4,2},{6,4},{8,6},{10,8},{12,10},{14,12},{16,14},{18,16},{20... | collective-permute-start | bytes 2359304 | tf_op jit(solution)/shard_map/ppermute | solution.py:277
  10.8 2.4 %collective-permute-start.8 = (bf16[128,3072]{1,0:T(8,128)(2,1)}, bf16[128,3072]{1,0:T(8,128)(2,1)S(1)}, u32[]{:S(2)}, u32[]{:S(2)}) collective-permute-start(bf16[128,3072]{1,0:T(8,128)(2,1)} %get-tuple-element.12), channel_id=1, source_target_pairs={{0,1},{1,0},{2,3},{3,2},{4,5},{5,4},{6,7},{7,6},{8,9},{9,8},{10,11... | collective-permute-start | bytes 2359304 | tf_op jit(solution)/shard_map/ppermute | solution.py:172
  13.2 0.1 collective-permute-start.14
  13.3 2.0 %collective-permute-start = (bf16[3,8,8,128]{3,2,1,0:T(8,128)(2,1)S(1)}, bf16[3,8,8,128]{3,2,1,0:T(8,128)(2,1)S(1)}, u32[]{:S(2)}, u32[]{:S(2)}) collective-permute-start(bf16[3,8,8,128]{3,2,1,0:T(8,128)(2,1)S(1)} %convert_element_type.132), channel_id=1, source_target_pairs={{0,1},{1,0},{2,3},{3,2},{4,5},{5,4},{6,7},{7,6},{8,9},{9,8},{10,11... | collective-permute-start | bytes 147464 | tf_op jit(solution)/shard_map/ppermute | solution.py:172
  15.3 33.5 %collective-permute-done = bf16[3,8,8,128]{3,2,1,0:T(8,128)(2,1)S(1)} collective-permute-done((bf16[3,8,8,128]{3,2,1,0:T(8,128)(2,1)S(1)}, bf16[3,8,8,128]{3,2,1,0:T(8,128)(2,1)S(1)}, u32[]{:S(2)}, u32[]{:S(2)}) %collective-permute-start) | collective-permute-done | bytes 49184 | tf_op jit(solution)/shard_map/ppermute | solution.py:172
  48.8 0.0 collective-permute-done.1.refs_2_
  48.8 0.0 collective-permute-done.2.refs_3_
  48.8 9.3 %advected.1 = bf16[8,256,3072]{2,1,0:T(8,128)(2,1)S(1)} custom-call(f32[8]{0:T(128)S(1)} %copy-done.4, s32[8,128]{1,0:T(8,128)S(1)} %bitcast.71, f32[3,8,8,128]{3,2,1,0:T(8,128)S(1)} %convert_add_fusion.1.chosen_ref, bf16[256,1536]{1,0:T(8,128)(2,1)} %get-tuple-element.10.refs_0_, bf16[256,1536]{1,0:T(8,128)(2,1)} %get-tuple-element.11.refs_1_, ...), custom_call_target="tpu_custom_call" | custom-call | flops 31457280 | bytes 12582912 | tf_op jit(solution)/shard_map/advected/pallas_call | solution.py:132
  58.1 0.0 collective-permute-done.8.left_ref
  58.1 5.2 %contract.4 = f32[128,2048]{1,0:T(8,128)S(1)} custom-call(bf16[128,3072]{1,0:T(8,128)(2,1)S(1)} %collective-permute-done.8.left_ref, bf16[2048,3072]{1,0:T(8,128)(2,1)S(1)} %bitcast.59), custom_call_target="tpu_custom_call" | custom-call | flops 1610612736 | bytes 12582912 | tf_op jit(solution)/shard_map/contract/pallas_call | solution.py:155
  63.4 0.8 collective-permute-start.9
  64.2 0.0 collective-permute-done.14.left_ref
  64.2 5.2 %contract.5 = f32[128,2048]{1,0:T(8,128)S(1)} custom-call(bf16[128,3072]{1,0:T(8,128)(2,1)S(1)} %collective-permute-done.14.left_ref, bf16[2048,3072]{1,0:T(8,128)(2,1)S(1)} %bitcast.60), custom_call_target="tpu_custom_call" | custom-call | flops 1610612736 | bytes 12582912 | tf_op jit(solution)/shard_map/contract/pallas_call | solution.py:155
  69.5 0.1 collective-permute-start.15
  69.6 5.0 %contract.3 = f32[256,2048]{1,0:T(8,128)S(1)} custom-call(bf16[256,3072]{1,0:T(8,128)(2,1)S(1)} %get-tuple-element.8.left_ref, bf16[2048,3072]{1,0:T(8,128)(2,1)S(1)} %bitcast.61), custom_call_target="tpu_custom_call" | custom-call | flops 3221225472 | bytes 12582912 | tf_op jit(solution)/shard_map/contract/pallas_call | solution.py:155
  74.6 0.1 fusion
  74.7 0.5 collective-permute-start.3
  75.2 0.0 collective-permute-done.9
  75.2 0.0 collective-permute-done.15
  75.2 0.1 bitcast_add_fusion.1
  75.4 2.9 %collective-permute-start.10 = (bf16[4,8,2048]{2,1,0:T(8,128)(2,1)S(1)}, bf16[4,8,2048]{2,1,0:T(8,128)(2,1)S(1)}, u32[]{:S(2)}, u32[]{:S(2)}) collective-permute-start(bf16[4,8,2048]{2,1,0:T(8,128)(2,1)S(1)} %fusion.4), channel_id=1, source_target_pairs={{0,4},{2,6},{4,0},{6,2},{8,12},{10,14},{12,8},{14,10},{16,20},{18,... | collective-permute-start | bytes 393224 | tf_op jit(solution)/shard_map/ppermute | solution.py:172
  78.3 0.1 collective-permute-start.16
  78.4 4.2 %collective-permute-done.10 = bf16[4,8,2048]{2,1,0:T(8,128)(2,1)S(1)} collective-permute-done((bf16[4,8,2048]{2,1,0:T(8,128)(2,1)S(1)}, bf16[4,8,2048]{2,1,0:T(8,128)(2,1)S(1)}, u32[]{:S(2)}, u32[]{:S(2)}) %collective-permute-start.10) | collective-permute-done | bytes 131104 | tf_op jit(solution)/shard_map/ppermute | solution.py:172
  82.6 2.0 %collective-permute-start.11 = (bf16[1,8,2048]{2,1,0:T(8,128)(2,1)S(1)}, bf16[1,8,2048]{2,1,0:T(8,128)(2,1)S(1)}, u32[]{:S(2)}, u32[]{:S(2)}) collective-permute-start(bf16[1,8,2048]{2,1,0:T(8,128)(2,1)S(1)} %get-tuple-element.17), channel_id=1, source_target_pairs={{0,8},{2,10},{4,12},{6,14},{8,16},{10,18},{12,20},{14,22},{16,24},... | collective-permute-start | bytes 98312 | tf_op jit(solution)/shard_map/ppermute | solution.py:172
  84.7 2.6 %collective-permute-start.12 = (bf16[1,8,2048]{2,1,0:T(8,128)(2,1)S(1)}, bf16[1,8,2048]{2,1,0:T(8,128)(2,1)S(1)}, u32[]{:S(2)}, u32[]{:S(2)}) collective-permute-start(bf16[1,8,2048]{2,1,0:T(8,128)(2,1)S(1)} %get-tuple-element.19), channel_id=1, source_target_pairs={{0,16},{2,18},{4,20},{6,22},{8,24},{10,26},{12,28},{14,30},{16,0},... | collective-permute-start | bytes 98312 | tf_op jit(solution)/shard_map/ppermute | solution.py:172
  87.3 1.3 %collective-permute-start.13 = (bf16[1,8,2048]{2,1,0:T(8,128)(2,1)S(1)}, bf16[1,8,2048]{2,1,0:T(8,128)(2,1)S(1)}, u32[]{:S(2)}, u32[]{:S(2)}) collective-permute-start(bf16[1,8,2048]{2,1,0:T(8,128)(2,1)S(1)} %get-tuple-element.18), channel_id=1, source_target_pairs={{0,24},{2,26},{4,28},{6,30},{8,0},{10,2},{12,4},{14,6},{16,8},{18,... | collective-permute-start | bytes 98312 | tf_op jit(solution)/shard_map/ppermute | solution.py:172
  88.6 0.0 collective-permute-done.16
  88.7 0.7 collective-permute-start.17
  89.4 0.0 collective-permute-done.11
  89.4 0.3 collective-permute-start.18
  89.8 0.0 collective-permute-done.12
  89.8 2.9 %collective-permute-start.19 = (bf16[1,8,2048]{2,1,0:T(8,128)(2,1)S(1)}, bf16[1,8,2048]{2,1,0:T(8,128)(2,1)S(1)}, u32[]{:S(2)}, u32[]{:S(2)}) collective-permute-start(bf16[1,8,2048]{2,1,0:T(8,128)(2,1)S(1)} %get-tuple-element.21), channel_id=1, source_target_pairs={{0,24},{2,26},{4,28},{6,30},{8,0},{10,2},{12,4},{14,6},{16,8},{18,... | collective-permute-start | bytes 98312 | tf_op jit(solution)/shard_map/ppermute | solution.py:172
  92.6 0.0 collective-permute-done.13
  92.6 0.0 copy-start.5
  92.7 0.0 copy-start.6
  92.7 0.0 collective-permute-done.3
  92.7 0.1 bitcast_add_fusion
  92.8 1.6 %collective-permute-start.4 = (bf16[4,16,2048]{2,1,0:T(8,128)(2,1)S(1)}, bf16[4,16,2048]{2,1,0:T(8,128)(2,1)S(1)}, u32[]{:S(2)}, u32[]{:S(2)}) collective-permute-start(bf16[4,16,2048]{2,1,0:T(8,128)(2,1)S(1)} %fusion.1), channel_id=1, source_target_pairs={{0,4},{2,6},{4,0},{6,2},{8,12},{10,14},{12,8},{14,10},{16,20},{18,... | collective-permute-start | bytes 786440 | tf_op jit(solution)/shard_map/ppermute | solution.py:172
  94.4 0.1 collective-permute-done.17
  94.5 0.5 collective-permute-done.18
  95.0 0.0 collective-permute-done.19
  95.1 1.6 %collective-permute-start.20 = (f32[16,2048]{1,0:T(8,128)S(1)}, f32[16,2048]{1,0:T(8,128)S(1)}, u32[]{:S(2)}, u32[]{:S(2)}) collective-permute-start(f32[16,2048]{1,0:T(8,128)S(1)} %pad_maximum_fusion), channel_id=1, source_target_pairs={{0,1},{1,0},{2,3},{3,2},{4,5},{5,4},{6,7},{7,6},{8,9},{9,8},{10,11... | collective-permute-start | bytes 393224 | tf_op jit(solution)/shard_map/ppermute | solution.py:172
  96.7 2.6 %collective-permute-done.4 = bf16[4,16,2048]{2,1,0:T(8,128)(2,1)S(1)} collective-permute-done((bf16[4,16,2048]{2,1,0:T(8,128)(2,1)S(1)}, bf16[4,16,2048]{2,1,0:T(8,128)(2,1)S(1)}, u32[]{:S(2)}, u32[]{:S(2)}) %collective-permute-start.4) | collective-permute-done | bytes 262176 | tf_op jit(solution)/shard_map/ppermute | solution.py:172
  99.3 0.1 bitcast_add_fusion.3
  99.4 0.6 collective-permute-start.5
  99.9 1.8 %collective-permute-start.6 = (bf16[1,16,2048]{2,1,0:T(8,128)(2,1)S(1)}, bf16[1,16,2048]{2,1,0:T(8,128)(2,1)S(1)}, u32[]{:S(2)}, u32[]{:S(2)}) collective-permute-start(bf16[1,16,2048]{2,1,0:T(8,128)(2,1)S(1)} %get-tuple-element.16), channel_id=1, source_target_pairs={{0,16},{2,18},{4,20},{6,22},{8,24},{10,26},{12,28},{14,30},{16,0},... | collective-permute-start | bytes 196616 | tf_op jit(solution)/shard_map/ppermute | solution.py:172
  101.7 2.6 %collective-permute-start.7 = (bf16[1,16,2048]{2,1,0:T(8,128)(2,1)S(1)}, bf16[1,16,2048]{2,1,0:T(8,128)(2,1)S(1)}, u32[]{:S(2)}, u32[]{:S(2)}) collective-permute-start(bf16[1,16,2048]{2,1,0:T(8,128)(2,1)S(1)} %get-tuple-element.15), channel_id=1, source_target_pairs={{0,24},{2,26},{4,28},{6,30},{8,0},{10,2},{12,4},{14,6},{16,8},{18,... | collective-permute-start | bytes 196616 | tf_op jit(solution)/shard_map/ppermute | solution.py:172
  104.4 0.0 collective-permute-done.20
  104.4 0.1 copy.14
  104.5 1.1 collective-permute-done.5
  105.6 0.2 collective-permute-done.6
  105.9 0.7 collective-permute-done.7
  106.6 0.1 copy.10
  106.7 0.1 broadcast_in_dim.8
  106.8 0.9 dynamic_update_slice.7
  107.7 0.9 dynamic_update_slice.8
  108.7 0.2 copy.19
  108.8 0.0 copy-start
  108.8 3.4 %copy-done = f32[2048,1024]{1,0:T(8,128)S(1)} copy-done((f32[2048,1024]{1,0:T(8,128)S(1)}, f32[2048,1024]{1,0:T(8,128)}, u32[]{:S(2)}) %copy-start) | copy-done | bytes 8388632
  112.2 6.0 %finish.1 = (f32[16,8,512]{2,1,0:T(8,128)}, f32[16,1024]{1,0:T(8,128)}) custom-call(s32[1,2048]{1,0:T(1,128)S(1)} %bitcast.70, f32[16,4096]{1,0:T(8,128)S(1)} %bitcast.69, f32[2048,1024]{1,0:T(8,128)S(1)} %copy-done), custom_call_target="tpu_custom_call" | custom-call | flops 402653184 | bytes 8388608 | tf_op jit(solution)/shard_map/finish/pallas_call | solution.py:238
  (25 shorter events, 0.4 us)
Async XLA Ops:
  0.6 48.2 %copy-start.2 = (s32[4,2,128]{2,1,0:T(2,128)S(1)}, s32[4,2,128]{2,1,0:T(2,128)}, u32[]{:S(2)}) copy-start(s32[4,2,128]{2,1,0:T(2,128)} %param.8) | copy-start | bytes 12292
  0.6 48.2 %copy-start.4 = (f32[8]{0:T(128)S(1)}, f32[8]{0:T(128)}, u32[]{:S(2)}) copy-start(f32[8]{0:T(128)} %volume_ref.1) | copy-start | bytes 100
  0.7 1.4 %copy-start.1 = (bf16[3,256,4,2,128]{4,3,2,1,0:T(2,128)(2,1)S(1)}, bf16[3,256,4,2,128]{4,3,2,1,0:T(2,128)(2,1)}, u32[]{:S(2)}) copy-start(bf16[3,256,4,2,128]{4,3,2,1,0:T(2,128)(2,1)} %param.7) | copy-start | bytes 4718596
  2.1 0.7 copy-start.3
  6.3 42.5 %collective-permute-start.1 = (bf16[256,1536]{1,0:T(8,128)(2,1)}, bf16[256,1536]{1,0:T(8,128)(2,1)}, u32[]{:S(2)}, u32[]{:S(2)}) collective-permute-start(bf16[256,1536]{1,0:T(8,128)(2,1)} %get-tuple-element.11.refs_1_), channel_id=1, source_target_pairs={{0,2},{2,4},{4,6},{6,8},{8,10},{10,12},{12,14},{14,16},{16,18},{18... | collective-permute-start | bytes 2359304 | tf_op jit(solution)/shard_map/ppermute | solution.py:276
  9.5 39.3 %collective-permute-start.2 = (bf16[256,1536]{1,0:T(8,128)(2,1)}, bf16[256,1536]{1,0:T(8,128)(2,1)}, u32[]{:S(2)}, u32[]{:S(2)}) collective-permute-start(bf16[256,1536]{1,0:T(8,128)(2,1)} %get-tuple-element.10.refs_0_), channel_id=1, source_target_pairs={{2,0},{4,2},{6,4},{8,6},{10,8},{12,10},{14,12},{16,14},{18,16},{20... | collective-permute-start | bytes 2359304 | tf_op jit(solution)/shard_map/ppermute | solution.py:277
  10.8 47.3 %collective-permute-start.8 = (bf16[128,3072]{1,0:T(8,128)(2,1)}, bf16[128,3072]{1,0:T(8,128)(2,1)S(1)}, u32[]{:S(2)}, u32[]{:S(2)}) collective-permute-start(bf16[128,3072]{1,0:T(8,128)(2,1)} %get-tuple-element.12), channel_id=1, source_target_pairs={{0,1},{1,0},{2,3},{3,2},{4,5},{5,4},{6,7},{7,6},{8,9},{9,8},{10,11... | collective-permute-start | bytes 2359304 | tf_op jit(solution)/shard_map/ppermute | solution.py:172
  13.2 51.0 %collective-permute-start.14 = (bf16[128,3072]{1,0:T(8,128)(2,1)}, bf16[128,3072]{1,0:T(8,128)(2,1)S(1)}, u32[]{:S(2)}, u32[]{:S(2)}) collective-permute-start(bf16[128,3072]{1,0:T(8,128)(2,1)} %get-tuple-element.13), channel_id=1, source_target_pairs={{0,1},{1,0},{2,3},{3,2},{4,5},{5,4},{6,7},{7,6},{8,9},{9,8},{10,11... | collective-permute-start | bytes 2359304 | tf_op jit(solution)/shard_map/ppermute | solution.py:172
  13.3 35.5 %collective-permute-start = (bf16[3,8,8,128]{3,2,1,0:T(8,128)(2,1)S(1)}, bf16[3,8,8,128]{3,2,1,0:T(8,128)(2,1)S(1)}, u32[]{:S(2)}, u32[]{:S(2)}) collective-permute-start(bf16[3,8,8,128]{3,2,1,0:T(8,128)(2,1)S(1)} %convert_element_type.132), channel_id=1, source_target_pairs={{0,1},{1,0},{2,3},{3,2},{4,5},{5,4},{6,7},{7,6},{8,9},{9,8},{10,11... | collective-permute-start | bytes 147464 | tf_op jit(solution)/shard_map/ppermute | solution.py:172
  63.4 11.8 %collective-permute-start.9 = (bf16[8,8,2048]{2,1,0:T(8,128)(2,1)S(1)}, bf16[8,8,2048]{2,1,0:T(8,128)(2,1)S(1)}, u32[]{:S(2)}, u32[]{:S(2)}) collective-permute-start(bf16[8,8,2048]{2,1,0:T(8,128)(2,1)S(1)} %fusion.3), channel_id=1, source_target_pairs={{0,2},{2,0},{4,6},{6,4},{8,10},{10,8},{12,14},{14,12},{16,18},{18,... | collective-permute-start | bytes 786440 | tf_op jit(solution)/shard_map/ppermute | solution.py:172
  69.5 5.7 %collective-permute-start.15 = (bf16[8,8,2048]{2,1,0:T(8,128)(2,1)S(1)}, bf16[8,8,2048]{2,1,0:T(8,128)(2,1)S(1)}, u32[]{:S(2)}, u32[]{:S(2)}) collective-permute-start(bf16[8,8,2048]{2,1,0:T(8,128)(2,1)S(1)} %fusion.2), channel_id=1, source_target_pairs={{0,2},{2,0},{4,6},{6,4},{8,10},{10,8},{12,14},{14,12},{16,18},{18,... | collective-permute-start | bytes 786440 | tf_op jit(solution)/shard_map/ppermute | solution.py:172
  74.7 18.0 %collective-permute-start.3 = (bf16[8,16,2048]{2,1,0:T(8,128)(2,1)S(1)}, bf16[8,16,2048]{2,1,0:T(8,128)(2,1)S(1)}, u32[]{:S(2)}, u32[]{:S(2)}) collective-permute-start(bf16[8,16,2048]{2,1,0:T(8,128)(2,1)S(1)} %fusion), channel_id=1, source_target_pairs={{0,2},{2,0},{4,6},{6,4},{8,10},{10,8},{12,14},{14,12},{16,18},{18,... | collective-permute-start | bytes 1572872 | tf_op jit(solution)/shard_map/ppermute | solution.py:172
  75.4 7.2 %collective-permute-start.10 = (bf16[4,8,2048]{2,1,0:T(8,128)(2,1)S(1)}, bf16[4,8,2048]{2,1,0:T(8,128)(2,1)S(1)}, u32[]{:S(2)}, u32[]{:S(2)}) collective-permute-start(bf16[4,8,2048]{2,1,0:T(8,128)(2,1)S(1)} %fusion.4), channel_id=1, source_target_pairs={{0,4},{2,6},{4,0},{6,2},{8,12},{10,14},{12,8},{14,10},{16,20},{18,... | collective-permute-start | bytes 393224 | tf_op jit(solution)/shard_map/ppermute | solution.py:172
  78.3 10.4 %collective-permute-start.16 = (bf16[4,8,2048]{2,1,0:T(8,128)(2,1)S(1)}, bf16[4,8,2048]{2,1,0:T(8,128)(2,1)S(1)}, u32[]{:S(2)}, u32[]{:S(2)}) collective-permute-start(bf16[4,8,2048]{2,1,0:T(8,128)(2,1)S(1)} %fusion.5), channel_id=1, source_target_pairs={{0,4},{2,6},{4,0},{6,2},{8,12},{10,14},{12,8},{14,10},{16,20},{18,... | collective-permute-start | bytes 393224 | tf_op jit(solution)/shard_map/ppermute | solution.py:172
  82.6 6.8 %collective-permute-start.11 = (bf16[1,8,2048]{2,1,0:T(8,128)(2,1)S(1)}, bf16[1,8,2048]{2,1,0:T(8,128)(2,1)S(1)}, u32[]{:S(2)}, u32[]{:S(2)}) collective-permute-start(bf16[1,8,2048]{2,1,0:T(8,128)(2,1)S(1)} %get-tuple-element.17), channel_id=1, source_target_pairs={{0,8},{2,10},{4,12},{6,14},{8,16},{10,18},{12,20},{14,22},{16,24},... | collective-permute-start | bytes 98312 | tf_op jit(solution)/shard_map/ppermute | solution.py:172
  84.7 5.1 %collective-permute-start.12 = (bf16[1,8,2048]{2,1,0:T(8,128)(2,1)S(1)}, bf16[1,8,2048]{2,1,0:T(8,128)(2,1)S(1)}, u32[]{:S(2)}, u32[]{:S(2)}) collective-permute-start(bf16[1,8,2048]{2,1,0:T(8,128)(2,1)S(1)} %get-tuple-element.19), channel_id=1, source_target_pairs={{0,16},{2,18},{4,20},{6,22},{8,24},{10,26},{12,28},{14,30},{16,0},... | collective-permute-start | bytes 98312 | tf_op jit(solution)/shard_map/ppermute | solution.py:172
  87.3 5.3 %collective-permute-start.13 = (bf16[1,8,2048]{2,1,0:T(8,128)(2,1)S(1)}, bf16[1,8,2048]{2,1,0:T(8,128)(2,1)S(1)}, u32[]{:S(2)}, u32[]{:S(2)}) collective-permute-start(bf16[1,8,2048]{2,1,0:T(8,128)(2,1)S(1)} %get-tuple-element.18), channel_id=1, source_target_pairs={{0,24},{2,26},{4,28},{6,30},{8,0},{10,2},{12,4},{14,6},{16,8},{18,... | collective-permute-start | bytes 98312 | tf_op jit(solution)/shard_map/ppermute | solution.py:172
  88.7 5.9 %collective-permute-start.17 = (bf16[1,8,2048]{2,1,0:T(8,128)(2,1)S(1)}, bf16[1,8,2048]{2,1,0:T(8,128)(2,1)S(1)}, u32[]{:S(2)}, u32[]{:S(2)}) collective-permute-start(bf16[1,8,2048]{2,1,0:T(8,128)(2,1)S(1)} %get-tuple-element.20), channel_id=1, source_target_pairs={{0,8},{2,10},{4,12},{6,14},{8,16},{10,18},{12,20},{14,22},{16,24},... | collective-permute-start | bytes 98312 | tf_op jit(solution)/shard_map/ppermute | solution.py:172
  89.4 5.6 %collective-permute-start.18 = (bf16[1,8,2048]{2,1,0:T(8,128)(2,1)S(1)}, bf16[1,8,2048]{2,1,0:T(8,128)(2,1)S(1)}, u32[]{:S(2)}, u32[]{:S(2)}) collective-permute-start(bf16[1,8,2048]{2,1,0:T(8,128)(2,1)S(1)} %get-tuple-element.22), channel_id=1, source_target_pairs={{0,16},{2,18},{4,20},{6,22},{8,24},{10,26},{12,28},{14,30},{16,0},... | collective-permute-start | bytes 98312 | tf_op jit(solution)/shard_map/ppermute | solution.py:172
  89.8 5.3 %collective-permute-start.19 = (bf16[1,8,2048]{2,1,0:T(8,128)(2,1)S(1)}, bf16[1,8,2048]{2,1,0:T(8,128)(2,1)S(1)}, u32[]{:S(2)}, u32[]{:S(2)}) collective-permute-start(bf16[1,8,2048]{2,1,0:T(8,128)(2,1)S(1)} %get-tuple-element.21), channel_id=1, source_target_pairs={{0,24},{2,26},{4,28},{6,30},{8,0},{10,2},{12,4},{14,6},{16,8},{18,... | collective-permute-start | bytes 98312 | tf_op jit(solution)/shard_map/ppermute | solution.py:172
  92.6 11.7 %copy-start.5 = (s32[2048]{0:T(1024)S(1)}, s32[2048]{0:T(1024)}, u32[]{:S(2)}) copy-start(s32[2048]{0:T(1024)} %param.11) | copy-start | bytes 24580
  92.7 11.7 %copy-start.6 = (s32[2048]{0:T(1024)S(1)}, s32[2048]{0:T(1024)}, u32[]{:S(2)}) copy-start(s32[2048]{0:T(1024)} %param.12) | copy-start | bytes 24580
  92.8 6.4 %collective-permute-start.4 = (bf16[4,16,2048]{2,1,0:T(8,128)(2,1)S(1)}, bf16[4,16,2048]{2,1,0:T(8,128)(2,1)S(1)}, u32[]{:S(2)}, u32[]{:S(2)}) collective-permute-start(bf16[4,16,2048]{2,1,0:T(8,128)(2,1)S(1)} %fusion.1), channel_id=1, source_target_pairs={{0,4},{2,6},{4,0},{6,2},{8,12},{10,14},{12,8},{14,10},{16,20},{18,... | collective-permute-start | bytes 786440 | tf_op jit(solution)/shard_map/ppermute | solution.py:172
  95.1 9.3 %collective-permute-start.20 = (f32[16,2048]{1,0:T(8,128)S(1)}, f32[16,2048]{1,0:T(8,128)S(1)}, u32[]{:S(2)}, u32[]{:S(2)}) collective-permute-start(f32[16,2048]{1,0:T(8,128)S(1)} %pad_maximum_fusion), channel_id=1, source_target_pairs={{0,1},{1,0},{2,3},{3,2},{4,5},{5,4},{6,7},{7,6},{8,9},{9,8},{10,11... | collective-permute-start | bytes 393224 | tf_op jit(solution)/shard_map/ppermute | solution.py:172
  99.4 6.2 %collective-permute-start.5 = (bf16[1,16,2048]{2,1,0:T(8,128)(2,1)S(1)}, bf16[1,16,2048]{2,1,0:T(8,128)(2,1)S(1)}, u32[]{:S(2)}, u32[]{:S(2)}) collective-permute-start(bf16[1,16,2048]{2,1,0:T(8,128)(2,1)S(1)} %get-tuple-element.14), channel_id=1, source_target_pairs={{0,8},{2,10},{4,12},{6,14},{8,16},{10,18},{12,20},{14,22},{16,24},... | collective-permute-start | bytes 196616 | tf_op jit(solution)/shard_map/ppermute | solution.py:172
  99.9 5.9 %collective-permute-start.6 = (bf16[1,16,2048]{2,1,0:T(8,128)(2,1)S(1)}, bf16[1,16,2048]{2,1,0:T(8,128)(2,1)S(1)}, u32[]{:S(2)}, u32[]{:S(2)}) collective-permute-start(bf16[1,16,2048]{2,1,0:T(8,128)(2,1)S(1)} %get-tuple-element.16), channel_id=1, source_target_pairs={{0,16},{2,18},{4,20},{6,22},{8,24},{10,26},{12,28},{14,30},{16,0},... | collective-permute-start | bytes 196616 | tf_op jit(solution)/shard_map/ppermute | solution.py:172
  101.7 4.8 %collective-permute-start.7 = (bf16[1,16,2048]{2,1,0:T(8,128)(2,1)S(1)}, bf16[1,16,2048]{2,1,0:T(8,128)(2,1)S(1)}, u32[]{:S(2)}, u32[]{:S(2)}) collective-permute-start(bf16[1,16,2048]{2,1,0:T(8,128)(2,1)S(1)} %get-tuple-element.15), channel_id=1, source_target_pairs={{0,24},{2,26},{4,28},{6,30},{8,0},{10,2},{12,4},{14,6},{16,8},{18,... | collective-permute-start | bytes 196616 | tf_op jit(solution)/shard_map/ppermute | solution.py:172
  108.8 3.4 %copy-start = (f32[2048,1024]{1,0:T(8,128)S(1)}, f32[2048,1024]{1,0:T(8,128)}, u32[]{:S(2)}) copy-start(f32[2048,1024]{1,0:T(8,128)} %amp_ref.1) | copy-start | bytes 25165828

commit v2 on v0

v2 whole, which is shorter than its diff:
```python
import functools
import math

import jax
import jax.numpy as jnp
from jax import lax
from jax.experimental import pallas as pl
from jax.experimental.pallas import tpu as pltpu
from jax.sharding import PartitionSpec as P

LANES = 128
F32 = jnp.float32
BF16 = jnp.bfloat16


def whole(memory_space=pltpu.VMEM):
    return pl.BlockSpec(memory_space=memory_space)


def params(mib):
    return pltpu.CompilerParams(vmem_limit_bytes=mib * 2**20)


SHORT = pl.CostEstimate(flops=1, bytes_accessed=1, transcendentals=0)


def choose_kernel(index_ref, pods_ref, out_ref, held, sems):
    modes = pods_ref.shape[1]
    base = lax.axis_index("mode") * modes
    count = out_ref.shape[0]
    copies = []
    for j in range(count):
        local = jnp.clip(index_ref[j] - base, 0, modes - 1)
        copies.append(pltpu.make_async_copy(pods_ref.at[:, local], held.at[j], sems.at[j]))
        copies[-1].start()
    for j in range(count):
        copies[j].wait()
        local = index_ref[j] - base
        inside = jnp.logical_and(local >= 0, local < modes)
        out_ref[j] = jnp.where(inside, held[j].astype(F32), 0.0).astype(BF16)


def choose(flat, advect_index):
    comps, modes, cells, width = flat.shape
    shape = (advect_index.shape[0], comps, cells, width)
    return pl.pallas_call(
        choose_kernel,
        in_specs=[whole(pltpu.SMEM), whole(pltpu.HBM)],
        out_specs=whole(),
        out_shape=jax.ShapeDtypeStruct(shape, BF16),
        scratch_shapes=[pltpu.VMEM(shape, BF16), pltpu.SemaphoreType.DMA((shape[0],))],
        compiler_params=params(58),
        cost_estimate=SHORT,
        name="choose",
    )(advect_index, flat)


def pack_kernel(planes, rows_y, groups, apart, pods_ref, after_ref, *refs):
    comps, modes, cells, _ = pods_ref.shape
    part = planes * LANES
    outs, wide = refs[:-1], refs[-1]
    for g, group in enumerate(groups):
        for k, c in enumerate(group):
            wide[...] = pods_ref[c].astype(F32).reshape(modes * cells, LANES)
            for r in range(rows_y):
                for p in range(planes):
                    value = wide[pl.ds(p * rows_y + r, modes, stride=cells), :].astype(BF16)
                    ref = outs[g * rows_y + r] if apart else outs[g]
                    at = (k if apart else r * len(group) + k) * part + p * LANES
                    ref[:, at : at + LANES] = value


def pack(flat, after, planes, rows_y, groups, apart):
    comps, modes, cells, width = flat.shape
    part = planes * width
    shapes = []
    for group in groups:
        shapes += [(modes, len(group) * part)] * rows_y if apart else [(modes, len(group) * rows_y * part)]
    return pl.pallas_call(
        functools.partial(pack_kernel, planes, rows_y, groups, apart),
        in_specs=[whole(), whole(pl.ANY)],
        out_specs=[whole()] * len(shapes),
        out_shape=[jax.ShapeDtypeStruct(s, BF16) for s in shapes],
        scratch_shapes=[pltpu.VMEM((modes * cells, width), F32)],
        compiler_params=params(8),
        cost_estimate=SHORT,
        name="edges" if apart else "together",
    )(flat, after)


def advected_kernel(members, planes, rows_y, tall, volume_ref, map_ref, chosen_ref, back_ref, *refs):
    row_refs, below_ref, above_ref = refs[:rows_y], refs[rows_y], refs[rows_y + 1]
    out_ref, weighted = refs[-2], refs[-1]
    advect_count, comps = chosen_ref.shape[:2]
    modes = below_ref.shape[0]
    slabs = map_ref[...]
    volume = jnp.zeros(slabs.shape, F32)
    for level in range(volume_ref.shape[0]):
        volume = jnp.where(slabs == level, volume_ref[level], volume)
    for d in range(comps):
        for j in range(advect_count):
            chosen = chosen_ref[j, d].astype(F32)
            for s in range(back_ref.shape[0]):
                chosen = chosen + back_ref[s, j, d].astype(F32)
            weighted[d, j] = 0.5 * (chosen * volume)

    def rounded(x):
        return x.astype(BF16).astype(F32)

    @pl.loop(0, modes // tall)
    def _(b):
        here = pl.ds(pl.multiple_of(b * tall, tall), tall)

        def at(ref, k, p):
            lane = (k * planes + p) * LANES
            return ref[here, lane : lane + LANES].astype(F32)

        for k in range(members):
            lines = [[at(ref, k, p) for p in range(planes)] for ref in row_refs]
            for p in range(planes):
                column = [at(below_ref, k, p)] + [line[p] for line in lines] + [at(above_ref, k, p)]
                for r in range(rows_y):
                    u = lines[r][p]
                    grads = (
                        rounded(lines[r][(p + 1) % planes] - lines[r][(p - 1) % planes]),
                        rounded(column[r + 2] - column[r]),
                        rounded(pltpu.roll(u, LANES - 1, 1) - pltpu.roll(u, 1, 1)),
                    )
                    cell = p * rows_y + r
                    lane = ((r * members + k) * planes + p) * LANES
                    for j in range(advect_count):
                        total = weighted[0, j, cell : cell + 1, :] * grads[0]
                        for d in range(1, comps):
                            total = total + weighted[d, j, cell : cell + 1, :] * grads[d]
                        out_ref[j, here, lane : lane + LANES] = total.astype(BF16)


def advected(members, rows, below, above, chosen, back, slab_map, slab_volume):
    advect_count, comps, cells, width = chosen.shape
    rows_y = len(rows)
    planes = cells // rows_y
    modes = rows[0].shape[0]
    depth = members * cells * width
    return pl.pallas_call(
        functools.partial(advected_kernel, members, planes, rows_y, 16),
        in_specs=[whole(pltpu.SMEM)] + [whole()] * (rows_y + 5),
        out_specs=whole(),
        out_shape=jax.ShapeDtypeStruct((advect_count, modes, depth), BF16),
        scratch_shapes=[pltpu.VMEM((comps, advect_count, cells, width), F32)],
        compiler_params=params(8),
        cost_estimate=SHORT,
        name="advected",
    )(slab_volume, slab_map.reshape(cells, width), chosen, back, *rows, below, above)


def digits(number, sizes):
    ways, span = sizes[number], math.prod(sizes[:number])
    own = lax.axis_index("cell") // span % ways
    return [lax.rem(own + s, ways) for s in range(ways)]


def contract_kernel(sizes, groups, rows_y, wide, left_ref, *refs):
    outs = refs[len(groups) : -1]
    right_refs, scratch = refs[: len(groups)], refs[-1]
    columns = right_refs[0].shape[0]
    depth = left_ref.shape[1]
    comps = sum(len(group) for group in groups)
    part = depth // rows_y // comps
    pieces = []
    for group in groups:
        for r in range(rows_y):
            first = (r * comps + group[0]) * part
            pieces.append(left_ref[:, first : first + len(group) * part])
    left = jnp.concatenate(pieces, axis=1)
    places = digits(0, sizes)
    for n in range(columns // wide):
        here = slice(n * wide, (n + 1) * wide)
        right = jnp.concatenate([ref[here, :] for ref in right_refs], axis=1)
        value = lax.dot_general(left, right, (((1,), (1,)), ((), ())), preferred_element_type=F32)
        scratch[n % 2] = value.reshape(scratch.shape[1:])
        for q in range(outs[0].shape[0]):
            for out, place in zip(outs, places):
                out[q, :, here] = scratch[n % 2, q * sizes[0] + place].astype(out.dtype)


def contract(left, groups, right, sizes, rows_y):
    columns = right[0].shape[0]
    rows, depth = left.shape
    owners = math.prod(sizes)
    wide = min(columns, 256)
    shape = (owners // sizes[0], rows // owners, columns)
    return pl.pallas_call(
        functools.partial(contract_kernel, sizes, groups, rows_y, wide),
        in_specs=[whole()] * (1 + len(right)),
        out_specs=[whole()] * sizes[0],
        out_shape=[jax.ShapeDtypeStruct(shape, BF16 if s else F32) for s in range(sizes[0])],
        scratch_shapes=[pltpu.VMEM((2, owners, rows // owners, wide), F32)],
        compiler_params=params(8),
        cost_estimate=SHORT,
        name="contract",
    )(left, *right)


def fold_kernel(number, sizes, arrived, *refs):
    kept_ref, arrived_refs, outs = refs[0], refs[1 : 1 + arrived], refs[1 + arrived :]
    places = [0] if number == len(sizes) else digits(number, sizes)
    ways = len(places)
    for q in range(kept_ref.shape[0] // ways):
        for out, place in zip(outs, places):
            total = kept_ref[q * ways + place]
            for ref in arrived_refs:
                total = total + ref[q * ways + place].astype(F32)
            out[q] = total.astype(out.dtype)


def fold(kept, arrived, number, sizes):
    ways = 1 if number == len(sizes) else sizes[number]
    shape = (kept.shape[0] // ways, *kept.shape[1:])
    return pl.pallas_call(
        functools.partial(fold_kernel, number, sizes, len(arrived)),
        in_specs=[whole()] * (1 + len(arrived)),
        out_specs=[whole()] * ways,
        out_shape=[jax.ShapeDtypeStruct(shape, BF16 if s else F32) for s in range(ways)],
        compiler_params=params(8),
        cost_estimate=SHORT,
        name="fold",
    )(kept, *arrived)


def shifted(block, axis, distance, size, span):
    route = []
    for i in range(lax.axis_size(axis)):
        digit = i // span % size
        route.append((i, i + ((digit + distance) % size - digit) * span))
    return lax.ppermute(block, axis, route)


def stages(count):
    sizes = []
    while count % 4 == 0 and count > 4:
        sizes, count = sizes + [4], count // 4
    if count == 4:
        sizes, count = sizes + [2], 2
    return [count] + sizes[::-1] if count > 1 else sizes[::-1]


def stage(parts, number, sizes):
    span = math.prod(sizes[:number])
    arrived = [shifted(part, "cell", s + 1, sizes[number], span) for s, part in enumerate(parts[1:])]
    return fold(parts[0], arrived, number + 1, sizes)


def finish_kernel(advect_count, per_block, scale_factor, me_ref, slot_ref, *refs):
    *part_refs, amp_ref, tensor_ref, out_ref, flat, both, amps, sems = refs
    blocks, rows = flat.shape[0], flat.shape[1]
    steps, tall, _ = amps.shape
    copies = []
    for i in range(steps):
        copies.append(pltpu.make_async_copy(amp_ref.at[pl.ds(i * tall, tall)], amps.at[i], sems.at[i]))
        copies[-1].start()
    for s, ref in enumerate(part_refs):
        flat[s] = ref[...] * scale_factor
    for b in range(blocks):
        for j in range(advect_count):
            at = slice(j * per_block, (j + 1) * per_block)
            value = flat[0, :, at]
            for s in range(1, blocks):
                value = jnp.where((me_ref[0] + s) % blocks == b, flat[s, :, at], value)
            tensor_ref[:, j, b * per_block : (b + 1) * per_block] = value

    groups = flat.shape[2] // LANES
    for g in range(both.shape[1] // LANES):
        here = slice(g * LANES, (g + 1) * LANES)
        slot = slot_ref[:, here]
        lane = jnp.broadcast_to(slot % LANES, (rows, LANES))
        group = jnp.broadcast_to(slot // LANES, (rows, LANES))
        found = jnp.zeros((rows, LANES), F32)
        for b in range(blocks):
            for s in range(groups):
                source = flat[b, :, s * LANES : (s + 1) * LANES]
                taken = jnp.take_along_axis(source, lane, axis=1)
                found = jnp.where(group == b * groups + s, taken, found)
        high = found.astype(BF16).astype(F32)
        both[:rows, here] = high
        both[rows:, here] = found - high
    total = jnp.zeros(out_ref.shape, F32)
    for i in range(steps):
        copies[i].wait()
        columns = both[:, i * tall : (i + 1) * tall].astype(BF16)
        amp = amps[i]
        high = amp.astype(BF16)
        low = (amp - high.astype(F32)).astype(BF16)
        term = jnp.dot(columns, high, preferred_element_type=F32)
        small = jnp.dot(columns[:rows], low, preferred_element_type=F32)
        total = total + (term[:rows] + (term[rows:] + small))
    out_ref[...] = total


def finish(me, slot, parts, amp, advect_count, scale_factor):
    pairs, snaps = amp.shape
    tall = 512 if pairs % 512 == 0 else pairs
    rows, columns = parts[0].shape
    blocks = len(parts)
    per_block = columns // advect_count
    return pl.pallas_call(
        functools.partial(finish_kernel, advect_count, per_block, scale_factor),
        in_specs=[whole(pltpu.SMEM)] + [whole()] * (1 + blocks) + [whole(pltpu.HBM)],
        out_specs=[whole(), whole()],
        out_shape=[
            jax.ShapeDtypeStruct((rows, advect_count, blocks * per_block), F32),
            jax.ShapeDtypeStruct((rows, snaps), F32),
        ],
        scratch_shapes=[
            pltpu.VMEM((blocks, rows, columns), F32),
            pltpu.VMEM((2 * rows, pairs), F32),
            pltpu.VMEM((pairs // tall, tall, snaps), F32),
            pltpu.SemaphoreType.DMA((pairs // tall,)),
        ],
        compiler_params=params(58),
        cost_estimate=SHORT,
        name="finish",
    )(me.reshape(1), slot.reshape(1, pairs), *parts, amp)


def shards(pod_modes, slab_map, slab_volume, advect_index, pair_adv, pair_mode, pair_amp):
    comps, mode_block, planes, rows_y, width = pod_modes.shape
    mode_devs = lax.axis_size("mode")
    cell_devs = lax.axis_size("cell")
    advect_count = advect_index.shape[0]
    scale_factor = float(planes * rows_y * cell_devs * width) ** (-0.5)
    me = lax.axis_index("mode")
    rows_here = mode_block // cell_devs

    flat = pod_modes.reshape(comps, mode_block, planes * rows_y, width)
    chosen = choose(flat, advect_index)
    everything = (tuple(range(comps)),)
    groups = (tuple(range(comps - 1)), (comps - 1,))
    (own,) = pack(flat, chosen, planes, rows_y, everything, False)
    back = jnp.stack([shifted(chosen, "mode", s, mode_devs, 1) for s in range(1, mode_devs)])
    own, back = lax.optimization_barrier((own, back))
    arrived = [shifted(own, "mode", s, mode_devs, 1) for s in range(1, mode_devs)]
    up = [(i, i + 1) for i in range(cell_devs - 1)]
    down = [(j, i) for i, j in up]
    before, halos = own, []
    for group in groups:
        lines = pack(flat, before, planes, rows_y, (group,), True)
        halos.append((lines, lax.ppermute(lines[-1], "cell", up), lax.ppermute(lines[0], "cell", down)))
        before = lines[0]
    right = []
    for group, (lines, below, above) in zip(groups, halos):
        if right:
            right[-1], below, above = lax.optimization_barrier((right[-1], below, above))
        block = advected(len(group), lines, below, above, chosen, back, slab_map, slab_volume)
        right.append(block.reshape(-1, block.shape[-1]))

    sizes = stages(cell_devs)
    early = min(2, len(sizes))

    def summed(parts, first, last):
        for number in range(first, last):
            parts = stage(parts, number, sizes)
        return list(parts)

    mine = summed(contract(own, groups, right, sizes, rows_y), 0, early)
    mine[0], *arrived = lax.optimization_barrier((mine[0], *arrived))
    result = []
    for s in range(1, mode_devs):
        block = summed(contract(arrived[s - 1], groups, right, sizes, rows_y), 0, early)
        if s == 1:
            mine = summed(mine, early, len(sizes))
            mine[0], block[0] = lax.optimization_barrier((mine[0], block[0]))
            result.append(mine[0][0])
        block = summed(block, early, len(sizes))[0][0]
        result.append(shifted(block, "mode", mode_devs - s, mode_devs, 1))
    block_of = (pair_mode // mode_block - me) % mode_devs
    slot = (block_of * advect_count + pair_adv) * mode_block + pair_mode % mode_block
    tensor, response = finish(me, slot, result, pair_amp, advect_count, scale_factor)
    return (tensor, response)


def solution(mesh):
    in_specs = (P(None, "mode", None, "cell", None), P(None, "cell", None), P(), P(), P(), P(), P())
    out_specs = (P(("mode", "cell"), None, None), P(("mode", "cell"), None))
    return jax.shard_map(shards, mesh=mesh, in_specs=in_specs, out_specs=out_specs, check_vma=False)
```

time: 268 us -> 87.8 us (0.33)
  waiting for transfers between devices: 160 us -> 18.1 us
  matrix products: 37.2 us -> 0 us
  local copies, waits for them, and re-layouts: 36.9 us -> 3.52 us
  starting transfers between devices: 8.4 us -> 38.1 us
  Pallas kernels: 0 us -> 26 us
  between operations: 14 us -> 1.02 us
  other arithmetic: 11.3 us -> 0.62 us
    reduce_scatter x2 -> x0, waiting for transfers between devices: 60.6 us -> none  [owner_rows(): lax.psum_scatter(partial_value, 'cell', scatter_dimension=0, tiled=True)]
    ppermute x3 -> x17, waiting for transfers between devices: 69.5 us -> 18.1 us  [the longest x13 18 us: shifted(): return lax.ppermute(block, axis, route)]
    dot_general x3 -> x0, matrix products: 37.2 us -> none  [the longest x2 29.9 us: contract(): jnp.einsum('ijdcxyz,dckxyz->ijk', left_factor, grads, preferred_element_t...]
    ppermute x3 -> x17, starting transfers between devices: 8.06 us -> 38.1 us  [the longest x13 29.5 us: shifted(): return lax.ppermute(block, axis, route)]
    all_gather x1 -> x0, waiting for transfers between devices: 29.6 us -> none  [shards(): all_modes = lax.all_gather(pod_modes, 'mode', axis=1, tiled=True)]
    pallas_call x0 -> x15, Pallas kernels: none -> 26 us  [the longest x2 8.44 us: advected(): pl.pallas_call(functools.partial(advected_kernel, members, planes, rows_y...]
    slice x4 -> x0, local copies, waits for them, and re-layouts: 10.4 us -> none  [the longest x2 6.39 us: gradients(): jnp.roll(interior, 1, axis=4)]
    concatenate x5 -> x0, local copies, waits for them, and re-layouts: 9.68 us -> none  [the longest x2 4.01 us: gradients(): jnp.roll(interior, 1, axis=2)]
  transfers between devices with their start and end apart: 6 -> 17, of which waited for: 3 -> 7; matrix products, arithmetic and copies ran while one was open for 23% -> 1% of each run, Pallas kernels for 0% -> 16%
where the time goes in v2:
time: 87.8 us; the launch traced here: 87.4 us
  starting transfers between devices  38.1 us (43%)
  Pallas kernels  26 us (30%)
  waiting for transfers between devices  18.1 us (21%)
  local copies, waits for them, and re-layouts  3.52 us (4%)
  between operations  1.02 us (1%)
    ppermute x13, starting transfers between devices, shifted(): return lax.ppermute(block, axis, route)  29.5 us
    ppermute x13, waiting for transfers between devices, shifted(): return lax.ppermute(block, axis, route)  18 us
    pallas_call x2, Pallas kernels, advected(): pl.pallas_call(functools.partial(advected_kernel, members, planes, rows_y...  8.44 us
    pallas_call x2, Pallas kernels, contract(): pl.pallas_call(functools.partial(contract_kernel, sizes, groups, rows_y,...  7.81 us
    ppermute x2, starting transfers between devices, shards(): lax.ppermute(lines[-1], 'cell', up)  6.06 us
    pallas_call x1, Pallas kernels, finish(): pl.pallas_call(functools.partial(finish_kernel, advect_count, per_block,...  5.58 us
    unnamed x18, local copies, waits for them, and re-layouts  3.52 us
    ppermute x2, starting transfers between devices, shards(): lax.ppermute(lines[0], 'cell', down)  2.58 us
  transfers between devices with their start and end apart: 17, of which 7 were waited for; matrix products, arithmetic and copies ran while one was open for 1% of the time, Pallas kernels for 16%

profile of v2, /device:TPU:0, one launch (start us, length us, event | category | flops | bytes accessed | tf_op | source)
XLA Modules:
  0.0 87.4 jit_solution(6944799361500607551)
XLA Ops:
  0.6 2.2 %choose.1.after_ref.chosen_ref = bf16[8,3,8,128]{3,2,1,0:T(8,128)(2,1)} custom-call(s32[8]{0:T(128)} %index_ref.1, bf16[3,256,8,128]{3,2,1,0:T(8,128)(2,1)} %bitcast.13), custom_call_target="tpu_custom_call" | custom-call | flops 1 | bytes 1 | tf_op jit(solution)/shard_map/choose/pallas_call | solution.py:46
  2.9 3.0 %collective-permute-start = (bf16[8,3,8,128]{3,2,1,0:T(8,128)(2,1)}, bf16[8,3,8,128]{3,2,1,0:T(8,128)(2,1)S(1)}, u32[]{:S(2)}, u32[]{:S(2)}) collective-permute-start(bf16[8,3,8,128]{3,2,1,0:T(8,128)(2,1)} %choose.1.after_ref.chosen_ref), channel_id=1, source_target_pairs={{0,1},{1,0},{2,3},{3,2},{4,5},{5,4},{6,7},{7,6},{8,9},{9,8},{10,11... | collective-permute-start | bytes 147464 | tf_op jit(solution)/shard_map/ppermute | solution.py:235
  5.9 0.0 copy-start
  5.9 1.4 %copy-done = bf16[3,256,4,2,128]{4,3,2,1,0:T(2,128)(2,1)S(1)} copy-done((bf16[3,256,4,2,128]{4,3,2,1,0:T(2,128)(2,1)S(1)}, bf16[3,256,4,2,128]{4,3,2,1,0:T(2,128)(2,1)}, u32[]{:S(2)}) %copy-start) | copy-done | bytes 1572888
  7.3 0.0 copy-start.1
  7.3 0.8 copy-done.1
  8.1 0.0 copy-start.2
  8.1 0.0 copy-start.4
  8.1 0.0 copy-start.5
  8.1 0.8 together.1.after_ref.left_ref
  8.9 0.0 collective-permute-done
  8.9 1.2 %collective-permute-start.7 = (bf16[256,3072]{1,0:T(8,128)(2,1)S(1)}, bf16[256,3072]{1,0:T(8,128)(2,1)S(1)}, u32[]{:S(2)}, u32[]{:S(2)}) collective-permute-start(bf16[256,3072]{1,0:T(8,128)(2,1)S(1)} %together.1.after_ref.left_ref), channel_id=1, source_target_pairs={{0,1},{1,0},{2,3},{3,2},{4,5},{5,4},{6,7},{7,6},{8,9},{9,8},{10,11... | collective-permute-start | bytes 4718600 | tf_op jit(solution)/shard_map/ppermute | solution.py:235
  10.2 0.5 edges.2
  10.7 1.3 %collective-permute-start.2 = (bf16[256,1024]{1,0:T(8,128)(2,1)S(1)}, bf16[256,1024]{1,0:T(8,128)(2,1)S(1)}, u32[]{:S(2)}, u32[]{:S(2)}) collective-permute-start(bf16[256,1024]{1,0:T(8,128)(2,1)S(1)} %get-tuple-element.33.refs_0_.after_ref), channel_id=1, source_target_pairs={{2,0},{4,2},{6,4},{8,6},{10,8},{12,10},{14,12},{16,14},{18,16},{20... | collective-permute-start | bytes 1572872 | tf_op jit(solution)/shard_map/ppermute | solution.py:347
  12.0 3.1 %collective-permute-start.1 = (bf16[256,1024]{1,0:T(8,128)(2,1)S(1)}, bf16[256,1024]{1,0:T(8,128)(2,1)S(1)}, u32[]{:S(2)}, u32[]{:S(2)}) collective-permute-start(bf16[256,1024]{1,0:T(8,128)(2,1)S(1)} %get-tuple-element.34.refs_1_), channel_id=1, source_target_pairs={{0,2},{2,4},{4,6},{6,8},{8,10},{10,12},{12,14},{14,16},{16,18},{18... | collective-permute-start | bytes 1572872 | tf_op jit(solution)/shard_map/ppermute | solution.py:347
  15.1 0.3 edges.3
  15.4 3.0 %collective-permute-start.3 = (bf16[256,512]{1,0:T(8,128)(2,1)S(1)}, bf16[256,512]{1,0:T(8,128)(2,1)S(1)}, u32[]{:S(2)}, u32[]{:S(2)}) collective-permute-start(bf16[256,512]{1,0:T(8,128)(2,1)S(1)} %get-tuple-element.35.refs_1_), channel_id=1, source_target_pairs={{0,2},{2,4},{4,6},{6,8},{8,10},{10,12},{12,14},{14,16},{16,18},{18... | collective-permute-start | bytes 786440 | tf_op jit(solution)/shard_map/ppermute | solution.py:347
  18.4 1.3 %collective-permute-start.4 = (bf16[256,512]{1,0:T(8,128)(2,1)S(1)}, bf16[256,512]{1,0:T(8,128)(2,1)S(1)}, u32[]{:S(2)}, u32[]{:S(2)}) collective-permute-start(bf16[256,512]{1,0:T(8,128)(2,1)S(1)} %get-tuple-element.36.refs_0_), channel_id=1, source_target_pairs={{2,0},{4,2},{6,4},{8,6},{10,8},{12,10},{14,12},{16,14},{18,16},{20... | collective-permute-start | bytes 786440 | tf_op jit(solution)/shard_map/ppermute | solution.py:347
  19.7 0.0 collective-permute-done.2.refs_3_
  19.7 0.0 collective-permute-done.1.refs_2_
  19.7 0.0 copy-done.2
  19.7 0.0 copy-done.4
  19.7 0.0 copy-done.5
  19.7 5.4 %advected.2 = bf16[8,256,2048]{2,1,0:T(8,128)(2,1)S(1)} custom-call(f32[8]{0:T(128)S(1)} %copy-done.5, s32[8,128]{1,0:T(8,128)S(1)} %bitcast.21, bf16[8,3,8,128]{3,2,1,0:T(8,128)(2,1)S(1)} %copy-done.2, bf16[1,8,3,8,128]{4,3,2,1,0:T(8,128)(2,1)S(1)} %bitcast.18, bf16[256,1024]{1,0:T(8,128)(2,1)S(1)} %get-tuple-element.33.refs_0_.after_ref, ...), custom_call_target="tpu_custom_call" | custom-call | flops 1 | bytes 1 | tf_op jit(solution)/shard_map/advected/pallas_call | solution.py:144
  25.1 0.0 collective-permute-done.3.refs_2_
  25.1 0.0 collective-permute-done.4.refs_3_
  25.2 3.1 %advected.3 = bf16[8,256,1024]{2,1,0:T(8,128)(2,1)S(1)} custom-call(f32[8]{0:T(128)S(1)} %copy-done.5, s32[8,128]{1,0:T(8,128)S(1)} %bitcast.22, bf16[8,3,8,128]{3,2,1,0:T(8,128)(2,1)S(1)} %copy-done.2, bf16[1,8,3,8,128]{4,3,2,1,0:T(8,128)(2,1)S(1)} %bitcast.19, bf16[256,512]{1,0:T(8,128)(2,1)S(1)} %get-tuple-element.36.refs_0_, ...), custom_call_target="tpu_custom_call" | custom-call | flops 1 | bytes 1 | tf_op jit(solution)/shard_map/advected/pallas_call | solution.py:144
  28.2 3.9 %contract.2 = (f32[8,16,2048]{2,1,0:T(8,128)S(1)}, bf16[8,16,2048]{2,1,0:T(8,128)(2,1)S(1)}) custom-call(bf16[256,3072]{1,0:T(8,128)(2,1)S(1)} %together.1.after_ref.left_ref, bf16[2048,2048]{1,0:T(8,128)(2,1)S(1)} %bitcast.9, bf16[2048,1024]{1,0:T(8,128)(2,1)S(1)} %bitcast.11), custom_call_target="tpu_custom_call" | custom-call | flops 1 | bytes 1 | tf_op jit(solution)/shard_map/contract/pallas_call | solution.py:192
  32.1 9.2 %collective-permute-start.5 = (bf16[8,16,2048]{2,1,0:T(8,128)(2,1)S(1)}, bf16[8,16,2048]{2,1,0:T(8,128)(2,1)S(1)}, u32[]{:S(2)}, u32[]{:S(2)}) collective-permute-start(bf16[8,16,2048]{2,1,0:T(8,128)(2,1)S(1)} %get-tuple-element.41), channel_id=1, source_target_pairs={{0,2},{2,0},{4,6},{6,4},{8,10},{10,8},{12,14},{14,12},{16,18},{18,... | collective-permute-start | bytes 1572872 | tf_op jit(solution)/shard_map/ppermute | solution.py:235
  41.4 1.5 %collective-permute-done.5.refs_1_ = bf16[8,16,2048]{2,1,0:T(8,128)(2,1)S(1)} collective-permute-done((bf16[8,16,2048]{2,1,0:T(8,128)(2,1)S(1)}, bf16[8,16,2048]{2,1,0:T(8,128)(2,1)S(1)}, u32[]{:S(2)}, u32[]{:S(2)}) %collective-permute-start.5) | collective-permute-done | bytes 524320 | tf_op jit(solution)/shard_map/ppermute | solution.py:235
  42.9 0.1 fold.6
  43.0 2.8 %collective-permute-start.6 = (bf16[4,16,2048]{2,1,0:T(8,128)(2,1)S(1)}, bf16[4,16,2048]{2,1,0:T(8,128)(2,1)S(1)}, u32[]{:S(2)}, u32[]{:S(2)}) collective-permute-start(bf16[4,16,2048]{2,1,0:T(8,128)(2,1)S(1)} %get-tuple-element.43), channel_id=1, source_target_pairs={{0,4},{2,6},{4,0},{6,2},{8,12},{10,14},{12,8},{14,10},{16,20},{18,... | collective-permute-start | bytes 786440 | tf_op jit(solution)/shard_map/ppermute | solution.py:235
  45.8 6.6 %collective-permute-done.6.refs_1_ = bf16[4,16,2048]{2,1,0:T(8,128)(2,1)S(1)} collective-permute-done((bf16[4,16,2048]{2,1,0:T(8,128)(2,1)S(1)}, bf16[4,16,2048]{2,1,0:T(8,128)(2,1)S(1)}, u32[]{:S(2)}, u32[]{:S(2)}) %collective-permute-start.6) | collective-permute-done | bytes 262176 | tf_op jit(solution)/shard_map/ppermute | solution.py:235
  52.4 0.0 collective-permute-done.7.left_ref
  52.5 0.0 copy-start.7
  52.5 0.0 copy-start.8
  52.5 3.9 %contract.3 = (f32[8,16,2048]{2,1,0:T(8,128)S(1)}, bf16[8,16,2048]{2,1,0:T(8,128)(2,1)S(1)}) custom-call(bf16[256,3072]{1,0:T(8,128)(2,1)S(1)} %collective-permute-done.7.left_ref, bf16[2048,2048]{1,0:T(8,128)(2,1)S(1)} %bitcast.10, bf16[2048,1024]{1,0:T(8,128)(2,1)S(1)} %bitcast.12), custom_call_target="tpu_custom_call" | custom-call | flops 1 | bytes 1 | tf_op jit(solution)/shard_map/contract/pallas_call | solution.py:192
  56.4 0.1 collective-permute-start.11
  56.5 1.9 %collective-permute-done.11.refs_1_ = bf16[8,16,2048]{2,1,0:T(8,128)(2,1)S(1)} collective-permute-done((bf16[8,16,2048]{2,1,0:T(8,128)(2,1)S(1)}, bf16[8,16,2048]{2,1,0:T(8,128)(2,1)S(1)}, u32[]{:S(2)}, u32[]{:S(2)}) %collective-permute-start.11) | collective-permute-done | bytes 524320 | tf_op jit(solution)/shard_map/ppermute | solution.py:235
  58.4 0.1 fold.9
  58.5 1.8 %collective-permute-start.12 = (bf16[4,16,2048]{2,1,0:T(8,128)(2,1)S(1)}, bf16[4,16,2048]{2,1,0:T(8,128)(2,1)S(1)}, u32[]{:S(2)}, u32[]{:S(2)}) collective-permute-start(bf16[4,16,2048]{2,1,0:T(8,128)(2,1)S(1)} %get-tuple-element.53), channel_id=1, source_target_pairs={{0,4},{2,6},{4,0},{6,2},{8,12},{10,14},{12,8},{14,10},{16,20},{18,... | collective-permute-start | bytes 786440 | tf_op jit(solution)/shard_map/ppermute | solution.py:235
  60.3 2.3 %collective-permute-start.10 = (bf16[1,16,2048]{2,1,0:T(8,128)(2,1)S(1)}, bf16[1,16,2048]{2,1,0:T(8,128)(2,1)S(1)}, u32[]{:S(2)}, u32[]{:S(2)}) collective-permute-start(bf16[1,16,2048]{2,1,0:T(8,128)(2,1)S(1)} %get-tuple-element.48), channel_id=1, source_target_pairs={{0,24},{2,26},{4,28},{6,30},{8,0},{10,2},{12,4},{14,6},{16,8},{18,... | collective-permute-start | bytes 196616 | tf_op jit(solution)/shard_map/ppermute | solution.py:235
  62.6 0.0 collective-permute-start.8
  62.6 2.3 %collective-permute-start.9 = (bf16[1,16,2048]{2,1,0:T(8,128)(2,1)S(1)}, bf16[1,16,2048]{2,1,0:T(8,128)(2,1)S(1)}, u32[]{:S(2)}, u32[]{:S(2)}) collective-permute-start(bf16[1,16,2048]{2,1,0:T(8,128)(2,1)S(1)} %get-tuple-element.47), channel_id=1, source_target_pairs={{0,16},{2,18},{4,20},{6,22},{8,24},{10,26},{12,28},{14,30},{16,0},... | collective-permute-start | bytes 196616 | tf_op jit(solution)/shard_map/ppermute | solution.py:235
  64.9 2.0 %collective-permute-done.12.refs_1_ = bf16[4,16,2048]{2,1,0:T(8,128)(2,1)S(1)} collective-permute-done((bf16[4,16,2048]{2,1,0:T(8,128)(2,1)S(1)}, bf16[4,16,2048]{2,1,0:T(8,128)(2,1)S(1)}, u32[]{:S(2)}, u32[]{:S(2)}) %collective-permute-start.12) | collective-permute-done | bytes 262176 | tf_op jit(solution)/shard_map/ppermute | solution.py:235
  66.9 1.8 %collective-permute-start.13 = (bf16[1,16,2048]{2,1,0:T(8,128)(2,1)S(1)}, bf16[1,16,2048]{2,1,0:T(8,128)(2,1)S(1)}, u32[]{:S(2)}, u32[]{:S(2)}) collective-permute-start(bf16[1,16,2048]{2,1,0:T(8,128)(2,1)S(1)} %get-tuple-element.57), channel_id=1, source_target_pairs={{0,8},{2,10},{4,12},{6,14},{8,16},{10,18},{12,20},{14,22},{16,24},... | collective-permute-start | bytes 196616 | tf_op jit(solution)/shard_map/ppermute | solution.py:235
  68.7 2.6 %collective-permute-start.14 = (bf16[1,16,2048]{2,1,0:T(8,128)(2,1)S(1)}, bf16[1,16,2048]{2,1,0:T(8,128)(2,1)S(1)}, u32[]{:S(2)}, u32[]{:S(2)}) collective-permute-start(bf16[1,16,2048]{2,1,0:T(8,128)(2,1)S(1)} %get-tuple-element.58), channel_id=1, source_target_pairs={{0,16},{2,18},{4,20},{6,22},{8,24},{10,26},{12,28},{14,30},{16,0},... | collective-permute-start | bytes 196616 | tf_op jit(solution)/shard_map/ppermute | solution.py:235
  71.3 0.0 collective-permute-done.10.refs_3_
  71.3 1.3 %collective-permute-start.15 = (bf16[1,16,2048]{2,1,0:T(8,128)(2,1)S(1)}, bf16[1,16,2048]{2,1,0:T(8,128)(2,1)S(1)}, u32[]{:S(2)}, u32[]{:S(2)}) collective-permute-start(bf16[1,16,2048]{2,1,0:T(8,128)(2,1)S(1)} %get-tuple-element.59), channel_id=1, source_target_pairs={{0,24},{2,26},{4,28},{6,30},{8,0},{10,2},{12,4},{14,6},{16,8},{18,... | collective-permute-start | bytes 196616 | tf_op jit(solution)/shard_map/ppermute | solution.py:235
  72.7 0.0 collective-permute-done.8.refs_1_
  72.7 0.0 collective-permute-done.9.refs_2_
  72.7 0.0 copy-start.3
  72.7 0.6 copy-done.3
  73.4 0.5 collective-permute-done.13.refs_1_
  73.9 2.1 %collective-permute-done.14.refs_2_ = bf16[1,16,2048]{2,1,0:T(8,128)(2,1)S(1)} collective-permute-done((bf16[1,16,2048]{2,1,0:T(8,128)(2,1)S(1)}, bf16[1,16,2048]{2,1,0:T(8,128)(2,1)S(1)}, u32[]{:S(2)}, u32[]{:S(2)}) %collective-permute-start.14) | collective-permute-done | bytes 65568 | tf_op jit(solution)/shard_map/ppermute | solution.py:235
  75.9 0.0 collective-permute-done.15.refs_3_
  76.0 1.0 %collective-permute-start.16 = (f32[16,2048]{1,0:T(8,128)S(1)}, f32[16,2048]{1,0:T(8,128)S(1)}, u32[]{:S(2)}, u32[]{:S(2)}) collective-permute-start(f32[16,2048]{1,0:T(8,128)S(1)} %bitcast.20), channel_id=1, source_target_pairs={{0,1},{1,0},{2,3},{3,2},{4,5},{5,4},{6,7},{7,6},{8,9},{9,8},{10,11... | collective-permute-start | bytes 393224 | tf_op jit(solution)/shard_map/ppermute | solution.py:235
  76.9 0.0 copy-done.7
  76.9 0.0 copy-done.8
  76.9 0.6 fusion.5
  77.6 3.4 %collective-permute-done.16.refs_1_ = f32[16,2048]{1,0:T(8,128)S(1)} collective-permute-done((f32[16,2048]{1,0:T(8,128)S(1)}, f32[16,2048]{1,0:T(8,128)S(1)}, u32[]{:S(2)}, u32[]{:S(2)}) %collective-permute-start.16) | collective-permute-done | bytes 131104 | tf_op jit(solution)/shard_map/ppermute | solution.py:235
  81.0 0.0 copy-start.6
  81.0 0.6 copy-done.6
  81.6 5.6 %finish.1 = (f32[16,8,512]{2,1,0:T(8,128)}, f32[16,1024]{1,0:T(8,128)}) custom-call(s32[1]{0:T(128)} %bitcast.me_ref, s32[1,2048]{1,0:T(1,128)} %bitcast.23, f32[16,2048]{1,0:T(8,128)} %bitcast.17, f32[16,2048]{1,0:T(8,128)} %copy-done.6, f32[2048,1024]{1,0:T(8,128)} %refs_2_.1), custom_call_target="tpu_custom_call" | custom-call | flops 1 | bytes 1 | tf_op jit(solution)/shard_map/finish/pallas_call | solution.py:305
  (4 shorter events, 0.2 us)
Async XLA Ops:
  2.9 6.0 %collective-permute-start = (bf16[8,3,8,128]{3,2,1,0:T(8,128)(2,1)}, bf16[8,3,8,128]{3,2,1,0:T(8,128)(2,1)S(1)}, u32[]{:S(2)}, u32[]{:S(2)}) collective-permute-start(bf16[8,3,8,128]{3,2,1,0:T(8,128)(2,1)} %choose.1.after_ref.chosen_ref), channel_id=1, source_target_pairs={{0,1},{1,0},{2,3},{3,2},{4,5},{5,4},{6,7},{7,6},{8,9},{9,8},{10,11... | collective-permute-start | bytes 147464 | tf_op jit(solution)/shard_map/ppermute | solution.py:235
  5.9 1.4 %copy-start = (bf16[3,256,4,2,128]{4,3,2,1,0:T(2,128)(2,1)S(1)}, bf16[3,256,4,2,128]{4,3,2,1,0:T(2,128)(2,1)}, u32[]{:S(2)}) copy-start(bf16[3,256,4,2,128]{4,3,2,1,0:T(2,128)(2,1)} %param.7) | copy-start | bytes 4718596
  7.3 0.8 copy-start.1
  8.1 11.6 %copy-start.2 = (bf16[8,3,8,128]{3,2,1,0:T(8,128)(2,1)S(1)}, bf16[8,3,8,128]{3,2,1,0:T(8,128)(2,1)}, u32[]{:S(2)}) copy-start(bf16[8,3,8,128]{3,2,1,0:T(8,128)(2,1)} %choose.1.after_ref.chosen_ref) | copy-start | bytes 147460
  8.1 11.6 %copy-start.4 = (s32[4,2,128]{2,1,0:T(2,128)S(1)}, s32[4,2,128]{2,1,0:T(2,128)}, u32[]{:S(2)}) copy-start(s32[4,2,128]{2,1,0:T(2,128)} %param.8) | copy-start | bytes 12292
  8.1 11.6 %copy-start.5 = (f32[8]{0:T(128)S(1)}, f32[8]{0:T(128)}, u32[]{:S(2)}) copy-start(f32[8]{0:T(128)} %volume_ref.3) | copy-start | bytes 100
  8.9 43.5 %collective-permute-start.7 = (bf16[256,3072]{1,0:T(8,128)(2,1)S(1)}, bf16[256,3072]{1,0:T(8,128)(2,1)S(1)}, u32[]{:S(2)}, u32[]{:S(2)}) collective-permute-start(bf16[256,3072]{1,0:T(8,128)(2,1)S(1)} %together.1.after_ref.left_ref), channel_id=1, source_target_pairs={{0,1},{1,0},{2,3},{3,2},{4,5},{5,4},{6,7},{7,6},{8,9},{9,8},{10,11... | collective-permute-start | bytes 4718600 | tf_op jit(solution)/shard_map/ppermute | solution.py:235
  10.7 9.0 %collective-permute-start.2 = (bf16[256,1024]{1,0:T(8,128)(2,1)S(1)}, bf16[256,1024]{1,0:T(8,128)(2,1)S(1)}, u32[]{:S(2)}, u32[]{:S(2)}) collective-permute-start(bf16[256,1024]{1,0:T(8,128)(2,1)S(1)} %get-tuple-element.33.refs_0_.after_ref), channel_id=1, source_target_pairs={{2,0},{4,2},{6,4},{8,6},{10,8},{12,10},{14,12},{16,14},{18,16},{20... | collective-permute-start | bytes 1572872 | tf_op jit(solution)/shard_map/ppermute | solution.py:347
  12.0 7.7 %collective-permute-start.1 = (bf16[256,1024]{1,0:T(8,128)(2,1)S(1)}, bf16[256,1024]{1,0:T(8,128)(2,1)S(1)}, u32[]{:S(2)}, u32[]{:S(2)}) collective-permute-start(bf16[256,1024]{1,0:T(8,128)(2,1)S(1)} %get-tuple-element.34.refs_1_), channel_id=1, source_target_pairs={{0,2},{2,4},{4,6},{6,8},{8,10},{10,12},{12,14},{14,16},{16,18},{18... | collective-permute-start | bytes 1572872 | tf_op jit(solution)/shard_map/ppermute | solution.py:347
  15.4 9.7 %collective-permute-start.3 = (bf16[256,512]{1,0:T(8,128)(2,1)S(1)}, bf16[256,512]{1,0:T(8,128)(2,1)S(1)}, u32[]{:S(2)}, u32[]{:S(2)}) collective-permute-start(bf16[256,512]{1,0:T(8,128)(2,1)S(1)} %get-tuple-element.35.refs_1_), channel_id=1, source_target_pairs={{0,2},{2,4},{4,6},{6,8},{8,10},{10,12},{12,14},{14,16},{16,18},{18... | collective-permute-start | bytes 786440 | tf_op jit(solution)/shard_map/ppermute | solution.py:347
  18.4 6.8 %collective-permute-start.4 = (bf16[256,512]{1,0:T(8,128)(2,1)S(1)}, bf16[256,512]{1,0:T(8,128)(2,1)S(1)}, u32[]{:S(2)}, u32[]{:S(2)}) collective-permute-start(bf16[256,512]{1,0:T(8,128)(2,1)S(1)} %get-tuple-element.36.refs_0_), channel_id=1, source_target_pairs={{2,0},{4,2},{6,4},{8,6},{10,8},{12,10},{14,12},{16,14},{18,16},{20... | collective-permute-start | bytes 786440 | tf_op jit(solution)/shard_map/ppermute | solution.py:347
  32.1 10.8 %collective-permute-start.5 = (bf16[8,16,2048]{2,1,0:T(8,128)(2,1)S(1)}, bf16[8,16,2048]{2,1,0:T(8,128)(2,1)S(1)}, u32[]{:S(2)}, u32[]{:S(2)}) collective-permute-start(bf16[8,16,2048]{2,1,0:T(8,128)(2,1)S(1)} %get-tuple-element.41), channel_id=1, source_target_pairs={{0,2},{2,0},{4,6},{6,4},{8,10},{10,8},{12,14},{14,12},{16,18},{18,... | collective-permute-start | bytes 1572872 | tf_op jit(solution)/shard_map/ppermute | solution.py:235
  43.0 9.4 %collective-permute-start.6 = (bf16[4,16,2048]{2,1,0:T(8,128)(2,1)S(1)}, bf16[4,16,2048]{2,1,0:T(8,128)(2,1)S(1)}, u32[]{:S(2)}, u32[]{:S(2)}) collective-permute-start(bf16[4,16,2048]{2,1,0:T(8,128)(2,1)S(1)} %get-tuple-element.43), channel_id=1, source_target_pairs={{0,4},{2,6},{4,0},{6,2},{8,12},{10,14},{12,8},{14,10},{16,20},{18,... | collective-permute-start | bytes 786440 | tf_op jit(solution)/shard_map/ppermute | solution.py:235
  52.5 24.5 %copy-start.7 = (s32[2048]{0:T(1024)S(1)}, s32[2048]{0:T(1024)}, u32[]{:S(2)}) copy-start(s32[2048]{0:T(1024)} %param.11) | copy-start | bytes 24580
  52.5 24.5 %copy-start.8 = (s32[2048]{0:T(1024)S(1)}, s32[2048]{0:T(1024)}, u32[]{:S(2)}) copy-start(s32[2048]{0:T(1024)} %param.12) | copy-start | bytes 24580
  56.4 2.0 %collective-permute-start.11 = (bf16[8,16,2048]{2,1,0:T(8,128)(2,1)S(1)}, bf16[8,16,2048]{2,1,0:T(8,128)(2,1)S(1)}, u32[]{:S(2)}, u32[]{:S(2)}) collective-permute-start(bf16[8,16,2048]{2,1,0:T(8,128)(2,1)S(1)} %get-tuple-element.51), channel_id=1, source_target_pairs={{0,2},{2,0},{4,6},{6,4},{8,10},{10,8},{12,14},{14,12},{16,18},{18,... | collective-permute-start | bytes 1572872 | tf_op jit(solution)/shard_map/ppermute | solution.py:235
  58.5 8.4 %collective-permute-start.12 = (bf16[4,16,2048]{2,1,0:T(8,128)(2,1)S(1)}, bf16[4,16,2048]{2,1,0:T(8,128)(2,1)S(1)}, u32[]{:S(2)}, u32[]{:S(2)}) collective-permute-start(bf16[4,16,2048]{2,1,0:T(8,128)(2,1)S(1)} %get-tuple-element.53), channel_id=1, source_target_pairs={{0,4},{2,6},{4,0},{6,2},{8,12},{10,14},{12,8},{14,10},{16,20},{18,... | collective-permute-start | bytes 786440 | tf_op jit(solution)/shard_map/ppermute | solution.py:235
  60.3 11.1 %collective-permute-start.10 = (bf16[1,16,2048]{2,1,0:T(8,128)(2,1)S(1)}, bf16[1,16,2048]{2,1,0:T(8,128)(2,1)S(1)}, u32[]{:S(2)}, u32[]{:S(2)}) collective-permute-start(bf16[1,16,2048]{2,1,0:T(8,128)(2,1)S(1)} %get-tuple-element.48), channel_id=1, source_target_pairs={{0,24},{2,26},{4,28},{6,30},{8,0},{10,2},{12,4},{14,6},{16,8},{18,... | collective-permute-start | bytes 196616 | tf_op jit(solution)/shard_map/ppermute | solution.py:235
  62.6 10.1 %collective-permute-start.8 = (bf16[1,16,2048]{2,1,0:T(8,128)(2,1)S(1)}, bf16[1,16,2048]{2,1,0:T(8,128)(2,1)S(1)}, u32[]{:S(2)}, u32[]{:S(2)}) collective-permute-start(bf16[1,16,2048]{2,1,0:T(8,128)(2,1)S(1)} %get-tuple-element.46), channel_id=1, source_target_pairs={{0,8},{2,10},{4,12},{6,14},{8,16},{10,18},{12,20},{14,22},{16,24},... | collective-permute-start | bytes 196616 | tf_op jit(solution)/shard_map/ppermute | solution.py:235
  62.6 10.1 %collective-permute-start.9 = (bf16[1,16,2048]{2,1,0:T(8,128)(2,1)S(1)}, bf16[1,16,2048]{2,1,0:T(8,128)(2,1)S(1)}, u32[]{:S(2)}, u32[]{:S(2)}) collective-permute-start(bf16[1,16,2048]{2,1,0:T(8,128)(2,1)S(1)} %get-tuple-element.47), channel_id=1, source_target_pairs={{0,16},{2,18},{4,20},{6,22},{8,24},{10,26},{12,28},{14,30},{16,0},... | collective-permute-start | bytes 196616 | tf_op jit(solution)/shard_map/ppermute | solution.py:235
  66.9 7.0 %collective-permute-start.13 = (bf16[1,16,2048]{2,1,0:T(8,128)(2,1)S(1)}, bf16[1,16,2048]{2,1,0:T(8,128)(2,1)S(1)}, u32[]{:S(2)}, u32[]{:S(2)}) collective-permute-start(bf16[1,16,2048]{2,1,0:T(8,128)(2,1)S(1)} %get-tuple-element.57), channel_id=1, source_target_pairs={{0,8},{2,10},{4,12},{6,14},{8,16},{10,18},{12,20},{14,22},{16,24},... | collective-permute-start | bytes 196616 | tf_op jit(solution)/shard_map/ppermute | solution.py:235
  68.7 7.2 %collective-permute-start.14 = (bf16[1,16,2048]{2,1,0:T(8,128)(2,1)S(1)}, bf16[1,16,2048]{2,1,0:T(8,128)(2,1)S(1)}, u32[]{:S(2)}, u32[]{:S(2)}) collective-permute-start(bf16[1,16,2048]{2,1,0:T(8,128)(2,1)S(1)} %get-tuple-element.58), channel_id=1, source_target_pairs={{0,16},{2,18},{4,20},{6,22},{8,24},{10,26},{12,28},{14,30},{16,0},... | collective-permute-start | bytes 196616 | tf_op jit(solution)/shard_map/ppermute | solution.py:235
  71.3 4.6 %collective-permute-start.15 = (bf16[1,16,2048]{2,1,0:T(8,128)(2,1)S(1)}, bf16[1,16,2048]{2,1,0:T(8,128)(2,1)S(1)}, u32[]{:S(2)}, u32[]{:S(2)}) collective-permute-start(bf16[1,16,2048]{2,1,0:T(8,128)(2,1)S(1)} %get-tuple-element.59), channel_id=1, source_target_pairs={{0,24},{2,26},{4,28},{6,30},{8,0},{10,2},{12,4},{14,6},{16,8},{18,... | collective-permute-start | bytes 196616 | tf_op jit(solution)/shard_map/ppermute | solution.py:235
  72.7 0.7 copy-start.3
  76.0 5.0 %collective-permute-start.16 = (f32[16,2048]{1,0:T(8,128)S(1)}, f32[16,2048]{1,0:T(8,128)S(1)}, u32[]{:S(2)}, u32[]{:S(2)}) collective-permute-start(f32[16,2048]{1,0:T(8,128)S(1)} %bitcast.20), channel_id=1, source_target_pairs={{0,1},{1,0},{2,3},{3,2},{4,5},{5,4},{6,7},{7,6},{8,9},{9,8},{10,11... | collective-permute-start | bytes 393224 | tf_op jit(solution)/shard_map/ppermute | solution.py:235
  81.0 0.6 copy-start.6

commit v3 on v2

v3 whole, which is shorter than its diff:
```python
import functools
import math

import jax
import jax.numpy as jnp
from jax import lax
from jax.experimental import pallas as pl
from jax.experimental.pallas import tpu as pltpu
from jax.sharding import PartitionSpec as P

LANES = 128
F32 = jnp.float32
BF16 = jnp.bfloat16


def whole(memory_space=pltpu.VMEM):
    return pl.BlockSpec(memory_space=memory_space)


def params(mib):
    return pltpu.CompilerParams(vmem_limit_bytes=mib * 2**20)


SHORT = pl.CostEstimate(flops=1, bytes_accessed=1, transcendentals=0)


def lead_places(comps, advect_count, lanes):
    pairs = -(-advect_count // 2)
    spot = [divmod(c * pairs + j, lanes // LANES) for c in range(comps) for j in range(pairs)]
    return pairs, [(row * 16, lane * LANES) for row, lane in spot]


def lead_kernel(planes, rows_y, first, count, advect_count, *refs):
    index_ref, pods_ref, wide = refs[0], refs[1], refs[-1]
    ahead = refs[-2].shape == pods_ref.shape
    out_ref = refs[-3] if ahead else refs[-2]
    if ahead:
        refs[-2][...] = pods_ref[...]
    comps, modes, cells, _ = pods_ref.shape
    base = lax.axis_index("mode") * modes
    extra = out_ref.shape[0] - count
    pairs, places = lead_places(comps, advect_count, out_ref.shape[1])
    if extra:
        out_ref[:extra, :] = jnp.zeros((extra, out_ref.shape[1]), BF16)
    for c in range(comps):
        wide[...] = pods_ref[c].astype(F32).reshape(modes * cells, LANES)
        for r in range(rows_y):
            for p in range(planes):
                value = wide[pl.ds(first * cells + p * rows_y + r, count, stride=cells), :]
                at = ((r * comps + c) * planes + p) * LANES
                out_ref[extra:, at : at + LANES] = value.astype(BF16)
        for pair in range(pairs if extra else 0):
            blocks = []
            for j in (2 * pair, 2 * pair + 1):
                local = index_ref[min(j, advect_count - 1)] - base
                inside = jnp.logical_and(local >= 0, local < modes)
                row = pl.multiple_of(jnp.clip(local, 0, modes - 1) * cells, cells)
                blocks.append(jnp.where(inside, wide[pl.ds(row, cells), :], 0.0))
            row, lane = places[c * pairs + pair]
            out_ref[row : row + 2 * cells, lane : lane + LANES] = jnp.concatenate(blocks, axis=0).astype(BF16)


def lead(flat, advect_index, after, planes, rows_y, first, count, ahead):
    comps, modes, cells, width = flat.shape
    lanes = comps * cells * width
    extra = 0
    if ahead:
        _, places = lead_places(comps, advect_index.shape[0], lanes)
        extra = places[-1][0] + 16
    return pl.pallas_call(
        functools.partial(lead_kernel, planes, rows_y, first, count, advect_index.shape[0]),
        in_specs=[whole(pltpu.SMEM), whole()] + [whole(pl.ANY)] * len(after),
        out_specs=[whole()] * (1 + ahead),
        out_shape=[jax.ShapeDtypeStruct((extra + count, lanes), BF16)]
        + [jax.ShapeDtypeStruct(flat.shape, BF16)] * ahead,
        scratch_shapes=[pltpu.VMEM((modes * cells, width), F32)],
        compiler_params=params(8),
        cost_estimate=SHORT,
        name="lead",
    )(advect_index, flat, *after)


def edge_kernel(planes, rows_y, r, pods_ref, after_ref, out_ref, wide):
    comps, modes, cells, _ = pods_ref.shape
    for c in range(comps):
        wide[...] = pods_ref[c].astype(F32).reshape(modes * cells, LANES)
        for p in range(planes):
            value = wide[pl.ds(p * rows_y + r, modes, stride=cells), :]
            at = (c * planes + p) * LANES
            out_ref[:, at : at + LANES] = value.astype(BF16)


def edge(flat, after, planes, rows_y, r):
    comps, modes, cells, width = flat.shape
    return pl.pallas_call(
        functools.partial(edge_kernel, planes, rows_y, r),
        in_specs=[whole(), whole(pl.ANY)],
        out_specs=whole(),
        out_shape=jax.ShapeDtypeStruct((modes, comps * planes * width), BF16),
        scratch_shapes=[pltpu.VMEM((modes * cells, width), F32)],
        compiler_params=params(8),
        cost_estimate=SHORT,
        name="edge",
    )(flat, after)


def weight_kernel(volume_ref, map_ref, after_ref, out_ref):
    slabs = map_ref[...]
    weight = jnp.zeros(slabs.shape, F32)
    for level in range(volume_ref.shape[0]):
        weight = jnp.where(slabs == level, volume_ref[level], weight)
    out_ref[...] = weight


def weights(slab_map, slab_volume, after):
    planes, rows_y, width = slab_map.shape
    shape = (planes * rows_y, width)
    return pl.pallas_call(
        weight_kernel,
        in_specs=[whole(pltpu.SMEM), whole(), whole(pl.ANY)],
        out_specs=whole(),
        out_shape=jax.ShapeDtypeStruct(shape, F32),
        compiler_params=params(8),
        cost_estimate=SHORT,
        name="weights",
    )(slab_volume, slab_map.reshape(shape), after)


def advected_kernel(comps, planes, rows_y, r, tall, weight_ref, here_ref, under_ref, over_ref, *refs):
    lead_refs, out_ref, weighted = refs[:-2], refs[-2], refs[-1]
    advect_count = out_ref.shape[0]
    modes = here_ref.shape[0]
    cells = planes * rows_y
    weight = weight_ref[...]
    pairs, places = lead_places(comps, advect_count, lead_refs[0].shape[1])
    for d in range(comps):
        for pair in range(pairs):
            row, lane = places[d * pairs + pair]
            both = jnp.zeros((2 * cells, LANES), F32)
            for ref in lead_refs:
                both = both + ref[row : row + 2 * cells, lane : lane + LANES].astype(F32)
            for k in range(min(2, advect_count - 2 * pair)):
                weighted[d, 2 * pair + k] = 0.5 * (both[k * cells : (k + 1) * cells] * weight)

    def rounded(x):
        return x.astype(BF16).astype(F32)

    @pl.loop(0, modes // tall)
    def _(b):
        here = pl.ds(pl.multiple_of(b * tall, tall), tall)

        def at(ref, k, p):
            lane = (k * planes + p) * LANES
            return ref[here, lane : lane + LANES].astype(F32)

        for k in range(comps):
            line = [at(here_ref, k, p) for p in range(planes)]
            for p in range(planes):
                grads = (
                    rounded(line[(p + 1) % planes] - line[(p - 1) % planes]),
                    rounded(at(over_ref, k, p) - at(under_ref, k, p)),
                    rounded(pltpu.roll(line[p], LANES - 1, 1) - pltpu.roll(line[p], 1, 1)),
                )
                cell = p * rows_y + r
                lane = (k * planes + p) * LANES
                for j in range(advect_count):
                    total = weighted[0, j, cell : cell + 1, :] * grads[0]
                    for d in range(1, comps):
                        total = total + weighted[d, j, cell : cell + 1, :] * grads[d]
                    out_ref[j, here, lane : lane + LANES] = total.astype(BF16)


def advected(leads, here, under, over, weight, rows_y, r, advect_count):
    cells, width = weight.shape
    planes = cells // rows_y
    modes, depth = here.shape
    comps = depth // (planes * width)
    return pl.pallas_call(
        functools.partial(advected_kernel, comps, planes, rows_y, r, 32),
        in_specs=[whole()] * (len(leads) + 4),
        out_specs=whole(),
        out_shape=jax.ShapeDtypeStruct((advect_count, modes, depth), BF16),
        scratch_shapes=[pltpu.VMEM((comps, advect_count, cells, width), F32)],
        compiler_params=params(8),
        cost_estimate=SHORT,
        name="advected",
    )(weight, here, under, over, *leads)


def digits(number, sizes):
    ways, span = sizes[number], math.prod(sizes[:number])
    own = lax.axis_index("cell") // span % ways
    return [lax.rem(own + s, ways) for s in range(ways)]


def contract_kernel(sizes, wide, rows_y, ahead_ref, rest_ref, *refs):
    right_refs, outs, scratch = refs[:rows_y], refs[rows_y:-1], refs[-1]
    columns = right_refs[0].shape[0]
    extra = ahead_ref.shape[0] - rest_ref.shape[0]
    left = jnp.concatenate([ahead_ref[extra:, :], rest_ref[...]], axis=0)
    places = digits(0, sizes)
    for n in range(columns // wide):
        here = slice(n * wide, (n + 1) * wide)
        right = jnp.concatenate([ref[here, :] for ref in right_refs], axis=1)
        value = lax.dot_general(left, right, (((1,), (1,)), ((), ())), preferred_element_type=F32)
        scratch[n % 2] = value.reshape(scratch.shape[1:])
        for q in range(outs[0].shape[0]):
            for out, place in zip(outs, places):
                out[q, :, here] = scratch[n % 2, q * sizes[0] + place].astype(out.dtype)


def contract(left, right, sizes):
    columns = right[0].shape[0]
    rows = 2 * left[1].shape[0]
    owners = math.prod(sizes)
    wide = min(columns, 256)
    shape = (owners // sizes[0], rows // owners, columns)
    return pl.pallas_call(
        functools.partial(contract_kernel, sizes, wide, len(right)),
        in_specs=[whole()] * (2 + len(right)),
        out_specs=[whole()] * sizes[0],
        out_shape=[jax.ShapeDtypeStruct(shape, BF16 if s else F32) for s in range(sizes[0])],
        scratch_shapes=[pltpu.VMEM((2, owners, rows // owners, wide), F32)],
        compiler_params=params(8),
        cost_estimate=SHORT,
        name="contract",
    )(*left, *right)


def fold_kernel(number, sizes, arrived, *refs):
    kept_ref, arrived_refs, outs = refs[0], refs[1 : 1 + arrived], refs[1 + arrived :]
    places = [0] if number == len(sizes) else digits(number, sizes)
    ways = len(places)
    for q in range(kept_ref.shape[0] // ways):
        for out, place in zip(outs, places):
            total = kept_ref[q * ways + place]
            for ref in arrived_refs:
                total = total + ref[q * ways + place].astype(F32)
            out[q] = total.astype(out.dtype)


def fold(kept, arrived, number, sizes):
    ways = 1 if number == len(sizes) else sizes[number]
    shape = (kept.shape[0] // ways, *kept.shape[1:])
    return pl.pallas_call(
        functools.partial(fold_kernel, number, sizes, len(arrived)),
        in_specs=[whole()] * (1 + len(arrived)),
        out_specs=[whole()] * ways,
        out_shape=[jax.ShapeDtypeStruct(shape, BF16 if s else F32) for s in range(ways)],
        compiler_params=params(8),
        cost_estimate=SHORT,
        name="fold",
    )(kept, *arrived)


def shifted(block, axis, distance, size, span):
    route = []
    for i in range(lax.axis_size(axis)):
        digit = i // span % size
        route.append((i, i + ((digit + distance) % size - digit) * span))
    return lax.ppermute(block, axis, route)


def stages(count):
    sizes = []
    while count % 4 == 0 and count > 4:
        sizes, count = sizes + [4], count // 4
    if count == 4:
        sizes, count = sizes + [2], 2
    return [count] + sizes[::-1] if count > 1 else sizes[::-1]


def stage(parts, number, sizes):
    span = math.prod(sizes[:number])
    arrived = [shifted(part, "cell", s + 1, sizes[number], span) for s, part in enumerate(parts[1:])]
    return fold(parts[0], arrived, number + 1, sizes)


def finish_kernel(advect_count, per_block, scale_factor, adv_ref, mode_ref, *refs):
    *part_refs, amp_ref, tensor_ref, out_ref, flat, both, amps, sems = refs
    blocks, rows = flat.shape[0], flat.shape[1]
    steps, tall, _ = amps.shape
    me = lax.axis_index("mode")
    copies = []
    for i in range(steps):
        copies.append(pltpu.make_async_copy(amp_ref.at[pl.ds(i * tall, tall)], amps.at[i], sems.at[i]))
        copies[-1].start()
    for s, ref in enumerate(part_refs):
        flat[s] = ref[...] * scale_factor
    for b in range(blocks):
        for j in range(advect_count):
            at = slice(j * per_block, (j + 1) * per_block)
            value = flat[0, :, at]
            for s in range(1, blocks):
                value = jnp.where(lax.rem(me + s, blocks) == b, flat[s, :, at], value)
            tensor_ref[:, j, b * per_block : (b + 1) * per_block] = value

    groups = flat.shape[2] // LANES
    for g in range(both.shape[1] // LANES):
        here = slice(g * LANES, (g + 1) * LANES)
        mode = mode_ref[:, here]
        part = lax.rem(mode // per_block - me + blocks, blocks)
        slot = (part * advect_count + adv_ref[:, here]) * per_block + lax.rem(mode, per_block)
        lane = jnp.broadcast_to(lax.rem(slot, LANES), (rows, LANES))
        group = jnp.broadcast_to(slot // LANES, (rows, LANES))
        found = jnp.zeros((rows, LANES), F32)
        for b in range(blocks):
            for s in range(groups):
                source = flat[b, :, s * LANES : (s + 1) * LANES]
                taken = jnp.take_along_axis(source, lane, axis=1)
                found = jnp.where(group == b * groups + s, taken, found)
        high = found.astype(BF16).astype(F32)
        both[:rows, here] = high
        both[rows:, here] = found - high
    total = jnp.zeros(out_ref.shape, F32)
    for i in range(steps):
        copies[i].wait()
        columns = both[:, i * tall : (i + 1) * tall].astype(BF16)
        amp = amps[i]
        high = amp.astype(BF16)
        low = (amp - high.astype(F32)).astype(BF16)
        term = jnp.dot(columns, high, preferred_element_type=F32)
        small = jnp.dot(columns[:rows], low, preferred_element_type=F32)
        total = total + (term[:rows] + (term[rows:] + small))
    out_ref[...] = total


def finish(pair_adv, pair_mode, parts, amp, advect_count, scale_factor):
    pairs, snaps = amp.shape
    tall = 512 if pairs % 512 == 0 else pairs
    rows, columns = parts[0].shape
    blocks = len(parts)
    per_block = columns // advect_count
    return pl.pallas_call(
        functools.partial(finish_kernel, advect_count, per_block, scale_factor),
        in_specs=[whole()] * (2 + blocks) + [whole(pltpu.HBM)],
        out_specs=[whole(), whole()],
        out_shape=[
            jax.ShapeDtypeStruct((rows, advect_count, blocks * per_block), F32),
            jax.ShapeDtypeStruct((rows, snaps), F32),
        ],
        scratch_shapes=[
            pltpu.VMEM((blocks, rows, columns), F32),
            pltpu.VMEM((2 * rows, pairs), F32),
            pltpu.VMEM((pairs // tall, tall, snaps), F32),
            pltpu.SemaphoreType.DMA((pairs // tall,)),
        ],
        compiler_params=params(52),
        cost_estimate=SHORT,
        name="finish",
    )(pair_adv.reshape(1, pairs), pair_mode.reshape(1, pairs), *parts, amp)


def shards(pod_modes, slab_map, slab_volume, advect_index, pair_adv, pair_mode, pair_amp):
    comps, mode_block, planes, rows_y, width = pod_modes.shape
    mode_devs = lax.axis_size("mode")
    cell_devs = lax.axis_size("cell")
    advect_count = advect_index.shape[0]
    scale_factor = float(planes * rows_y * cell_devs * width) ** (-0.5)
    me = lax.axis_index("mode")
    rows_here = mode_block // cell_devs

    flat = pod_modes.reshape(comps, mode_block, planes * rows_y, width)
    half = mode_block // 2
    first, held = lead(flat, advect_index, (), planes, rows_y, 0, half, True)
    own = [first]
    rows, before = {}, own[0]
    for r in [rows_y - 1, *range(rows_y - 1)]:
        rows[r] = edge(held, before, planes, rows_y, r)
        before = rows[r]
    own += lead(held, advect_index, (before,), planes, rows_y, half, mode_block - half, False)
    weight = weights(slab_map, slab_volume, own[1])
    arrived = [[shifted(block, "mode", s, mode_devs, 1) for block in own] for s in range(1, mode_devs)]
    up = [(i, i + 1) for i in range(cell_devs - 1)]
    rows[-1] = lax.ppermute(rows[rows_y - 1], "cell", up)
    rows[rows_y] = lax.ppermute(rows[0], "cell", [(j, i) for i, j in up])
    leads = [own[0]] + [block[0] for block in arrived]
    right = []
    for r in range(rows_y):
        if right:
            right[-1], rows[r + 1] = lax.optimization_barrier((right[-1], rows[r + 1]))
        block = advected(leads, rows[r], rows[r - 1], rows[r + 1], weight, rows_y, r, advect_count)
        right.append(block.reshape(-1, block.shape[-1]))

    sizes = stages(cell_devs)
    early = min(1, len(sizes))

    def summed(parts, first, last):
        for number in range(first, min(last, len(sizes))):
            parts = stage(parts, number, sizes)
        return list(parts)

    mine = summed(contract(own, right, sizes), 0, early)
    mine[0], arrived = lax.optimization_barrier((mine[0], arrived))
    mine = summed(mine, early, early + 1)
    result = []
    for s in range(1, mode_devs):
        block = contract(arrived[s - 1], right, sizes)
        if s == 1:
            mine, block = lax.optimization_barrier((mine, block))
        block = summed(block, 0, early + 1)
        if s == 1:
            mine = summed(mine, early + 1, len(sizes))
            mine, block = lax.optimization_barrier((mine, block))
            result.append(mine[0][0])
        block = summed(block, early + 1, len(sizes))[0][0]
        result.append(shifted(block, "mode", mode_devs - s, mode_devs, 1))
    tensor, response = finish(pair_adv, pair_mode, result, pair_amp, advect_count, scale_factor)
    return (tensor, response)


def solution(mesh):
    in_specs = (P(None, "mode", None, "cell", None), P(None, "cell", None), P(), P(), P(), P(), P())
    out_specs = (P(("mode", "cell"), None, None), P(("mode", "cell"), None))
    return jax.shard_map(shards, mesh=mesh, in_specs=in_specs, out_specs=out_specs, check_vma=False)
```

time: 87.8 us -> 81.6 us (0.929)
  starting transfers between devices: 38.1 us -> 21.9 us
  waiting for transfers between devices: 18.1 us -> 33.2 us
  Pallas kernels: 26 us -> 23.3 us
  local copies, waits for them, and re-layouts: 3.52 us -> 2.08 us
    ppermute x13, waiting for transfers between devices: 18 us -> 33.2 us  [shifted(): return lax.ppermute(block, axis, route)]
    ppermute x13, starting transfers between devices: 29.5 us -> 19.1 us  [shifted(): return lax.ppermute(block, axis, route)]
    ppermute x4 -> x2, starting transfers between devices: 8.65 us -> 2.8 us  [the longest x1 1.51 us: shards(): rows[-1] = lax.ppermute(rows[rows_y - 1], 'cell', up)]
    pallas_call x8 -> x9, Pallas kernels: 20.1 us -> 18.4 us  [the longest x2 7.84 us: contract(): pl.pallas_call(functools.partial(contract_kernel, sizes, wide, len(right)...]
    unnamed x18 -> x12, local copies, waits for them, and re-layouts: 3.52 us -> 2.08 us
    pallas_call x1, Pallas kernels: 5.58 us -> 4.62 us  [finish(): pl.pallas_call(functools.partial(finish_kernel, advect_count, per_block,...]
  transfers between devices with their start and end apart: 17 -> 15, of which waited for: 7 -> 9; matrix products, arithmetic and copies ran while one was open for 1% -> 0% of each run, Pallas kernels for 16% -> 21%
where the time goes in v3:
time: 81.6 us; the launch traced here: 81.4 us
  waiting for transfers between devices  33.2 us (41%)
  Pallas kernels  23.3 us (29%)
  starting transfers between devices  21.9 us (27%)
  local copies, waits for them, and re-layouts  2.08 us (3%)
  between operations  0.95 us (1%)
    ppermute x13, waiting for transfers between devices, shifted(): return lax.ppermute(block, axis, route)  33.2 us
    ppermute x13, starting transfers between devices, shifted(): return lax.ppermute(block, axis, route)  19.1 us
    pallas_call x2, Pallas kernels, contract(): pl.pallas_call(functools.partial(contract_kernel, sizes, wide, len(right)...  7.84 us
    pallas_call x2, Pallas kernels, advected(): pl.pallas_call(functools.partial(advected_kernel, comps, planes, rows_y,...  6.8 us
    pallas_call x1, Pallas kernels, finish(): pl.pallas_call(functools.partial(finish_kernel, advect_count, per_block,...  4.62 us
    pallas_call x2, Pallas kernels, lead(): pl.pallas_call(functools.partial(lead_kernel, planes, rows_y, first, coun...  2.15 us
    unnamed x12, local copies, waits for them, and re-layouts  2.08 us
  transfers between devices with their start and end apart: 15, of which 9 were waited for; matrix products, arithmetic and copies ran while one was open for 0% of the time, Pallas kernels for 21%

profile of v3, /device:TPU:0, one launch (start us, length us, event | category | flops | bytes accessed | tf_op | source)
XLA Modules:
  0.0 81.4 jit_solution(17511021258035916006)
XLA Ops:
  0.6 0.0 copy-start.5
  0.6 0.0 copy-start
  0.7 1.4 %copy-done = bf16[3,256,4,2,128]{4,3,2,1,0:T(2,128)(2,1)S(1)} copy-done((bf16[3,256,4,2,128]{4,3,2,1,0:T(2,128)(2,1)S(1)}, bf16[3,256,4,2,128]{4,3,2,1,0:T(2,128)(2,1)}, u32[]{:S(2)}) %copy-start) | copy-done | bytes 1572888
  2.1 0.0 copy-start.4
  2.1 0.7 copy-done.4
  2.7 0.0 copy-start.3
  2.7 1.2 %lead.2 = (bf16[144,3072]{1,0:T(8,128)(2,1)S(1)}, bf16[3,256,8,128]{3,2,1,0:T(8,128)(2,1)S(1)}) custom-call(s32[8]{0:T(128)S(1)} %copy-done.4, bf16[3,256,8,128]{3,2,1,0:T(8,128)(2,1)S(1)} %bitcast.12), custom_call_target="tpu_custom_call" | custom-call | flops 1 | bytes 1 | tf_op jit(solution)/shard_map/lead/pallas_call | solution.py:70
  3.9 3.0 %collective-permute-start.1 = (bf16[144,3072]{1,0:T(8,128)(2,1)S(1)}, bf16[144,3072]{1,0:T(8,128)(2,1)S(1)}, u32[]{:S(2)}, u32[]{:S(2)}) collective-permute-start(bf16[144,3072]{1,0:T(8,128)(2,1)S(1)} %get-tuple-element.36.after_ref.refs_0_.ahead_ref), channel_id=1, source_target_pairs={{0,1},{1,0},{2,3},{3,2},{4,5},{5,4},{6,7},{7,6},{8,9},{9,8},{10,11... | collective-permute-start | bytes 2654216 | tf_op jit(solution)/shard_map/ppermute | solution.py:261
  7.0 0.5 edge.2.after_ref.over_ref.here_ref
  7.5 1.5 %collective-permute-start = (bf16[256,1536]{1,0:T(8,128)(2,1)S(1)}, bf16[256,1536]{1,0:T(8,128)(2,1)S(1)}, u32[]{:S(2)}, u32[]{:S(2)}) collective-permute-start(bf16[256,1536]{1,0:T(8,128)(2,1)S(1)} %edge.2.after_ref.over_ref.here_ref), channel_id=1, source_target_pairs={{0,2},{2,4},{4,6},{6,8},{8,10},{10,12},{12,14},{14,16},{16,18},{18... | collective-permute-start | bytes 2359304 | tf_op jit(solution)/shard_map/ppermute | solution.py:375
  9.0 0.5 edge.3.refs_2_.here_ref.under_ref
  9.5 1.3 %collective-permute-start.2 = (bf16[256,1536]{1,0:T(8,128)(2,1)S(1)}, bf16[256,1536]{1,0:T(8,128)(2,1)S(1)}, u32[]{:S(2)}, u32[]{:S(2)}) collective-permute-start(bf16[256,1536]{1,0:T(8,128)(2,1)S(1)} %edge.3.refs_2_.here_ref.under_ref), channel_id=1, source_target_pairs={{2,0},{4,2},{6,4},{8,6},{10,8},{12,10},{14,12},{16,14},{18,16},{20... | collective-permute-start | bytes 2359304 | tf_op jit(solution)/shard_map/ppermute | solution.py:376
  10.8 0.9 %lead.3.after_ref.rest_ref = bf16[128,3072]{1,0:T(8,128)(2,1)S(1)} custom-call(s32[8]{0:T(128)S(1)} %copy-done.4, bf16[3,256,8,128]{3,2,1,0:T(8,128)(2,1)S(1)} %get-tuple-element.37.pods_ref.refs_1_, bf16[256,1536]{1,0:T(8,128)(2,1)S(1)} %edge.3.refs_2_.here_ref.under_ref), custom_call_target="tpu_custom_call" | custom-call | flops 1 | bytes 1 | tf_op jit(solution)/shard_map/lead/pallas_call | solution.py:70
  11.8 0.4 collective-permute-start.4
  12.1 0.0 copy-done.5
  12.1 0.0 copy-done.3
  12.1 0.5 weights.1.weight_ref
  12.7 0.0 collective-permute-done.under_ref
  12.7 14.7 %collective-permute-done.1.refs_1_.ahead_ref = bf16[144,3072]{1,0:T(8,128)(2,1)S(1)} collective-permute-done((bf16[144,3072]{1,0:T(8,128)(2,1)S(1)}, bf16[144,3072]{1,0:T(8,128)(2,1)S(1)}, u32[]{:S(2)}, u32[]{:S(2)}) %collective-permute-start.1) | collective-permute-done | bytes 884768 | tf_op jit(solution)/shard_map/ppermute | solution.py:261
  27.4 3.4 %advected.2 = bf16[8,256,1536]{2,1,0:T(8,128)(2,1)S(1)} custom-call(f32[8,128]{1,0:T(8,128)S(1)} %weights.1.weight_ref, bf16[256,1536]{1,0:T(8,128)(2,1)S(1)} %edge.3.refs_2_.here_ref.under_ref, bf16[256,1536]{1,0:T(8,128)(2,1)S(1)} %collective-permute-done.under_ref, bf16[256,1536]{1,0:T(8,128)(2,1)S(1)} %edge.2.after_ref.over_ref.here_ref, ...), custom_call_target="tpu_custom_call" | custom-call | flops 1 | bytes 1 | tf_op jit(solution)/shard_map/advected/pallas_call | solution.py:178
  30.8 0.0 collective-permute-done.2.over_ref
  30.9 3.4 %advected.3 = bf16[8,256,1536]{2,1,0:T(8,128)(2,1)S(1)} custom-call(f32[8,128]{1,0:T(8,128)S(1)} %weights.1.weight_ref, bf16[256,1536]{1,0:T(8,128)(2,1)S(1)} %edge.2.after_ref.over_ref.here_ref, bf16[256,1536]{1,0:T(8,128)(2,1)S(1)} %edge.3.refs_2_.here_ref.under_ref, bf16[256,1536]{1,0:T(8,128)(2,1)S(1)} %collective-permute-done.2.over_ref, ...), custom_call_target="tpu_custom_call" | custom-call | flops 1 | bytes 1 | tf_op jit(solution)/shard_map/advected/pallas_call | solution.py:178
  34.3 3.9 %contract.2 = (f32[8,16,2048]{2,1,0:T(8,128)S(1)}, bf16[8,16,2048]{2,1,0:T(8,128)(2,1)S(1)}) custom-call(bf16[144,3072]{1,0:T(8,128)(2,1)S(1)} %get-tuple-element.36.after_ref.refs_0_.ahead_ref, bf16[128,3072]{1,0:T(8,128)(2,1)S(1)} %lead.3.after_ref.rest_ref, bf16[2048,1536]{1,0:T(8,128)(2,1)S(1)} %bitcast.8, bf16[2048,1536]{1,0:T(8,128)(2,1)S(1)} %bitcast.10), custom_call_target="tpu_custom_call" | custom-call | flops 1 | bytes 1 | tf_op jit(solution)/shard_map/contract/pallas_call | solution.py:218
  38.2 1.0 %collective-permute-start.3 = (bf16[8,16,2048]{2,1,0:T(8,128)(2,1)S(1)}, bf16[8,16,2048]{2,1,0:T(8,128)(2,1)S(1)}, u32[]{:S(2)}, u32[]{:S(2)}) collective-permute-start(bf16[8,16,2048]{2,1,0:T(8,128)(2,1)S(1)} %get-tuple-element.41), channel_id=1, source_target_pairs={{0,2},{2,0},{4,6},{6,4},{8,10},{10,8},{12,14},{14,12},{16,18},{18,... | collective-permute-start | bytes 1572872 | tf_op jit(solution)/shard_map/ppermute | solution.py:261
  39.2 1.5 %collective-permute-done.3.refs_1_ = bf16[8,16,2048]{2,1,0:T(8,128)(2,1)S(1)} collective-permute-done((bf16[8,16,2048]{2,1,0:T(8,128)(2,1)S(1)}, bf16[8,16,2048]{2,1,0:T(8,128)(2,1)S(1)}, u32[]{:S(2)}, u32[]{:S(2)}) %collective-permute-start.3) | collective-permute-done | bytes 524320 | tf_op jit(solution)/shard_map/ppermute | solution.py:261
  40.7 0.1 fold.6
  40.8 2.8 %collective-permute-start.5 = (bf16[4,16,2048]{2,1,0:T(8,128)(2,1)S(1)}, bf16[4,16,2048]{2,1,0:T(8,128)(2,1)S(1)}, u32[]{:S(2)}, u32[]{:S(2)}) collective-permute-start(bf16[4,16,2048]{2,1,0:T(8,128)(2,1)S(1)} %get-tuple-element.44), channel_id=1, source_target_pairs={{0,4},{2,6},{4,0},{6,2},{8,12},{10,14},{12,8},{14,10},{16,20},{18,... | collective-permute-start | bytes 786440 | tf_op jit(solution)/shard_map/ppermute | solution.py:261
  43.6 0.0 collective-permute-done.4.rest_ref
  43.6 0.0 copy-start.1
  43.6 0.0 copy-start.2
  43.6 3.9 %contract.3 = (f32[8,16,2048]{2,1,0:T(8,128)S(1)}, bf16[8,16,2048]{2,1,0:T(8,128)(2,1)S(1)}) custom-call(bf16[144,3072]{1,0:T(8,128)(2,1)S(1)} %collective-permute-done.1.refs_1_.ahead_ref, bf16[128,3072]{1,0:T(8,128)(2,1)S(1)} %collective-permute-done.4.rest_ref, bf16[2048,1536]{1,0:T(8,128)(2,1)S(1)} %bitcast.9, bf16[2048,1536]{1,0:T(8,128)(2,1)S(1)} %bitcast.11), custom_call_target="tpu_custom_call" | custom-call | flops 1 | bytes 1 | tf_op jit(solution)/shard_map/contract/pallas_call | solution.py:218
  47.5 2.7 %collective-permute-done.5.refs_1_ = bf16[4,16,2048]{2,1,0:T(8,128)(2,1)S(1)} collective-permute-done((bf16[4,16,2048]{2,1,0:T(8,128)(2,1)S(1)}, bf16[4,16,2048]{2,1,0:T(8,128)(2,1)S(1)}, u32[]{:S(2)}, u32[]{:S(2)}) %collective-permute-start.5) | collective-permute-done | bytes 262176 | tf_op jit(solution)/shard_map/ppermute | solution.py:261
  50.3 0.1 collective-permute-start.9
  50.3 1.9 %collective-permute-done.9.refs_1_ = bf16[8,16,2048]{2,1,0:T(8,128)(2,1)S(1)} collective-permute-done((bf16[8,16,2048]{2,1,0:T(8,128)(2,1)S(1)}, bf16[8,16,2048]{2,1,0:T(8,128)(2,1)S(1)}, u32[]{:S(2)}, u32[]{:S(2)}) %collective-permute-start.9) | collective-permute-done | bytes 524320 | tf_op jit(solution)/shard_map/ppermute | solution.py:261
  52.2 0.1 fold.9
  52.3 1.8 %collective-permute-start.10 = (bf16[4,16,2048]{2,1,0:T(8,128)(2,1)S(1)}, bf16[4,16,2048]{2,1,0:T(8,128)(2,1)S(1)}, u32[]{:S(2)}, u32[]{:S(2)}) collective-permute-start(bf16[4,16,2048]{2,1,0:T(8,128)(2,1)S(1)} %get-tuple-element.60), channel_id=1, source_target_pairs={{0,4},{2,6},{4,0},{6,2},{8,12},{10,14},{12,8},{14,10},{16,20},{18,... | collective-permute-start | bytes 786440 | tf_op jit(solution)/shard_map/ppermute | solution.py:261
  54.1 1.6 %collective-permute-start.6 = (bf16[1,16,2048]{2,1,0:T(8,128)(2,1)S(1)}, bf16[1,16,2048]{2,1,0:T(8,128)(2,1)S(1)}, u32[]{:S(2)}, u32[]{:S(2)}) collective-permute-start(bf16[1,16,2048]{2,1,0:T(8,128)(2,1)S(1)} %get-tuple-element.54), channel_id=1, source_target_pairs={{0,8},{2,10},{4,12},{6,14},{8,16},{10,18},{12,20},{14,22},{16,24},... | collective-permute-start | bytes 196616 | tf_op jit(solution)/shard_map/ppermute | solution.py:261
  55.7 1.4 %collective-permute-start.7 = (bf16[1,16,2048]{2,1,0:T(8,128)(2,1)S(1)}, bf16[1,16,2048]{2,1,0:T(8,128)(2,1)S(1)}, u32[]{:S(2)}, u32[]{:S(2)}) collective-permute-start(bf16[1,16,2048]{2,1,0:T(8,128)(2,1)S(1)} %get-tuple-element.55), channel_id=1, source_target_pairs={{0,16},{2,18},{4,20},{6,22},{8,24},{10,26},{12,28},{14,30},{16,0},... | collective-permute-start | bytes 196616 | tf_op jit(solution)/shard_map/ppermute | solution.py:261
  57.1 2.6 %collective-permute-start.8 = (bf16[1,16,2048]{2,1,0:T(8,128)(2,1)S(1)}, bf16[1,16,2048]{2,1,0:T(8,128)(2,1)S(1)}, u32[]{:S(2)}, u32[]{:S(2)}) collective-permute-start(bf16[1,16,2048]{2,1,0:T(8,128)(2,1)S(1)} %get-tuple-element.56), channel_id=1, source_target_pairs={{0,24},{2,26},{4,28},{6,30},{8,0},{10,2},{12,4},{14,6},{16,8},{18,... | collective-permute-start | bytes 196616 | tf_op jit(solution)/shard_map/ppermute | solution.py:261
  59.6 1.0 %collective-permute-done.6.refs_1_ = bf16[1,16,2048]{2,1,0:T(8,128)(2,1)S(1)} collective-permute-done((bf16[1,16,2048]{2,1,0:T(8,128)(2,1)S(1)}, bf16[1,16,2048]{2,1,0:T(8,128)(2,1)S(1)}, u32[]{:S(2)}, u32[]{:S(2)}) %collective-permute-start.6) | collective-permute-done | bytes 65568 | tf_op jit(solution)/shard_map/ppermute | solution.py:261
  60.6 2.4 %collective-permute-done.7.refs_2_ = bf16[1,16,2048]{2,1,0:T(8,128)(2,1)S(1)} collective-permute-done((bf16[1,16,2048]{2,1,0:T(8,128)(2,1)S(1)}, bf16[1,16,2048]{2,1,0:T(8,128)(2,1)S(1)}, u32[]{:S(2)}, u32[]{:S(2)}) %collective-permute-start.7) | collective-permute-done | bytes 65568 | tf_op jit(solution)/shard_map/ppermute | solution.py:261
  63.1 0.0 collective-permute-done.8.refs_3_
  63.1 0.0 collective-permute-done.10.refs_1_
  63.1 0.1 fold.10
  63.2 1.6 %collective-permute-start.11 = (bf16[1,16,2048]{2,1,0:T(8,128)(2,1)S(1)}, bf16[1,16,2048]{2,1,0:T(8,128)(2,1)S(1)}, u32[]{:S(2)}, u32[]{:S(2)}) collective-permute-start(bf16[1,16,2048]{2,1,0:T(8,128)(2,1)S(1)} %get-tuple-element.67), channel_id=1, source_target_pairs={{0,8},{2,10},{4,12},{6,14},{8,16},{10,18},{12,20},{14,22},{16,24},... | collective-permute-start | bytes 196616 | tf_op jit(solution)/shard_map/ppermute | solution.py:261
  64.7 1.9 %collective-permute-start.12 = (bf16[1,16,2048]{2,1,0:T(8,128)(2,1)S(1)}, bf16[1,16,2048]{2,1,0:T(8,128)(2,1)S(1)}, u32[]{:S(2)}, u32[]{:S(2)}) collective-permute-start(bf16[1,16,2048]{2,1,0:T(8,128)(2,1)S(1)} %get-tuple-element.68), channel_id=1, source_target_pairs={{0,16},{2,18},{4,20},{6,22},{8,24},{10,26},{12,28},{14,30},{16,0},... | collective-permute-start | bytes 196616 | tf_op jit(solution)/shard_map/ppermute | solution.py:261
  66.7 0.5 collective-permute-start.13
  67.2 2.7 %collective-permute-done.11.refs_1_ = bf16[1,16,2048]{2,1,0:T(8,128)(2,1)S(1)} collective-permute-done((bf16[1,16,2048]{2,1,0:T(8,128)(2,1)S(1)}, bf16[1,16,2048]{2,1,0:T(8,128)(2,1)S(1)}, u32[]{:S(2)}, u32[]{:S(2)}) %collective-permute-start.11) | collective-permute-done | bytes 65568 | tf_op jit(solution)/shard_map/ppermute | solution.py:261
  69.8 1.8 %collective-permute-done.12.refs_2_ = bf16[1,16,2048]{2,1,0:T(8,128)(2,1)S(1)} collective-permute-done((bf16[1,16,2048]{2,1,0:T(8,128)(2,1)S(1)}, bf16[1,16,2048]{2,1,0:T(8,128)(2,1)S(1)}, u32[]{:S(2)}, u32[]{:S(2)}) %collective-permute-start.12) | collective-permute-done | bytes 65568 | tf_op jit(solution)/shard_map/ppermute | solution.py:261
  71.6 0.0 collective-permute-done.13.refs_3_
  71.6 0.6 collective-permute-start.14
  72.2 4.5 %collective-permute-done.14.refs_1_ = f32[16,2048]{1,0:T(8,128)S(1)} collective-permute-done((f32[16,2048]{1,0:T(8,128)S(1)}, f32[16,2048]{1,0:T(8,128)S(1)}, u32[]{:S(2)}, u32[]{:S(2)}) %collective-permute-start.14) | collective-permute-done | bytes 131104 | tf_op jit(solution)/shard_map/ppermute | solution.py:261
  76.7 0.0 copy-done.1
  76.7 0.0 copy-done.2
  76.7 4.6 %finish.1 = (f32[16,8,512]{2,1,0:T(8,128)}, f32[16,1024]{1,0:T(8,128)}) custom-call(s32[1,2048]{1,0:T(1,128)S(1)} %bitcast.15, s32[1,2048]{1,0:T(1,128)S(1)} %bitcast.16, f32[16,2048]{1,0:T(8,128)S(1)} %bitcast.13, f32[16,2048]{1,0:T(8,128)S(1)} %collective-permute-done.14.refs_1_, f32[2048,1024]{1,0:T(8,128)} %refs_2_.1), custom_call_target="tpu_custom_call" | custom-call | flops 1 | bytes 1 | tf_op jit(solution)/shard_map/finish/pallas_call | solution.py:334
  (3 shorter events, 0.1 us)
Async XLA Ops:
  0.6 11.5 %copy-start.5 = (f32[8]{0:T(128)S(1)}, f32[8]{0:T(128)}, u32[]{:S(2)}) copy-start(f32[8]{0:T(128)} %volume_ref.1) | copy-start | bytes 100
  0.6 1.4 %copy-start = (bf16[3,256,4,2,128]{4,3,2,1,0:T(2,128)(2,1)S(1)}, bf16[3,256,4,2,128]{4,3,2,1,0:T(2,128)(2,1)}, u32[]{:S(2)}) copy-start(bf16[3,256,4,2,128]{4,3,2,1,0:T(2,128)(2,1)} %param.7) | copy-start | bytes 4718596
  2.1 0.7 copy-start.4
  2.7 9.4 %copy-start.3 = (s32[4,2,128]{2,1,0:T(2,128)S(1)}, s32[4,2,128]{2,1,0:T(2,128)}, u32[]{:S(2)}) copy-start(s32[4,2,128]{2,1,0:T(2,128)} %param.8) | copy-start | bytes 12292
  3.9 23.5 %collective-permute-start.1 = (bf16[144,3072]{1,0:T(8,128)(2,1)S(1)}, bf16[144,3072]{1,0:T(8,128)(2,1)S(1)}, u32[]{:S(2)}, u32[]{:S(2)}) collective-permute-start(bf16[144,3072]{1,0:T(8,128)(2,1)S(1)} %get-tuple-element.36.after_ref.refs_0_.ahead_ref), channel_id=1, source_target_pairs={{0,1},{1,0},{2,3},{3,2},{4,5},{5,4},{6,7},{7,6},{8,9},{9,8},{10,11... | collective-permute-start | bytes 2654216 | tf_op jit(solution)/shard_map/ppermute | solution.py:261
  7.5 5.2 %collective-permute-start = (bf16[256,1536]{1,0:T(8,128)(2,1)S(1)}, bf16[256,1536]{1,0:T(8,128)(2,1)S(1)}, u32[]{:S(2)}, u32[]{:S(2)}) collective-permute-start(bf16[256,1536]{1,0:T(8,128)(2,1)S(1)} %edge.2.after_ref.over_ref.here_ref), channel_id=1, source_target_pairs={{0,2},{2,4},{4,6},{6,8},{8,10},{10,12},{12,14},{14,16},{16,18},{18... | collective-permute-start | bytes 2359304 | tf_op jit(solution)/shard_map/ppermute | solution.py:375
  9.5 21.3 %collective-permute-start.2 = (bf16[256,1536]{1,0:T(8,128)(2,1)S(1)}, bf16[256,1536]{1,0:T(8,128)(2,1)S(1)}, u32[]{:S(2)}, u32[]{:S(2)}) collective-permute-start(bf16[256,1536]{1,0:T(8,128)(2,1)S(1)} %edge.3.refs_2_.here_ref.under_ref), channel_id=1, source_target_pairs={{2,0},{4,2},{6,4},{8,6},{10,8},{12,10},{14,12},{16,14},{18,16},{20... | collective-permute-start | bytes 2359304 | tf_op jit(solution)/shard_map/ppermute | solution.py:376
  11.8 31.8 %collective-permute-start.4 = (bf16[128,3072]{1,0:T(8,128)(2,1)S(1)}, bf16[128,3072]{1,0:T(8,128)(2,1)S(1)}, u32[]{:S(2)}, u32[]{:S(2)}) collective-permute-start(bf16[128,3072]{1,0:T(8,128)(2,1)S(1)} %lead.3.after_ref.rest_ref), channel_id=1, source_target_pairs={{0,1},{1,0},{2,3},{3,2},{4,5},{5,4},{6,7},{7,6},{8,9},{9,8},{10,11... | collective-permute-start | bytes 2359304 | tf_op jit(solution)/shard_map/ppermute | solution.py:261
  38.2 2.5 %collective-permute-start.3 = (bf16[8,16,2048]{2,1,0:T(8,128)(2,1)S(1)}, bf16[8,16,2048]{2,1,0:T(8,128)(2,1)S(1)}, u32[]{:S(2)}, u32[]{:S(2)}) collective-permute-start(bf16[8,16,2048]{2,1,0:T(8,128)(2,1)S(1)} %get-tuple-element.41), channel_id=1, source_target_pairs={{0,2},{2,0},{4,6},{6,4},{8,10},{10,8},{12,14},{14,12},{16,18},{18,... | collective-permute-start | bytes 1572872 | tf_op jit(solution)/shard_map/ppermute | solution.py:261
  40.8 9.4 %collective-permute-start.5 = (bf16[4,16,2048]{2,1,0:T(8,128)(2,1)S(1)}, bf16[4,16,2048]{2,1,0:T(8,128)(2,1)S(1)}, u32[]{:S(2)}, u32[]{:S(2)}) collective-permute-start(bf16[4,16,2048]{2,1,0:T(8,128)(2,1)S(1)} %get-tuple-element.44), channel_id=1, source_target_pairs={{0,4},{2,6},{4,0},{6,2},{8,12},{10,14},{12,8},{14,10},{16,20},{18,... | collective-permute-start | bytes 786440 | tf_op jit(solution)/shard_map/ppermute | solution.py:261
  43.6 33.1 %copy-start.1 = (s32[2048]{0:T(1024)S(1)}, s32[2048]{0:T(1024)}, u32[]{:S(2)}) copy-start(s32[2048]{0:T(1024)} %param.11) | copy-start | bytes 24580
  43.6 33.1 %copy-start.2 = (s32[2048]{0:T(1024)S(1)}, s32[2048]{0:T(1024)}, u32[]{:S(2)}) copy-start(s32[2048]{0:T(1024)} %param.12) | copy-start | bytes 24580
  50.3 2.0 %collective-permute-start.9 = (bf16[8,16,2048]{2,1,0:T(8,128)(2,1)S(1)}, bf16[8,16,2048]{2,1,0:T(8,128)(2,1)S(1)}, u32[]{:S(2)}, u32[]{:S(2)}) collective-permute-start(bf16[8,16,2048]{2,1,0:T(8,128)(2,1)S(1)} %get-tuple-element.58), channel_id=1, source_target_pairs={{0,2},{2,0},{4,6},{6,4},{8,10},{10,8},{12,14},{14,12},{16,18},{18,... | collective-permute-start | bytes 1572872 | tf_op jit(solution)/shard_map/ppermute | solution.py:261
  52.3 10.8 %collective-permute-start.10 = (bf16[4,16,2048]{2,1,0:T(8,128)(2,1)S(1)}, bf16[4,16,2048]{2,1,0:T(8,128)(2,1)S(1)}, u32[]{:S(2)}, u32[]{:S(2)}) collective-permute-start(bf16[4,16,2048]{2,1,0:T(8,128)(2,1)S(1)} %get-tuple-element.60), channel_id=1, source_target_pairs={{0,4},{2,6},{4,0},{6,2},{8,12},{10,14},{12,8},{14,10},{16,20},{18,... | collective-permute-start | bytes 786440 | tf_op jit(solution)/shard_map/ppermute | solution.py:261
  54.1 6.5 %collective-permute-start.6 = (bf16[1,16,2048]{2,1,0:T(8,128)(2,1)S(1)}, bf16[1,16,2048]{2,1,0:T(8,128)(2,1)S(1)}, u32[]{:S(2)}, u32[]{:S(2)}) collective-permute-start(bf16[1,16,2048]{2,1,0:T(8,128)(2,1)S(1)} %get-tuple-element.54), channel_id=1, source_target_pairs={{0,8},{2,10},{4,12},{6,14},{8,16},{10,18},{12,20},{14,22},{16,24},... | collective-permute-start | bytes 196616 | tf_op jit(solution)/shard_map/ppermute | solution.py:261
  55.7 7.3 %collective-permute-start.7 = (bf16[1,16,2048]{2,1,0:T(8,128)(2,1)S(1)}, bf16[1,16,2048]{2,1,0:T(8,128)(2,1)S(1)}, u32[]{:S(2)}, u32[]{:S(2)}) collective-permute-start(bf16[1,16,2048]{2,1,0:T(8,128)(2,1)S(1)} %get-tuple-element.55), channel_id=1, source_target_pairs={{0,16},{2,18},{4,20},{6,22},{8,24},{10,26},{12,28},{14,30},{16,0},... | collective-permute-start | bytes 196616 | tf_op jit(solution)/shard_map/ppermute | solution.py:261
  57.1 6.0 %collective-permute-start.8 = (bf16[1,16,2048]{2,1,0:T(8,128)(2,1)S(1)}, bf16[1,16,2048]{2,1,0:T(8,128)(2,1)S(1)}, u32[]{:S(2)}, u32[]{:S(2)}) collective-permute-start(bf16[1,16,2048]{2,1,0:T(8,128)(2,1)S(1)} %get-tuple-element.56), channel_id=1, source_target_pairs={{0,24},{2,26},{4,28},{6,30},{8,0},{10,2},{12,4},{14,6},{16,8},{18,... | collective-permute-start | bytes 196616 | tf_op jit(solution)/shard_map/ppermute | solution.py:261
  63.2 6.6 %collective-permute-start.11 = (bf16[1,16,2048]{2,1,0:T(8,128)(2,1)S(1)}, bf16[1,16,2048]{2,1,0:T(8,128)(2,1)S(1)}, u32[]{:S(2)}, u32[]{:S(2)}) collective-permute-start(bf16[1,16,2048]{2,1,0:T(8,128)(2,1)S(1)} %get-tuple-element.67), channel_id=1, source_target_pairs={{0,8},{2,10},{4,12},{6,14},{8,16},{10,18},{12,20},{14,22},{16,24},... | collective-permute-start | bytes 196616 | tf_op jit(solution)/shard_map/ppermute | solution.py:261
  64.7 6.9 %collective-permute-start.12 = (bf16[1,16,2048]{2,1,0:T(8,128)(2,1)S(1)}, bf16[1,16,2048]{2,1,0:T(8,128)(2,1)S(1)}, u32[]{:S(2)}, u32[]{:S(2)}) collective-permute-start(bf16[1,16,2048]{2,1,0:T(8,128)(2,1)S(1)} %get-tuple-element.68), channel_id=1, source_target_pairs={{0,16},{2,18},{4,20},{6,22},{8,24},{10,26},{12,28},{14,30},{16,0},... | collective-permute-start | bytes 196616 | tf_op jit(solution)/shard_map/ppermute | solution.py:261
  66.7 4.9 %collective-permute-start.13 = (bf16[1,16,2048]{2,1,0:T(8,128)(2,1)S(1)}, bf16[1,16,2048]{2,1,0:T(8,128)(2,1)S(1)}, u32[]{:S(2)}, u32[]{:S(2)}) collective-permute-start(bf16[1,16,2048]{2,1,0:T(8,128)(2,1)S(1)} %get-tuple-element.69), channel_id=1, source_target_pairs={{0,24},{2,26},{4,28},{6,30},{8,0},{10,2},{12,4},{14,6},{16,8},{18,... | collective-permute-start | bytes 196616 | tf_op jit(solution)/shard_map/ppermute | solution.py:261
  71.6 5.0 %collective-permute-start.14 = (f32[16,2048]{1,0:T(8,128)S(1)}, f32[16,2048]{1,0:T(8,128)S(1)}, u32[]{:S(2)}, u32[]{:S(2)}) collective-permute-start(f32[16,2048]{1,0:T(8,128)S(1)} %bitcast.14), channel_id=1, source_target_pairs={{0,1},{1,0},{2,3},{3,2},{4,5},{5,4},{6,7},{7,6},{8,9},{9,8},{10,11... | collective-permute-start | bytes 393224 | tf_op jit(solution)/shard_map/ppermute | solution.py:261

commit v4 on v3

--- a/solution.py
+++ b/solution.py
@@ -239,26 +239,28 @@
             out[q] = total.astype(out.dtype)
 
 
-def fold(kept, arrived, number, sizes):
+def fold(kept, arrived, number, sizes, all_leave=False):
     ways = 1 if number == len(sizes) else sizes[number]
     shape = (kept.shape[0] // ways, *kept.shape[1:])
     return pl.pallas_call(
         functools.partial(fold_kernel, number, sizes, len(arrived)),
         in_specs=[whole()] * (1 + len(arrived)),
         out_specs=[whole()] * ways,
-        out_shape=[jax.ShapeDtypeStruct(shape, BF16 if s else F32) for s in range(ways)],
+        out_shape=[jax.ShapeDtypeStruct(shape, BF16 if s or all_leave else F32) for s in range(ways)],
         compiler_params=params(8),
         cost_estimate=SHORT,
         name="fold",
     )(kept, *arrived)
 
 
-def shifted(block, axis, distance, size, span):
+def shifted(block, axis, distance, size, span, turn=0):
+    reach, turns = lax.axis_size(axis), lax.axis_size("mode") if turn else 1
     route = []
-    for i in range(lax.axis_size(axis)):
+    for i in range(reach):
         digit = i // span % size
-        route.append((i, i + ((digit + distance) % size - digit) * span))
-    return lax.ppermute(block, axis, route)
+        to = i + ((digit + distance) % size - digit) * span
+        route += [(i * turns + m, to * turns + (m + turn) % turns) for m in range(turns)]
+    return lax.ppermute(block, (axis, "mode") if turn else axis, route)
 
 
 def stages(count):
@@ -270,23 +272,56 @@
     return [count] + sizes[::-1] if count > 1 else sizes[::-1]
 
 
-def stage(parts, number, sizes):
+def stage(parts, number, sizes, all_leave=False):
     span = math.prod(sizes[:number])
     arrived = [shifted(part, "cell", s + 1, sizes[number], span) for s, part in enumerate(parts[1:])]
-    return fold(parts[0], arrived, number + 1, sizes)
-
-
-def finish_kernel(advect_count, per_block, scale_factor, adv_ref, mode_ref, *refs):
-    *part_refs, amp_ref, tensor_ref, out_ref, flat, both, amps, sems = refs
-    blocks, rows = flat.shape[0], flat.shape[1]
+    return fold(parts[0], arrived, number + 1, sizes, all_leave)
+
+
+def prepare_kernel(amp_ref, high_ref, low_ref, amps, sems):
     steps, tall, _ = amps.shape
-    me = lax.axis_index("mode")
     copies = []
     for i in range(steps):
         copies.append(pltpu.make_async_copy(amp_ref.at[pl.ds(i * tall, tall)], amps.at[i], sems.at[i]))
         copies[-1].start()
-    for s, ref in enumerate(part_refs):
-        flat[s] = ref[...] * scale_factor
+    for i in range(steps):
+        copies[i].wait()
+        amp = amps[i]
+        high = amp.astype(BF16)
+        high_ref[i * tall : (i + 1) * tall, :] = high
+        low_ref[i * tall : (i + 1) * tall, :] = (amp - high.astype(F32)).astype(BF16)
+
+
+def prepare(amp):
+    pairs, snaps = amp.shape
+    tall = 256 if pairs % 256 == 0 else pairs
+    return pl.pallas_call(
+        prepare_kernel,
+        in_specs=[whole(pltpu.HBM)],
+        out_specs=[whole()] * 2,
+        out_shape=[jax.ShapeDtypeStruct(amp.shape, BF16)] * 2,
+        scratch_shapes=[
+            pltpu.VMEM((pairs // tall, tall, snaps), F32),
+            pltpu.SemaphoreType.DMA((pairs // tall,)),
+        ],
+        compiler_params=params(24),
+        cost_estimate=pl.CostEstimate(flops=4 * amp.size, bytes_accessed=8 * amp.size, transcendentals=0),
+        name="prepare",
+    )(amp)
+
+
+def finish_kernel(advect_count, per_block, scale_factor, counts, adv_ref, mode_ref, *refs):
+    *part_refs, high_ref, low_ref, tensor_ref, out_ref, flat = refs
+    blocks, rows = flat.shape[0], flat.shape[1]
+    me = lax.axis_index("mode")
+    tall = 512 if high_ref.shape[0] % 512 == 0 else high_ref.shape[0]
+    steps = high_ref.shape[0] // tall
+    terms = iter(part_refs)
+    for s, count in enumerate(counts):
+        total = next(terms)[0].astype(F32)
+        for _ in range(count - 1):
+            total = total + next(terms)[0].astype(F32)
+        flat[s] = total * scale_factor
     for b in range(blocks):
         for j in range(advect_count):
             at = slice(j * per_block, (j + 1) * per_block)
@@ -296,59 +331,59 @@
             tensor_ref[:, j, b * per_block : (b + 1) * per_block] = value
 
     groups = flat.shape[2] // LANES
-    for g in range(both.shape[1] // LANES):
-        here = slice(g * LANES, (g + 1) * LANES)
-        mode = mode_ref[:, here]
-        part = lax.rem(mode // per_block - me + blocks, blocks)
-        slot = (part * advect_count + adv_ref[:, here]) * per_block + lax.rem(mode, per_block)
-        lane = jnp.broadcast_to(lax.rem(slot, LANES), (rows, LANES))
-        group = jnp.broadcast_to(slot // LANES, (rows, LANES))
-        found = jnp.zeros((rows, LANES), F32)
-        for b in range(blocks):
-            for s in range(groups):
-                source = flat[b, :, s * LANES : (s + 1) * LANES]
-                taken = jnp.take_along_axis(source, lane, axis=1)
-                found = jnp.where(group == b * groups + s, taken, found)
-        high = found.astype(BF16).astype(F32)
-        both[:rows, here] = high
-        both[rows:, here] = found - high
+
+    def columns(i):
+        high, low = [], []
+        for g in range(i * tall // LANES, (i + 1) * tall // LANES):
+            here = slice(g * LANES, (g + 1) * LANES)
+            mode = mode_ref[:, here]
+            part = lax.rem(mode // per_block - me + blocks, blocks)
+            slot = (part * advect_count + adv_ref[:, here]) * per_block + lax.rem(mode, per_block)
+            lane = jnp.broadcast_to(lax.rem(slot, LANES), (rows, LANES))
+            group = jnp.broadcast_to(slot // LANES, (rows, LANES))
+            found = jnp.zeros((rows, LANES), F32)
+            for b in range(blocks):
+                for s in range(groups):
+                    source = flat[b, :, s * LANES : (s + 1) * LANES]
+                    taken = jnp.take_along_axis(source, lane, axis=1)
+                    found = jnp.where(group == b * groups + s, taken, found)
+            high.append(found.astype(BF16).astype(F32))
+            low.append(found - high[-1])
+        both = [jnp.concatenate(high, axis=1), jnp.concatenate(low, axis=1)]
+        return jnp.concatenate(both, axis=0).astype(BF16)
+
     total = jnp.zeros(out_ref.shape, F32)
+    now = columns(0)
     for i in range(steps):
-        copies[i].wait()
-        columns = both[:, i * tall : (i + 1) * tall].astype(BF16)
-        amp = amps[i]
-        high = amp.astype(BF16)
-        low = (amp - high.astype(F32)).astype(BF16)
-        term = jnp.dot(columns, high, preferred_element_type=F32)
-        small = jnp.dot(columns[:rows], low, preferred_element_type=F32)
+        here = slice(i * tall, (i + 1) * tall)
+        term = jnp.dot(now, high_ref[here, :], preferred_element_type=F32)
+        small = jnp.dot(now[:rows], low_ref[here, :], preferred_element_type=F32)
+        if i < steps - 1:
+            now = columns(i + 1)
         total = total + (term[:rows] + (term[rows:] + small))
     out_ref[...] = total
 
 
-def finish(pair_adv, pair_mode, parts, amp, advect_count, scale_factor):
-    pairs, snaps = amp.shape
-    tall = 512 if pairs % 512 == 0 else pairs
-    rows, columns = parts[0].shape
+def finish(pair_adv, pair_mode, parts, high, low, advect_count, scale_factor):
+    pairs, snaps = high.shape
+    _, rows, columns = parts[0][0].shape
     blocks = len(parts)
+    counts = [len(part) for part in parts]
+    terms = [term for part in parts for term in part]
     per_block = columns // advect_count
     return pl.pallas_call(
-        functools.partial(finish_kernel, advect_count, per_block, scale_factor),
-        in_specs=[whole()] * (2 + blocks) + [whole(pltpu.HBM)],
+        functools.partial(finish_kernel, advect_count, per_block, scale_factor, counts),
+        in_specs=[whole()] * (4 + len(terms)),
         out_specs=[whole(), whole()],
         out_shape=[
             jax.ShapeDtypeStruct((rows, advect_count, blocks * per_block), F32),
             jax.ShapeDtypeStruct((rows, snaps), F32),
         ],
-        scratch_shapes=[
-            pltpu.VMEM((blocks, rows, columns), F32),
-            pltpu.VMEM((2 * rows, pairs), F32),
-            pltpu.VMEM((pairs // tall, tall, snaps), F32),
-            pltpu.SemaphoreType.DMA((pairs // tall,)),
-        ],
-        compiler_params=params(52),
+        scratch_shapes=[pltpu.VMEM((blocks, rows, columns), F32)],
+        compiler_params=params(8),
         cost_estimate=SHORT,
         name="finish",
-    )(pair_adv.reshape(1, pairs), pair_mode.reshape(1, pairs), *parts, amp)
+    )(pair_adv.reshape(1, pairs), pair_mode.reshape(1, pairs), *terms, high, low)
 
 
 def shards(pod_modes, slab_map, slab_volume, advect_index, pair_adv, pair_mode, pair_amp):
@@ -383,29 +418,31 @@
         right.append(block.reshape(-1, block.shape[-1]))
 
     sizes = stages(cell_devs)
-    early = min(1, len(sizes))
-
-    def summed(parts, first, last):
-        for number in range(first, min(last, len(sizes))):
+    early, last = min(1, len(sizes)), len(sizes) - 1
+
+    def summed(parts, first, end, sizes):
+        for number in range(first, min(end, len(sizes))):
             parts = stage(parts, number, sizes)
         return list(parts)
 
-    mine = summed(contract(own, right, sizes), 0, early)
+    pairwise = sizes[:-1] + [2, 2] if sizes[-1] == 4 else sizes
+    mine = summed(contract(own, right, pairwise), 0, early, pairwise)
     mine[0], arrived = lax.optimization_barrier((mine[0], arrived))
-    mine = summed(mine, early, early + 1)
+    mine = summed(mine, early, early + 1, pairwise)
     result = []
     for s in range(1, mode_devs):
         block = contract(arrived[s - 1], right, sizes)
         if s == 1:
             mine, block = lax.optimization_barrier((mine, block))
-        block = summed(block, 0, early + 1)
+        block = stage(summed(block, 0, last - 1, sizes), last - 1, sizes, True)
         if s == 1:
-            mine = summed(mine, early + 1, len(sizes))
-            mine, block = lax.optimization_barrier((mine, block))
-            result.append(mine[0][0])
-        block = summed(block, early + 1, len(sizes))[0][0]
-        result.append(shifted(block, "mode", mode_devs - s, mode_devs, 1))
-    tensor, response = finish(pair_adv, pair_mode, result, pair_amp, advect_count, scale_factor)
+            mine = summed(mine, early + 1, early + 2, pairwise)
+            mine, block, pair_amp = lax.optimization_barrier((mine, block, pair_amp))
+            result.append(summed(mine, early + 2, len(pairwise), pairwise))
+        span = math.prod(sizes[:last])
+        result.append([shifted(b, "cell", n, sizes[last], span, mode_devs - s) for n, b in enumerate(block)])
+    high, low = prepare(pair_amp)
+    tensor, response = finish(pair_adv, pair_mode, result, high, low, advect_count, scale_factor)
     return (tensor, response)
 
 

time: 81.6 us -> 76 us (0.931)
  waiting for transfers between devices: 33.2 us -> 27.9 us
    ppermute x13 -> x12, waiting for transfers between devices: 33.2 us -> 27.9 us  [shifted(): return lax.ppermute(block, (axis, 'mode') if turn else axis, route)]
    pallas_call x1, Pallas kernels: 4.62 us -> 2.67 us  [finish(): pl.pallas_call(functools.partial(finish_kernel, advect_count, per_block,...]
    pallas_call x0 -> x1, Pallas kernels: none -> 1.76 us  [prepare(): pl.pallas_call(prepare_kernel, in_specs=[whole(pltpu.HBM)], out_specs=[wh...]
    ppermute x13 -> x12, starting transfers between devices: 19.1 us -> 19.2 us  [shifted(): return lax.ppermute(block, (axis, 'mode') if turn else axis, route)]
    unnamed x12 -> x16, local copies, waits for them, and re-layouts: 2.08 us -> 2.08 us
  transfers between devices with their start and end apart: 15 -> 14, of which waited for: 9 -> 8; matrix products, arithmetic and copies ran while one was open for 0% -> 0% of each run, Pallas kernels for 21% -> 25%
where the time goes in v4:
time: 76 us; the launch traced here: 75.8 us
  waiting for transfers between devices  27.9 us (37%)
  Pallas kernels  23.1 us (30%)
  starting transfers between devices  22 us (29%)
  local copies, waits for them, and re-layouts  2.08 us (3%)
  between operations  0.81 us (1%)
    ppermute x12, waiting for transfers between devices, shifted(): return lax.ppermute(block, (axis, 'mode') if turn else axis, route)  27.9 us
    ppermute x12, starting transfers between devices, shifted(): return lax.ppermute(block, (axis, 'mode') if turn else axis, route)  19.2 us
    pallas_call x2, Pallas kernels, contract(): pl.pallas_call(functools.partial(contract_kernel, sizes, wide, len(right)...  7.8 us
    pallas_call x2, Pallas kernels, advected(): pl.pallas_call(functools.partial(advected_kernel, comps, planes, rows_y,...  6.81 us
    pallas_call x1, Pallas kernels, finish(): pl.pallas_call(functools.partial(finish_kernel, advect_count, per_block,...  2.67 us
    pallas_call x2, Pallas kernels, lead(): pl.pallas_call(functools.partial(lead_kernel, planes, rows_y, first, coun...  2.15 us
    unnamed x16, local copies, waits for them, and re-layouts  2.08 us
    pallas_call x1, Pallas kernels, prepare(): pl.pallas_call(prepare_kernel, in_specs=[whole(pltpu.HBM)], out_specs=[wh...  1.76 us
  transfers between devices with their start and end apart: 14, of which 8 were waited for; matrix products, arithmetic and copies ran while one was open for 0% of the time, Pallas kernels for 25%

profile of v4, /device:TPU:0, one launch (start us, length us, event | category | flops | bytes accessed | tf_op | source)
XLA Modules:
  0.0 75.8 jit_solution(114361452419713272)
XLA Ops:
  0.6 0.0 copy-start
  0.6 1.4 %copy-done = bf16[3,256,4,2,128]{4,3,2,1,0:T(2,128)(2,1)S(1)} copy-done((bf16[3,256,4,2,128]{4,3,2,1,0:T(2,128)(2,1)S(1)}, bf16[3,256,4,2,128]{4,3,2,1,0:T(2,128)(2,1)}, u32[]{:S(2)}) %copy-start) | copy-done | bytes 1572888
  2.0 0.0 copy-start.4
  2.0 0.7 copy-done.4
  2.7 1.2 %lead.2 = (bf16[144,3072]{1,0:T(8,128)(2,1)S(1)}, bf16[3,256,8,128]{3,2,1,0:T(8,128)(2,1)S(1)}) custom-call(s32[8]{0:T(128)S(1)} %copy-done.4, bf16[3,256,8,128]{3,2,1,0:T(8,128)(2,1)S(1)} %bitcast.12), custom_call_target="tpu_custom_call" | custom-call | flops 1 | bytes 1 | tf_op jit(solution)/shard_map/lead/pallas_call | solution.py:70
  3.9 3.0 %collective-permute-start.1 = (bf16[144,3072]{1,0:T(8,128)(2,1)S(1)}, bf16[144,3072]{1,0:T(8,128)(2,1)S(1)}, u32[]{:S(2)}, u32[]{:S(2)}) collective-permute-start(bf16[144,3072]{1,0:T(8,128)(2,1)S(1)} %get-tuple-element.38.after_ref.refs_0_.ahead_ref), channel_id=1, source_target_pairs={{0,1},{1,0},{2,3},{3,2},{4,5},{5,4},{6,7},{7,6},{8,9},{9,8},{10,11... | collective-permute-start | bytes 2654216 | tf_op jit(solution)/shard_map/ppermute | solution.py:263
  6.9 0.0 copy-start.3
  6.9 0.0 copy-start.5
  7.0 0.5 edge.2.after_ref.over_ref.here_ref
  7.5 1.5 %collective-permute-start = (bf16[256,1536]{1,0:T(8,128)(2,1)S(1)}, bf16[256,1536]{1,0:T(8,128)(2,1)S(1)}, u32[]{:S(2)}, u32[]{:S(2)}) collective-permute-start(bf16[256,1536]{1,0:T(8,128)(2,1)S(1)} %edge.2.after_ref.over_ref.here_ref), channel_id=1, source_target_pairs={{0,2},{2,4},{4,6},{6,8},{8,10},{10,12},{12,14},{14,16},{16,18},{18... | collective-permute-start | bytes 2359304 | tf_op jit(solution)/shard_map/ppermute | solution.py:410
  9.0 0.5 edge.3.refs_2_.here_ref.under_ref
  9.5 1.3 %collective-permute-start.2 = (bf16[256,1536]{1,0:T(8,128)(2,1)S(1)}, bf16[256,1536]{1,0:T(8,128)(2,1)S(1)}, u32[]{:S(2)}, u32[]{:S(2)}) collective-permute-start(bf16[256,1536]{1,0:T(8,128)(2,1)S(1)} %edge.3.refs_2_.here_ref.under_ref), channel_id=1, source_target_pairs={{2,0},{4,2},{6,4},{8,6},{10,8},{12,10},{14,12},{16,14},{18,16},{20... | collective-permute-start | bytes 2359304 | tf_op jit(solution)/shard_map/ppermute | solution.py:411
  10.8 0.9 %lead.3.after_ref.rest_ref = bf16[128,3072]{1,0:T(8,128)(2,1)S(1)} custom-call(s32[8]{0:T(128)S(1)} %copy-done.4, bf16[3,256,8,128]{3,2,1,0:T(8,128)(2,1)S(1)} %get-tuple-element.39.pods_ref.refs_1_, bf16[256,1536]{1,0:T(8,128)(2,1)S(1)} %edge.3.refs_2_.here_ref.under_ref), custom_call_target="tpu_custom_call" | custom-call | flops 1 | bytes 1 | tf_op jit(solution)/shard_map/lead/pallas_call | solution.py:70
  11.7 0.4 collective-permute-start.4
  12.1 0.0 copy-done.3
  12.1 0.0 copy-done.5
  12.1 0.5 weights.1.weight_ref
  12.7 0.0 collective-permute-done.under_ref
  12.7 14.7 %collective-permute-done.1.refs_1_.ahead_ref = bf16[144,3072]{1,0:T(8,128)(2,1)S(1)} collective-permute-done((bf16[144,3072]{1,0:T(8,128)(2,1)S(1)}, bf16[144,3072]{1,0:T(8,128)(2,1)S(1)}, u32[]{:S(2)}, u32[]{:S(2)}) %collective-permute-start.1) | collective-permute-done | bytes 884768 | tf_op jit(solution)/shard_map/ppermute | solution.py:263
  27.4 3.4 %advected.2 = bf16[8,256,1536]{2,1,0:T(8,128)(2,1)S(1)} custom-call(f32[8,128]{1,0:T(8,128)S(1)} %weights.1.weight_ref, bf16[256,1536]{1,0:T(8,128)(2,1)S(1)} %edge.3.refs_2_.here_ref.under_ref, bf16[256,1536]{1,0:T(8,128)(2,1)S(1)} %collective-permute-done.under_ref, bf16[256,1536]{1,0:T(8,128)(2,1)S(1)} %edge.2.after_ref.over_ref.here_ref, ...), custom_call_target="tpu_custom_call" | custom-call | flops 1 | bytes 1 | tf_op jit(solution)/shard_map/advected/pallas_call | solution.py:178
  30.8 0.0 collective-permute-done.2.over_ref
  30.8 3.4 %advected.3 = bf16[8,256,1536]{2,1,0:T(8,128)(2,1)S(1)} custom-call(f32[8,128]{1,0:T(8,128)S(1)} %weights.1.weight_ref, bf16[256,1536]{1,0:T(8,128)(2,1)S(1)} %edge.2.after_ref.over_ref.here_ref, bf16[256,1536]{1,0:T(8,128)(2,1)S(1)} %edge.3.refs_2_.here_ref.under_ref, bf16[256,1536]{1,0:T(8,128)(2,1)S(1)} %collective-permute-done.2.over_ref, ...), custom_call_target="tpu_custom_call" | custom-call | flops 1 | bytes 1 | tf_op jit(solution)/shard_map/advected/pallas_call | solution.py:178
  34.2 3.9 %contract.2 = (f32[8,16,2048]{2,1,0:T(8,128)S(1)}, bf16[8,16,2048]{2,1,0:T(8,128)(2,1)S(1)}) custom-call(bf16[144,3072]{1,0:T(8,128)(2,1)S(1)} %get-tuple-element.38.after_ref.refs_0_.ahead_ref, bf16[128,3072]{1,0:T(8,128)(2,1)S(1)} %lead.3.after_ref.rest_ref, bf16[2048,1536]{1,0:T(8,128)(2,1)S(1)} %bitcast.6, bf16[2048,1536]{1,0:T(8,128)(2,1)S(1)} %bitcast.8), custom_call_target="tpu_custom_call" | custom-call | flops 1 | bytes 1 | tf_op jit(solution)/shard_map/contract/pallas_call | solution.py:218
  38.2 1.0 %collective-permute-start.3 = (bf16[8,16,2048]{2,1,0:T(8,128)(2,1)S(1)}, bf16[8,16,2048]{2,1,0:T(8,128)(2,1)S(1)}, u32[]{:S(2)}, u32[]{:S(2)}) collective-permute-start(bf16[8,16,2048]{2,1,0:T(8,128)(2,1)S(1)} %get-tuple-element.43), channel_id=1, source_target_pairs={{0,2},{2,0},{4,6},{6,4},{8,10},{10,8},{12,14},{14,12},{16,18},{18,... | collective-permute-start | bytes 1572872 | tf_op jit(solution)/shard_map/ppermute | solution.py:263
  39.2 1.5 %collective-permute-done.3.refs_1_ = bf16[8,16,2048]{2,1,0:T(8,128)(2,1)S(1)} collective-permute-done((bf16[8,16,2048]{2,1,0:T(8,128)(2,1)S(1)}, bf16[8,16,2048]{2,1,0:T(8,128)(2,1)S(1)}, u32[]{:S(2)}, u32[]{:S(2)}) %collective-permute-start.3) | collective-permute-done | bytes 524320 | tf_op jit(solution)/shard_map/ppermute | solution.py:263
  40.7 0.1 fold.6
  40.8 3.1 %collective-permute-start.5 = (bf16[4,16,2048]{2,1,0:T(8,128)(2,1)S(1)}, bf16[4,16,2048]{2,1,0:T(8,128)(2,1)S(1)}, u32[]{:S(2)}, u32[]{:S(2)}) collective-permute-start(bf16[4,16,2048]{2,1,0:T(8,128)(2,1)S(1)} %get-tuple-element.46), channel_id=1, source_target_pairs={{0,4},{2,6},{4,0},{6,2},{8,12},{10,14},{12,8},{14,10},{16,20},{18,... | collective-permute-start | bytes 786440 | tf_op jit(solution)/shard_map/ppermute | solution.py:263
  43.8 0.0 collective-permute-done.4.rest_ref
  43.8 0.0 slice-start
  43.9 0.0 slice-start.1
  43.9 3.9 %contract.3 = (f32[8,16,2048]{2,1,0:T(8,128)S(1)}, bf16[8,16,2048]{2,1,0:T(8,128)(2,1)S(1)}) custom-call(bf16[144,3072]{1,0:T(8,128)(2,1)S(1)} %collective-permute-done.1.refs_1_.ahead_ref, bf16[128,3072]{1,0:T(8,128)(2,1)S(1)} %collective-permute-done.4.rest_ref, bf16[2048,1536]{1,0:T(8,128)(2,1)S(1)} %bitcast.7, bf16[2048,1536]{1,0:T(8,128)(2,1)S(1)} %bitcast.9), custom_call_target="tpu_custom_call" | custom-call | flops 1 | bytes 1 | tf_op jit(solution)/shard_map/contract/pallas_call | solution.py:218
  47.7 2.7 %collective-permute-done.5.refs_1_ = bf16[4,16,2048]{2,1,0:T(8,128)(2,1)S(1)} collective-permute-done((bf16[4,16,2048]{2,1,0:T(8,128)(2,1)S(1)}, bf16[4,16,2048]{2,1,0:T(8,128)(2,1)S(1)}, u32[]{:S(2)}, u32[]{:S(2)}) %collective-permute-start.5) | collective-permute-done | bytes 262176 | tf_op jit(solution)/shard_map/ppermute | solution.py:263
  50.5 0.1 collective-permute-start.7
  50.6 1.9 %collective-permute-done.7.refs_1_ = bf16[8,16,2048]{2,1,0:T(8,128)(2,1)S(1)} collective-permute-done((bf16[8,16,2048]{2,1,0:T(8,128)(2,1)S(1)}, bf16[8,16,2048]{2,1,0:T(8,128)(2,1)S(1)}, u32[]{:S(2)}, u32[]{:S(2)}) %collective-permute-start.7) | collective-permute-done | bytes 524320 | tf_op jit(solution)/shard_map/ppermute | solution.py:263
  52.5 0.1 fold.9
  52.6 1.8 %collective-permute-start.8 = (bf16[4,16,2048]{2,1,0:T(8,128)(2,1)S(1)}, bf16[4,16,2048]{2,1,0:T(8,128)(2,1)S(1)}, u32[]{:S(2)}, u32[]{:S(2)}) collective-permute-start(bf16[4,16,2048]{2,1,0:T(8,128)(2,1)S(1)} %get-tuple-element.60), channel_id=1, source_target_pairs={{0,4},{2,6},{4,0},{6,2},{8,12},{10,14},{12,8},{14,10},{16,20},{18,... | collective-permute-start | bytes 786440 | tf_op jit(solution)/shard_map/ppermute | solution.py:263
  54.4 1.6 %collective-permute-start.6 = (bf16[2,16,2048]{2,1,0:T(8,128)(2,1)S(1)}, bf16[2,16,2048]{2,1,0:T(8,128)(2,1)S(1)}, u32[]{:S(2)}, u32[]{:S(2)}) collective-permute-start(bf16[2,16,2048]{2,1,0:T(8,128)(2,1)S(1)} %get-tuple-element.54), channel_id=1, source_target_pairs={{0,8},{2,10},{4,12},{6,14},{8,0},{10,2},{12,4},{14,6},{16,24},{18,... | collective-permute-start | bytes 393224 | tf_op jit(solution)/shard_map/ppermute | solution.py:263
  55.9 3.7 %collective-permute-done.6.refs_1_ = bf16[2,16,2048]{2,1,0:T(8,128)(2,1)S(1)} collective-permute-done((bf16[2,16,2048]{2,1,0:T(8,128)(2,1)S(1)}, bf16[2,16,2048]{2,1,0:T(8,128)(2,1)S(1)}, u32[]{:S(2)}, u32[]{:S(2)}) %collective-permute-start.6) | collective-permute-done | bytes 131104 | tf_op jit(solution)/shard_map/ppermute | solution.py:263
  59.7 1.3 %collective-permute-done.8.refs_1_ = bf16[4,16,2048]{2,1,0:T(8,128)(2,1)S(1)} collective-permute-done((bf16[4,16,2048]{2,1,0:T(8,128)(2,1)S(1)}, bf16[4,16,2048]{2,1,0:T(8,128)(2,1)S(1)}, u32[]{:S(2)}, u32[]{:S(2)}) %collective-permute-start.8) | collective-permute-done | bytes 262176 | tf_op jit(solution)/shard_map/ppermute | solution.py:263
  61.0 0.0 copy-start.1
  61.0 0.0 copy-start.2
  61.1 2.7 %collective-permute-start.9 = (bf16[1,16,2048]{2,1,0:T(8,128)(2,1)S(1)}, bf16[1,16,2048]{2,1,0:T(8,128)(2,1)S(1)}, u32[]{:S(2)}, u32[]{:S(2)}) collective-permute-start(bf16[1,16,2048]{2,1,0:T(8,128)(2,1)S(1)} %get-tuple-element.66), channel_id=1, source_target_pairs={{0,16},{2,18},{4,20},{6,22},{8,24},{10,26},{12,28},{14,30},{16,0},... | collective-permute-start | bytes 196616 | tf_op jit(solution)/shard_map/ppermute | solution.py:263
  63.7 0.3 collective-permute-start.10
  64.0 1.5 %collective-permute-start.11 = (bf16[1,16,2048]{2,1,0:T(8,128)(2,1)S(1)}, bf16[1,16,2048]{2,1,0:T(8,128)(2,1)S(1)}, u32[]{:S(2)}, u32[]{:S(2)}) collective-permute-start(bf16[1,16,2048]{2,1,0:T(8,128)(2,1)S(1)} %get-tuple-element.68), channel_id=1, source_target_pairs={{0,9},{1,8},{2,11},{3,10},{4,13},{5,12},{6,15},{7,14},{8,17},{9,16... | collective-permute-start | bytes 196616 | tf_op jit(solution)/shard_map/ppermute | solution.py:263
  65.5 1.3 %collective-permute-start.12 = (bf16[1,16,2048]{2,1,0:T(8,128)(2,1)S(1)}, bf16[1,16,2048]{2,1,0:T(8,128)(2,1)S(1)}, u32[]{:S(2)}, u32[]{:S(2)}) collective-permute-start(bf16[1,16,2048]{2,1,0:T(8,128)(2,1)S(1)} %get-tuple-element.69), channel_id=1, source_target_pairs={{0,17},{1,16},{2,19},{3,18},{4,21},{5,20},{6,23},{7,22},{8,25},{9,... | collective-permute-start | bytes 196616 | tf_op jit(solution)/shard_map/ppermute | solution.py:263
  66.8 2.5 %collective-permute-start.13 = (bf16[1,16,2048]{2,1,0:T(8,128)(2,1)S(1)}, bf16[1,16,2048]{2,1,0:T(8,128)(2,1)S(1)}, u32[]{:S(2)}, u32[]{:S(2)}) collective-permute-start(bf16[1,16,2048]{2,1,0:T(8,128)(2,1)S(1)} %get-tuple-element.70), channel_id=1, source_target_pairs={{0,25},{1,24},{2,27},{3,26},{4,29},{5,28},{6,31},{7,30},{8,1},{9,0... | collective-permute-start | bytes 196616 | tf_op jit(solution)/shard_map/ppermute | solution.py:263
  69.3 0.0 slice-done
  69.3 0.0 slice-done.1
  69.3 1.8 %prepare.1 = (bf16[2048,1024]{1,0:T(8,128)(2,1)S(1)}, bf16[2048,1024]{1,0:T(8,128)(2,1)S(1)}) custom-call(f32[2048,1024]{1,0:T(8,128)S(1)} %bitcast.11), custom_call_target="tpu_custom_call" | custom-call | flops 8388608 | bytes 16777216 | tf_op jit(solution)/shard_map/prepare/pallas_call | solution.py:298
  71.1 0.0 collective-permute-done.9.refs_1_
  71.1 0.0 collective-permute-done.10.refs_1_
  71.1 0.2 collective-permute-done.11.refs_2_
  71.4 1.8 %collective-permute-done.12.refs_3_ = bf16[1,16,2048]{2,1,0:T(8,128)(2,1)S(1)} collective-permute-done((bf16[1,16,2048]{2,1,0:T(8,128)(2,1)S(1)}, bf16[1,16,2048]{2,1,0:T(8,128)(2,1)S(1)}, u32[]{:S(2)}, u32[]{:S(2)}) %collective-permute-start.12) | collective-permute-done | bytes 65568 | tf_op jit(solution)/shard_map/ppermute | solution.py:263
  73.1 0.0 collective-permute-done.13.refs_4_
  73.1 0.0 copy-done.1
  73.2 0.0 copy-done.2
  73.2 2.7 %finish.1 = (f32[16,8,512]{2,1,0:T(8,128)}, f32[16,1024]{1,0:T(8,128)}) custom-call(s32[1,2048]{1,0:T(1,128)S(1)} %bitcast.13, s32[1,2048]{1,0:T(1,128)S(1)} %bitcast.14, f32[1,16,2048]{2,1,0:T(8,128)S(1)} %fold.11.refs_0_, bf16[1,16,2048]{2,1,0:T(8,128)(2,1)S(1)} %collective-permute-done.10.refs_1_, ...), custom_call_target="tpu_custom_call" | custom-call | flops 1 | bytes 1 | tf_op jit(solution)/shard_map/finish/pallas_call | solution.py:374
  (5 shorter events, 0.1 us)
Async XLA Ops:
  0.6 1.4 %copy-start = (bf16[3,256,4,2,128]{4,3,2,1,0:T(2,128)(2,1)S(1)}, bf16[3,256,4,2,128]{4,3,2,1,0:T(2,128)(2,1)}, u32[]{:S(2)}) copy-start(bf16[3,256,4,2,128]{4,3,2,1,0:T(2,128)(2,1)} %param.7) | copy-start | bytes 4718596
  2.0 0.7 copy-start.4
  3.9 23.5 %collective-permute-start.1 = (bf16[144,3072]{1,0:T(8,128)(2,1)S(1)}, bf16[144,3072]{1,0:T(8,128)(2,1)S(1)}, u32[]{:S(2)}, u32[]{:S(2)}) collective-permute-start(bf16[144,3072]{1,0:T(8,128)(2,1)S(1)} %get-tuple-element.38.after_ref.refs_0_.ahead_ref), channel_id=1, source_target_pairs={{0,1},{1,0},{2,3},{3,2},{4,5},{5,4},{6,7},{7,6},{8,9},{9,8},{10,11... | collective-permute-start | bytes 2654216 | tf_op jit(solution)/shard_map/ppermute | solution.py:263
  6.9 5.2 %copy-start.3 = (s32[4,2,128]{2,1,0:T(2,128)S(1)}, s32[4,2,128]{2,1,0:T(2,128)}, u32[]{:S(2)}) copy-start(s32[4,2,128]{2,1,0:T(2,128)} %param.8) | copy-start | bytes 12292
  6.9 5.2 %copy-start.5 = (f32[8]{0:T(128)S(1)}, f32[8]{0:T(128)}, u32[]{:S(2)}) copy-start(f32[8]{0:T(128)} %volume_ref.1) | copy-start | bytes 100
  7.5 5.2 %collective-permute-start = (bf16[256,1536]{1,0:T(8,128)(2,1)S(1)}, bf16[256,1536]{1,0:T(8,128)(2,1)S(1)}, u32[]{:S(2)}, u32[]{:S(2)}) collective-permute-start(bf16[256,1536]{1,0:T(8,128)(2,1)S(1)} %edge.2.after_ref.over_ref.here_ref), channel_id=1, source_target_pairs={{0,2},{2,4},{4,6},{6,8},{8,10},{10,12},{12,14},{14,16},{16,18},{18... | collective-permute-start | bytes 2359304 | tf_op jit(solution)/shard_map/ppermute | solution.py:410
  9.5 21.3 %collective-permute-start.2 = (bf16[256,1536]{1,0:T(8,128)(2,1)S(1)}, bf16[256,1536]{1,0:T(8,128)(2,1)S(1)}, u32[]{:S(2)}, u32[]{:S(2)}) collective-permute-start(bf16[256,1536]{1,0:T(8,128)(2,1)S(1)} %edge.3.refs_2_.here_ref.under_ref), channel_id=1, source_target_pairs={{2,0},{4,2},{6,4},{8,6},{10,8},{12,10},{14,12},{16,14},{18,16},{20... | collective-permute-start | bytes 2359304 | tf_op jit(solution)/shard_map/ppermute | solution.py:411
  11.7 32.1 %collective-permute-start.4 = (bf16[128,3072]{1,0:T(8,128)(2,1)S(1)}, bf16[128,3072]{1,0:T(8,128)(2,1)S(1)}, u32[]{:S(2)}, u32[]{:S(2)}) collective-permute-start(bf16[128,3072]{1,0:T(8,128)(2,1)S(1)} %lead.3.after_ref.rest_ref), channel_id=1, source_target_pairs={{0,1},{1,0},{2,3},{3,2},{4,5},{5,4},{6,7},{7,6},{8,9},{9,8},{10,11... | collective-permute-start | bytes 2359304 | tf_op jit(solution)/shard_map/ppermute | solution.py:263
  38.2 2.5 %collective-permute-start.3 = (bf16[8,16,2048]{2,1,0:T(8,128)(2,1)S(1)}, bf16[8,16,2048]{2,1,0:T(8,128)(2,1)S(1)}, u32[]{:S(2)}, u32[]{:S(2)}) collective-permute-start(bf16[8,16,2048]{2,1,0:T(8,128)(2,1)S(1)} %get-tuple-element.43), channel_id=1, source_target_pairs={{0,2},{2,0},{4,6},{6,4},{8,10},{10,8},{12,14},{14,12},{16,18},{18,... | collective-permute-start | bytes 1572872 | tf_op jit(solution)/shard_map/ppermute | solution.py:263
  40.8 9.7 %collective-permute-start.5 = (bf16[4,16,2048]{2,1,0:T(8,128)(2,1)S(1)}, bf16[4,16,2048]{2,1,0:T(8,128)(2,1)S(1)}, u32[]{:S(2)}, u32[]{:S(2)}) collective-permute-start(bf16[4,16,2048]{2,1,0:T(8,128)(2,1)S(1)} %get-tuple-element.46), channel_id=1, source_target_pairs={{0,4},{2,6},{4,0},{6,2},{8,12},{10,14},{12,8},{14,10},{16,20},{18,... | collective-permute-start | bytes 786440 | tf_op jit(solution)/shard_map/ppermute | solution.py:263
  43.8 25.5 %slice-start = ((s8[8388608]{0:T(1024)(128)(4,1)}), s8[4194304]{0:T(1024)(128)(4,1)S(1)}, s32[]{:S(2)}) async-start(s8[8388608]{0:T(1024)(128)(4,1)} %bitcast.10), calls=%async_computation | async-start | bytes 8388608
  43.9 25.5 %slice-start.1 = ((s8[8388608]{0:T(1024)(128)(4,1)}), s8[4194304]{0:T(1024)(128)(4,1)S(1)}, s32[]{:S(2)}) async-start(s8[8388608]{0:T(1024)(128)(4,1)} %bitcast.10), calls=%async_computation.1 | async-start | bytes 8388608
  50.5 2.0 %collective-permute-start.7 = (bf16[8,16,2048]{2,1,0:T(8,128)(2,1)S(1)}, bf16[8,16,2048]{2,1,0:T(8,128)(2,1)S(1)}, u32[]{:S(2)}, u32[]{:S(2)}) collective-permute-start(bf16[8,16,2048]{2,1,0:T(8,128)(2,1)S(1)} %get-tuple-element.58), channel_id=1, source_target_pairs={{0,2},{2,0},{4,6},{6,4},{8,10},{10,8},{12,14},{14,12},{16,18},{18,... | collective-permute-start | bytes 1572872 | tf_op jit(solution)/shard_map/ppermute | solution.py:263
  52.6 8.4 %collective-permute-start.8 = (bf16[4,16,2048]{2,1,0:T(8,128)(2,1)S(1)}, bf16[4,16,2048]{2,1,0:T(8,128)(2,1)S(1)}, u32[]{:S(2)}, u32[]{:S(2)}) collective-permute-start(bf16[4,16,2048]{2,1,0:T(8,128)(2,1)S(1)} %get-tuple-element.60), channel_id=1, source_target_pairs={{0,4},{2,6},{4,0},{6,2},{8,12},{10,14},{12,8},{14,10},{16,20},{18,... | collective-permute-start | bytes 786440 | tf_op jit(solution)/shard_map/ppermute | solution.py:263
  54.4 5.3 %collective-permute-start.6 = (bf16[2,16,2048]{2,1,0:T(8,128)(2,1)S(1)}, bf16[2,16,2048]{2,1,0:T(8,128)(2,1)S(1)}, u32[]{:S(2)}, u32[]{:S(2)}) collective-permute-start(bf16[2,16,2048]{2,1,0:T(8,128)(2,1)S(1)} %get-tuple-element.54), channel_id=1, source_target_pairs={{0,8},{2,10},{4,12},{6,14},{8,0},{10,2},{12,4},{14,6},{16,24},{18,... | collective-permute-start | bytes 393224 | tf_op jit(solution)/shard_map/ppermute | solution.py:263
  61.0 12.1 %copy-start.1 = (s32[2048]{0:T(1024)S(1)}, s32[2048]{0:T(1024)}, u32[]{:S(2)}) copy-start(s32[2048]{0:T(1024)} %param.11) | copy-start | bytes 24580
  61.0 12.1 %copy-start.2 = (s32[2048]{0:T(1024)S(1)}, s32[2048]{0:T(1024)}, u32[]{:S(2)}) copy-start(s32[2048]{0:T(1024)} %param.12) | copy-start | bytes 24580
  61.1 10.1 %collective-permute-start.9 = (bf16[1,16,2048]{2,1,0:T(8,128)(2,1)S(1)}, bf16[1,16,2048]{2,1,0:T(8,128)(2,1)S(1)}, u32[]{:S(2)}, u32[]{:S(2)}) collective-permute-start(bf16[1,16,2048]{2,1,0:T(8,128)(2,1)S(1)} %get-tuple-element.66), channel_id=1, source_target_pairs={{0,16},{2,18},{4,20},{6,22},{8,24},{10,26},{12,28},{14,30},{16,0},... | collective-permute-start | bytes 196616 | tf_op jit(solution)/shard_map/ppermute | solution.py:263
  63.7 7.4 %collective-permute-start.10 = (bf16[1,16,2048]{2,1,0:T(8,128)(2,1)S(1)}, bf16[1,16,2048]{2,1,0:T(8,128)(2,1)S(1)}, u32[]{:S(2)}, u32[]{:S(2)}) collective-permute-start(bf16[1,16,2048]{2,1,0:T(8,128)(2,1)S(1)} %get-tuple-element.67), channel_id=1, source_target_pairs={{0,1},{1,0},{2,3},{3,2},{4,5},{5,4},{6,7},{7,6},{8,9},{9,8},{10,11... | collective-permute-start | bytes 196616 | tf_op jit(solution)/shard_map/ppermute | solution.py:263
  64.0 7.4 %collective-permute-start.11 = (bf16[1,16,2048]{2,1,0:T(8,128)(2,1)S(1)}, bf16[1,16,2048]{2,1,0:T(8,128)(2,1)S(1)}, u32[]{:S(2)}, u32[]{:S(2)}) collective-permute-start(bf16[1,16,2048]{2,1,0:T(8,128)(2,1)S(1)} %get-tuple-element.68), channel_id=1, source_target_pairs={{0,9},{1,8},{2,11},{3,10},{4,13},{5,12},{6,15},{7,14},{8,17},{9,16... | collective-permute-start | bytes 196616 | tf_op jit(solution)/shard_map/ppermute | solution.py:263
  65.5 7.6 %collective-permute-start.12 = (bf16[1,16,2048]{2,1,0:T(8,128)(2,1)S(1)}, bf16[1,16,2048]{2,1,0:T(8,128)(2,1)S(1)}, u32[]{:S(2)}, u32[]{:S(2)}) collective-permute-start(bf16[1,16,2048]{2,1,0:T(8,128)(2,1)S(1)} %get-tuple-element.69), channel_id=1, source_target_pairs={{0,17},{1,16},{2,19},{3,18},{4,21},{5,20},{6,23},{7,22},{8,25},{9,... | collective-permute-start | bytes 196616 | tf_op jit(solution)/shard_map/ppermute | solution.py:263
  66.8 6.4 %collective-permute-start.13 = (bf16[1,16,2048]{2,1,0:T(8,128)(2,1)S(1)}, bf16[1,16,2048]{2,1,0:T(8,128)(2,1)S(1)}, u32[]{:S(2)}, u32[]{:S(2)}) collective-permute-start(bf16[1,16,2048]{2,1,0:T(8,128)(2,1)S(1)} %get-tuple-element.70), channel_id=1, source_target_pairs={{0,25},{1,24},{2,27},{3,26},{4,29},{5,28},{6,31},{7,30},{8,1},{9,0... | collective-permute-start | bytes 196616 | tf_op jit(solution)/shard_map/ppermute | solution.py:263

commit v5 on v4

--- a/solution.py
+++ b/solution.py
@@ -142,8 +142,8 @@
             for k in range(min(2, advect_count - 2 * pair)):
                 weighted[d, 2 * pair + k] = 0.5 * (both[k * cells : (k + 1) * cells] * weight)
 
-    def rounded(x):
-        return x.astype(BF16).astype(F32)
+    def difference(x, y):
+        return (x - y).astype(F32)
 
     @pl.loop(0, modes // tall)
     def _(b):
@@ -151,15 +151,15 @@
 
         def at(ref, k, p):
             lane = (k * planes + p) * LANES
-            return ref[here, lane : lane + LANES].astype(F32)
+            return ref[here, lane : lane + LANES]
 
         for k in range(comps):
             line = [at(here_ref, k, p) for p in range(planes)]
             for p in range(planes):
                 grads = (
-                    rounded(line[(p + 1) % planes] - line[(p - 1) % planes]),
-                    rounded(at(over_ref, k, p) - at(under_ref, k, p)),
-                    rounded(pltpu.roll(line[p], LANES - 1, 1) - pltpu.roll(line[p], 1, 1)),
+                    difference(line[(p + 1) % planes], line[(p - 1) % planes]),
+                    difference(at(over_ref, k, p), at(under_ref, k, p)),
+                    difference(pltpu.roll(line[p], LANES - 1, 1), pltpu.roll(line[p], 1, 1)),
                 )
                 cell = p * rows_y + r
                 lane = (k * planes + p) * LANES
@@ -437,8 +437,10 @@
         block = stage(summed(block, 0, last - 1, sizes), last - 1, sizes, True)
         if s == 1:
             mine = summed(mine, early + 1, early + 2, pairwise)
-            mine, block, pair_amp = lax.optimization_barrier((mine, block, pair_amp))
-            result.append(summed(mine, early + 2, len(pairwise), pairwise))
+            mine = summed(mine, early + 2, len(pairwise), pairwise)
+            block, pair_amp = lax.optimization_barrier((block, pair_amp))
+            mine, pair_amp = lax.optimization_barrier((mine, pair_amp))
+            result.append(mine)
         span = math.prod(sizes[:last])
         result.append([shifted(b, "cell", n, sizes[last], span, mode_devs - s) for n, b in enumerate(block)])
     high, low = prepare(pair_amp)

time: 76 us -> 74.5 us (0.980)
  waiting for transfers between devices: 27.9 us -> 26.1 us
    ppermute x12, waiting for transfers between devices: 27.9 us -> 26.1 us  [shifted(): return lax.ppermute(block, (axis, 'mode') if turn else axis, route)]
where the time goes in v5:
time: 74.5 us; the launch traced here: 74.3 us
  waiting for transfers between devices  26.1 us (35%)
  starting transfers between devices  22.7 us (30%)
  Pallas kernels  22.6 us (30%)
  local copies, waits for them, and re-layouts  2.08 us (3%)
  between operations  0.83 us (1%)
    ppermute x12, waiting for transfers between devices, shifted(): return lax.ppermute(block, (axis, 'mode') if turn else axis, route)  26.1 us
    ppermute x12, starting transfers between devices, shifted(): return lax.ppermute(block, (axis, 'mode') if turn else axis, route)  19.9 us
    pallas_call x2, Pallas kernels, contract(): pl.pallas_call(functools.partial(contract_kernel, sizes, wide, len(right)...  7.81 us
    pallas_call x2, Pallas kernels, advected(): pl.pallas_call(functools.partial(advected_kernel, comps, planes, rows_y,...  6.33 us
    pallas_call x1, Pallas kernels, finish(): pl.pallas_call(functools.partial(finish_kernel, advect_count, per_block,...  2.66 us
    pallas_call x2, Pallas kernels, lead(): pl.pallas_call(functools.partial(lead_kernel, planes, rows_y, first, coun...  2.16 us
    unnamed x16, local copies, waits for them, and re-layouts  2.08 us
    pallas_call x1, Pallas kernels, prepare(): pl.pallas_call(prepare_kernel, in_specs=[whole(pltpu.HBM)], out_specs=[wh...  1.76 us
  transfers between devices with their start and end apart: 14, of which 8 were waited for; matrix products, arithmetic and copies ran while one was open for 0% of the time, Pallas kernels for 25%

profile of v5, /device:TPU:0, one launch (start us, length us, event | category | flops | bytes accessed | tf_op | source)
XLA Modules:
  0.0 74.3 jit_solution(11748908078433257693)
XLA Ops:
  0.6 0.0 copy-start
  0.6 1.4 %copy-done = bf16[3,256,4,2,128]{4,3,2,1,0:T(2,128)(2,1)S(1)} copy-done((bf16[3,256,4,2,128]{4,3,2,1,0:T(2,128)(2,1)S(1)}, bf16[3,256,4,2,128]{4,3,2,1,0:T(2,128)(2,1)}, u32[]{:S(2)}) %copy-start) | copy-done | bytes 1572888
  2.0 0.0 copy-start.4
  2.0 0.7 copy-done.4
  2.7 1.2 %lead.2 = (bf16[144,3072]{1,0:T(8,128)(2,1)S(1)}, bf16[3,256,8,128]{3,2,1,0:T(8,128)(2,1)S(1)}) custom-call(s32[8]{0:T(128)S(1)} %copy-done.4, bf16[3,256,8,128]{3,2,1,0:T(8,128)(2,1)S(1)} %bitcast.12), custom_call_target="tpu_custom_call" | custom-call | flops 1 | bytes 1 | tf_op jit(solution)/shard_map/lead/pallas_call | solution.py:70
  3.9 3.0 %collective-permute-start.1 = (bf16[144,3072]{1,0:T(8,128)(2,1)S(1)}, bf16[144,3072]{1,0:T(8,128)(2,1)S(1)}, u32[]{:S(2)}, u32[]{:S(2)}) collective-permute-start(bf16[144,3072]{1,0:T(8,128)(2,1)S(1)} %get-tuple-element.38.after_ref.refs_0_.ahead_ref), channel_id=1, source_target_pairs={{0,1},{1,0},{2,3},{3,2},{4,5},{5,4},{6,7},{7,6},{8,9},{9,8},{10,11... | collective-permute-start | bytes 2654216 | tf_op jit(solution)/shard_map/ppermute | solution.py:263
  6.9 0.0 copy-start.3
  6.9 0.0 copy-start.5
  7.0 0.5 edge.2.after_ref.over_ref.here_ref
  7.5 1.5 %collective-permute-start = (bf16[256,1536]{1,0:T(8,128)(2,1)S(1)}, bf16[256,1536]{1,0:T(8,128)(2,1)S(1)}, u32[]{:S(2)}, u32[]{:S(2)}) collective-permute-start(bf16[256,1536]{1,0:T(8,128)(2,1)S(1)} %edge.2.after_ref.over_ref.here_ref), channel_id=1, source_target_pairs={{0,2},{2,4},{4,6},{6,8},{8,10},{10,12},{12,14},{14,16},{16,18},{18... | collective-permute-start | bytes 2359304 | tf_op jit(solution)/shard_map/ppermute | solution.py:410
  9.0 0.5 edge.3.refs_2_.here_ref.under_ref
  9.5 1.3 %collective-permute-start.2 = (bf16[256,1536]{1,0:T(8,128)(2,1)S(1)}, bf16[256,1536]{1,0:T(8,128)(2,1)S(1)}, u32[]{:S(2)}, u32[]{:S(2)}) collective-permute-start(bf16[256,1536]{1,0:T(8,128)(2,1)S(1)} %edge.3.refs_2_.here_ref.under_ref), channel_id=1, source_target_pairs={{2,0},{4,2},{6,4},{8,6},{10,8},{12,10},{14,12},{16,14},{18,16},{20... | collective-permute-start | bytes 2359304 | tf_op jit(solution)/shard_map/ppermute | solution.py:411
  10.8 0.9 %lead.3.after_ref.rest_ref = bf16[128,3072]{1,0:T(8,128)(2,1)S(1)} custom-call(s32[8]{0:T(128)S(1)} %copy-done.4, bf16[3,256,8,128]{3,2,1,0:T(8,128)(2,1)S(1)} %get-tuple-element.39.pods_ref.refs_1_, bf16[256,1536]{1,0:T(8,128)(2,1)S(1)} %edge.3.refs_2_.here_ref.under_ref), custom_call_target="tpu_custom_call" | custom-call | flops 1 | bytes 1 | tf_op jit(solution)/shard_map/lead/pallas_call | solution.py:70
  11.7 0.4 collective-permute-start.4
  12.1 0.0 copy-done.3
  12.1 0.0 copy-done.5
  12.1 0.5 weights.1.weight_ref
  12.7 0.0 collective-permute-done.under_ref
  12.7 14.7 %collective-permute-done.1.refs_1_.ahead_ref = bf16[144,3072]{1,0:T(8,128)(2,1)S(1)} collective-permute-done((bf16[144,3072]{1,0:T(8,128)(2,1)S(1)}, bf16[144,3072]{1,0:T(8,128)(2,1)S(1)}, u32[]{:S(2)}, u32[]{:S(2)}) %collective-permute-start.1) | collective-permute-done | bytes 884768 | tf_op jit(solution)/shard_map/ppermute | solution.py:263
  27.4 3.2 %advected.2 = bf16[8,256,1536]{2,1,0:T(8,128)(2,1)S(1)} custom-call(f32[8,128]{1,0:T(8,128)S(1)} %weights.1.weight_ref, bf16[256,1536]{1,0:T(8,128)(2,1)S(1)} %edge.3.refs_2_.here_ref.under_ref, bf16[256,1536]{1,0:T(8,128)(2,1)S(1)} %collective-permute-done.under_ref, bf16[256,1536]{1,0:T(8,128)(2,1)S(1)} %edge.2.after_ref.over_ref.here_ref, ...), custom_call_target="tpu_custom_call" | custom-call | flops 1 | bytes 1 | tf_op jit(solution)/shard_map/advected/pallas_call | solution.py:178
  30.6 0.0 collective-permute-done.2.over_ref
  30.6 3.2 %advected.3 = bf16[8,256,1536]{2,1,0:T(8,128)(2,1)S(1)} custom-call(f32[8,128]{1,0:T(8,128)S(1)} %weights.1.weight_ref, bf16[256,1536]{1,0:T(8,128)(2,1)S(1)} %edge.2.after_ref.over_ref.here_ref, bf16[256,1536]{1,0:T(8,128)(2,1)S(1)} %edge.3.refs_2_.here_ref.under_ref, bf16[256,1536]{1,0:T(8,128)(2,1)S(1)} %collective-permute-done.2.over_ref, ...), custom_call_target="tpu_custom_call" | custom-call | flops 1 | bytes 1 | tf_op jit(solution)/shard_map/advected/pallas_call | solution.py:178
  33.8 3.9 %contract.2 = (f32[8,16,2048]{2,1,0:T(8,128)S(1)}, bf16[8,16,2048]{2,1,0:T(8,128)(2,1)S(1)}) custom-call(bf16[144,3072]{1,0:T(8,128)(2,1)S(1)} %get-tuple-element.38.after_ref.refs_0_.ahead_ref, bf16[128,3072]{1,0:T(8,128)(2,1)S(1)} %lead.3.after_ref.rest_ref, bf16[2048,1536]{1,0:T(8,128)(2,1)S(1)} %bitcast.6, bf16[2048,1536]{1,0:T(8,128)(2,1)S(1)} %bitcast.8), custom_call_target="tpu_custom_call" | custom-call | flops 1 | bytes 1 | tf_op jit(solution)/shard_map/contract/pallas_call | solution.py:218
  37.7 1.0 %collective-permute-start.3 = (bf16[8,16,2048]{2,1,0:T(8,128)(2,1)S(1)}, bf16[8,16,2048]{2,1,0:T(8,128)(2,1)S(1)}, u32[]{:S(2)}, u32[]{:S(2)}) collective-permute-start(bf16[8,16,2048]{2,1,0:T(8,128)(2,1)S(1)} %get-tuple-element.43), channel_id=1, source_target_pairs={{0,2},{2,0},{4,6},{6,4},{8,10},{10,8},{12,14},{14,12},{16,18},{18,... | collective-permute-start | bytes 1572872 | tf_op jit(solution)/shard_map/ppermute | solution.py:263
  38.7 1.5 %collective-permute-done.3.refs_1_ = bf16[8,16,2048]{2,1,0:T(8,128)(2,1)S(1)} collective-permute-done((bf16[8,16,2048]{2,1,0:T(8,128)(2,1)S(1)}, bf16[8,16,2048]{2,1,0:T(8,128)(2,1)S(1)}, u32[]{:S(2)}, u32[]{:S(2)}) %collective-permute-start.3) | collective-permute-done | bytes 524320 | tf_op jit(solution)/shard_map/ppermute | solution.py:263
  40.2 0.1 fold.6
  40.3 2.8 %collective-permute-start.5 = (bf16[4,16,2048]{2,1,0:T(8,128)(2,1)S(1)}, bf16[4,16,2048]{2,1,0:T(8,128)(2,1)S(1)}, u32[]{:S(2)}, u32[]{:S(2)}) collective-permute-start(bf16[4,16,2048]{2,1,0:T(8,128)(2,1)S(1)} %get-tuple-element.46), channel_id=1, source_target_pairs={{0,4},{2,6},{4,0},{6,2},{8,12},{10,14},{12,8},{14,10},{16,20},{18,... | collective-permute-start | bytes 786440 | tf_op jit(solution)/shard_map/ppermute | solution.py:263
  43.1 0.3 collective-permute-done.4.rest_ref
  43.4 0.0 slice-start
  43.5 0.0 slice-start.1
  43.5 3.9 %contract.3 = (f32[8,16,2048]{2,1,0:T(8,128)S(1)}, bf16[8,16,2048]{2,1,0:T(8,128)(2,1)S(1)}) custom-call(bf16[144,3072]{1,0:T(8,128)(2,1)S(1)} %collective-permute-done.1.refs_1_.ahead_ref, bf16[128,3072]{1,0:T(8,128)(2,1)S(1)} %collective-permute-done.4.rest_ref, bf16[2048,1536]{1,0:T(8,128)(2,1)S(1)} %bitcast.7, bf16[2048,1536]{1,0:T(8,128)(2,1)S(1)} %bitcast.9), custom_call_target="tpu_custom_call" | custom-call | flops 1 | bytes 1 | tf_op jit(solution)/shard_map/contract/pallas_call | solution.py:218
  47.4 2.4 %collective-permute-done.5.refs_1_ = bf16[4,16,2048]{2,1,0:T(8,128)(2,1)S(1)} collective-permute-done((bf16[4,16,2048]{2,1,0:T(8,128)(2,1)S(1)}, bf16[4,16,2048]{2,1,0:T(8,128)(2,1)S(1)}, u32[]{:S(2)}, u32[]{:S(2)}) %collective-permute-start.5) | collective-permute-done | bytes 262176 | tf_op jit(solution)/shard_map/ppermute | solution.py:263
  49.8 0.1 collective-permute-start.8
  49.8 1.9 %collective-permute-done.8.refs_1_ = bf16[8,16,2048]{2,1,0:T(8,128)(2,1)S(1)} collective-permute-done((bf16[8,16,2048]{2,1,0:T(8,128)(2,1)S(1)}, bf16[8,16,2048]{2,1,0:T(8,128)(2,1)S(1)}, u32[]{:S(2)}, u32[]{:S(2)}) %collective-permute-start.8) | collective-permute-done | bytes 524320 | tf_op jit(solution)/shard_map/ppermute | solution.py:263
  51.7 0.1 fold.10
  51.8 1.8 %collective-permute-start.9 = (bf16[4,16,2048]{2,1,0:T(8,128)(2,1)S(1)}, bf16[4,16,2048]{2,1,0:T(8,128)(2,1)S(1)}, u32[]{:S(2)}, u32[]{:S(2)}) collective-permute-start(bf16[4,16,2048]{2,1,0:T(8,128)(2,1)S(1)} %get-tuple-element.60), channel_id=1, source_target_pairs={{0,4},{2,6},{4,0},{6,2},{8,12},{10,14},{12,8},{14,10},{16,20},{18,... | collective-permute-start | bytes 786440 | tf_op jit(solution)/shard_map/ppermute | solution.py:263
  53.6 1.6 %collective-permute-start.6 = (bf16[2,16,2048]{2,1,0:T(8,128)(2,1)S(1)}, bf16[2,16,2048]{2,1,0:T(8,128)(2,1)S(1)}, u32[]{:S(2)}, u32[]{:S(2)}) collective-permute-start(bf16[2,16,2048]{2,1,0:T(8,128)(2,1)S(1)} %get-tuple-element.54), channel_id=1, source_target_pairs={{0,8},{2,10},{4,12},{6,14},{8,0},{10,2},{12,4},{14,6},{16,24},{18,... | collective-permute-start | bytes 393224 | tf_op jit(solution)/shard_map/ppermute | solution.py:263
  55.2 3.7 %collective-permute-done.6.refs_1_ = bf16[2,16,2048]{2,1,0:T(8,128)(2,1)S(1)} collective-permute-done((bf16[2,16,2048]{2,1,0:T(8,128)(2,1)S(1)}, bf16[2,16,2048]{2,1,0:T(8,128)(2,1)S(1)}, u32[]{:S(2)}, u32[]{:S(2)}) %collective-permute-start.6) | collective-permute-done | bytes 131104 | tf_op jit(solution)/shard_map/ppermute | solution.py:263
  58.9 2.6 %collective-permute-start.7 = (bf16[1,16,2048]{2,1,0:T(8,128)(2,1)S(1)}, bf16[1,16,2048]{2,1,0:T(8,128)(2,1)S(1)}, u32[]{:S(2)}, u32[]{:S(2)}) collective-permute-start(bf16[1,16,2048]{2,1,0:T(8,128)(2,1)S(1)} %get-tuple-element.56), channel_id=1, source_target_pairs={{0,16},{2,18},{4,20},{6,22},{8,24},{10,26},{12,28},{14,30},{16,0},... | collective-permute-start | bytes 196616 | tf_op jit(solution)/shard_map/ppermute | solution.py:263
  61.6 0.0 collective-permute-done.9.refs_1_
  61.6 0.6 collective-permute-start.10
  62.2 1.3 %collective-permute-start.11 = (bf16[1,16,2048]{2,1,0:T(8,128)(2,1)S(1)}, bf16[1,16,2048]{2,1,0:T(8,128)(2,1)S(1)}, u32[]{:S(2)}, u32[]{:S(2)}) collective-permute-start(bf16[1,16,2048]{2,1,0:T(8,128)(2,1)S(1)} %get-tuple-element.68), channel_id=1, source_target_pairs={{0,9},{1,8},{2,11},{3,10},{4,13},{5,12},{6,15},{7,14},{8,17},{9,16... | collective-permute-start | bytes 196616 | tf_op jit(solution)/shard_map/ppermute | solution.py:263
  63.5 2.5 %collective-permute-start.12 = (bf16[1,16,2048]{2,1,0:T(8,128)(2,1)S(1)}, bf16[1,16,2048]{2,1,0:T(8,128)(2,1)S(1)}, u32[]{:S(2)}, u32[]{:S(2)}) collective-permute-start(bf16[1,16,2048]{2,1,0:T(8,128)(2,1)S(1)} %get-tuple-element.69), channel_id=1, source_target_pairs={{0,17},{1,16},{2,19},{3,18},{4,21},{5,20},{6,23},{7,22},{8,25},{9,... | collective-permute-start | bytes 196616 | tf_op jit(solution)/shard_map/ppermute | solution.py:263
  66.0 2.3 %collective-permute-start.13 = (bf16[1,16,2048]{2,1,0:T(8,128)(2,1)S(1)}, bf16[1,16,2048]{2,1,0:T(8,128)(2,1)S(1)}, u32[]{:S(2)}, u32[]{:S(2)}) collective-permute-start(bf16[1,16,2048]{2,1,0:T(8,128)(2,1)S(1)} %get-tuple-element.70), channel_id=1, source_target_pairs={{0,25},{1,24},{2,27},{3,26},{4,29},{5,28},{6,31},{7,30},{8,1},{9,0... | collective-permute-start | bytes 196616 | tf_op jit(solution)/shard_map/ppermute | solution.py:263
  68.2 0.0 collective-permute-done.7.refs_1_
  68.2 0.0 slice-done
  68.3 0.0 slice-done.1
  68.3 0.0 copy-start.1
  68.3 0.0 copy-start.2
  68.3 1.8 %prepare.1 = (bf16[2048,1024]{1,0:T(8,128)(2,1)S(1)}, bf16[2048,1024]{1,0:T(8,128)(2,1)S(1)}) custom-call(f32[2048,1024]{1,0:T(8,128)S(1)} %bitcast.11), custom_call_target="tpu_custom_call" | custom-call | flops 8388608 | bytes 16777216 | tf_op jit(solution)/shard_map/prepare/pallas_call | solution.py:298
  70.1 0.0 collective-permute-done.10.refs_1_
  70.1 0.0 collective-permute-done.11.refs_2_
  70.1 1.1 %collective-permute-done.12.refs_3_ = bf16[1,16,2048]{2,1,0:T(8,128)(2,1)S(1)} collective-permute-done((bf16[1,16,2048]{2,1,0:T(8,128)(2,1)S(1)}, bf16[1,16,2048]{2,1,0:T(8,128)(2,1)S(1)}, u32[]{:S(2)}, u32[]{:S(2)}) %collective-permute-start.12) | collective-permute-done | bytes 65568 | tf_op jit(solution)/shard_map/ppermute | solution.py:263
  71.2 0.4 collective-permute-done.13.refs_4_
  71.6 0.0 copy-done.1
  71.6 0.0 copy-done.2
  71.6 2.7 %finish.1 = (f32[16,8,512]{2,1,0:T(8,128)}, f32[16,1024]{1,0:T(8,128)}) custom-call(s32[1,2048]{1,0:T(1,128)S(1)} %bitcast.13, s32[1,2048]{1,0:T(1,128)S(1)} %bitcast.14, f32[1,16,2048]{2,1,0:T(8,128)S(1)} %fold.9.refs_0_, bf16[1,16,2048]{2,1,0:T(8,128)(2,1)S(1)} %collective-permute-done.10.refs_1_, ...), custom_call_target="tpu_custom_call" | custom-call | flops 1 | bytes 1 | tf_op jit(solution)/shard_map/finish/pallas_call | solution.py:374
  (5 shorter events, 0.1 us)
Async XLA Ops:
  0.6 1.4 %copy-start = (bf16[3,256,4,2,128]{4,3,2,1,0:T(2,128)(2,1)S(1)}, bf16[3,256,4,2,128]{4,3,2,1,0:T(2,128)(2,1)}, u32[]{:S(2)}) copy-start(bf16[3,256,4,2,128]{4,3,2,1,0:T(2,128)(2,1)} %param.7) | copy-start | bytes 4718596
  2.0 0.7 copy-start.4
  3.9 23.5 %collective-permute-start.1 = (bf16[144,3072]{1,0:T(8,128)(2,1)S(1)}, bf16[144,3072]{1,0:T(8,128)(2,1)S(1)}, u32[]{:S(2)}, u32[]{:S(2)}) collective-permute-start(bf16[144,3072]{1,0:T(8,128)(2,1)S(1)} %get-tuple-element.38.after_ref.refs_0_.ahead_ref), channel_id=1, source_target_pairs={{0,1},{1,0},{2,3},{3,2},{4,5},{5,4},{6,7},{7,6},{8,9},{9,8},{10,11... | collective-permute-start | bytes 2654216 | tf_op jit(solution)/shard_map/ppermute | solution.py:263
  6.9 5.2 %copy-start.3 = (s32[4,2,128]{2,1,0:T(2,128)S(1)}, s32[4,2,128]{2,1,0:T(2,128)}, u32[]{:S(2)}) copy-start(s32[4,2,128]{2,1,0:T(2,128)} %param.8) | copy-start | bytes 12292
  6.9 5.2 %copy-start.5 = (f32[8]{0:T(128)S(1)}, f32[8]{0:T(128)}, u32[]{:S(2)}) copy-start(f32[8]{0:T(128)} %volume_ref.1) | copy-start | bytes 100
  7.5 5.2 %collective-permute-start = (bf16[256,1536]{1,0:T(8,128)(2,1)S(1)}, bf16[256,1536]{1,0:T(8,128)(2,1)S(1)}, u32[]{:S(2)}, u32[]{:S(2)}) collective-permute-start(bf16[256,1536]{1,0:T(8,128)(2,1)S(1)} %edge.2.after_ref.over_ref.here_ref), channel_id=1, source_target_pairs={{0,2},{2,4},{4,6},{6,8},{8,10},{10,12},{12,14},{14,16},{16,18},{18... | collective-permute-start | bytes 2359304 | tf_op jit(solution)/shard_map/ppermute | solution.py:410
  9.5 21.1 %collective-permute-start.2 = (bf16[256,1536]{1,0:T(8,128)(2,1)S(1)}, bf16[256,1536]{1,0:T(8,128)(2,1)S(1)}, u32[]{:S(2)}, u32[]{:S(2)}) collective-permute-start(bf16[256,1536]{1,0:T(8,128)(2,1)S(1)} %edge.3.refs_2_.here_ref.under_ref), channel_id=1, source_target_pairs={{2,0},{4,2},{6,4},{8,6},{10,8},{12,10},{14,12},{16,14},{18,16},{20... | collective-permute-start | bytes 2359304 | tf_op jit(solution)/shard_map/ppermute | solution.py:411
  11.7 31.7 %collective-permute-start.4 = (bf16[128,3072]{1,0:T(8,128)(2,1)S(1)}, bf16[128,3072]{1,0:T(8,128)(2,1)S(1)}, u32[]{:S(2)}, u32[]{:S(2)}) collective-permute-start(bf16[128,3072]{1,0:T(8,128)(2,1)S(1)} %lead.3.after_ref.rest_ref), channel_id=1, source_target_pairs={{0,1},{1,0},{2,3},{3,2},{4,5},{5,4},{6,7},{7,6},{8,9},{9,8},{10,11... | collective-permute-start | bytes 2359304 | tf_op jit(solution)/shard_map/ppermute | solution.py:263
  37.7 2.5 %collective-permute-start.3 = (bf16[8,16,2048]{2,1,0:T(8,128)(2,1)S(1)}, bf16[8,16,2048]{2,1,0:T(8,128)(2,1)S(1)}, u32[]{:S(2)}, u32[]{:S(2)}) collective-permute-start(bf16[8,16,2048]{2,1,0:T(8,128)(2,1)S(1)} %get-tuple-element.43), channel_id=1, source_target_pairs={{0,2},{2,0},{4,6},{6,4},{8,10},{10,8},{12,14},{14,12},{16,18},{18,... | collective-permute-start | bytes 1572872 | tf_op jit(solution)/shard_map/ppermute | solution.py:263
  40.3 9.4 %collective-permute-start.5 = (bf16[4,16,2048]{2,1,0:T(8,128)(2,1)S(1)}, bf16[4,16,2048]{2,1,0:T(8,128)(2,1)S(1)}, u32[]{:S(2)}, u32[]{:S(2)}) collective-permute-start(bf16[4,16,2048]{2,1,0:T(8,128)(2,1)S(1)} %get-tuple-element.46), channel_id=1, source_target_pairs={{0,4},{2,6},{4,0},{6,2},{8,12},{10,14},{12,8},{14,10},{16,20},{18,... | collective-permute-start | bytes 786440 | tf_op jit(solution)/shard_map/ppermute | solution.py:263
  43.4 24.8 %slice-start = ((s8[8388608]{0:T(1024)(128)(4,1)}), s8[4194304]{0:T(1024)(128)(4,1)S(1)}, s32[]{:S(2)}) async-start(s8[8388608]{0:T(1024)(128)(4,1)} %bitcast.10), calls=%async_computation | async-start | bytes 8388608
  43.5 24.8 %slice-start.1 = ((s8[8388608]{0:T(1024)(128)(4,1)}), s8[4194304]{0:T(1024)(128)(4,1)S(1)}, s32[]{:S(2)}) async-start(s8[8388608]{0:T(1024)(128)(4,1)} %bitcast.10), calls=%async_computation.1 | async-start | bytes 8388608
  49.8 2.0 %collective-permute-start.8 = (bf16[8,16,2048]{2,1,0:T(8,128)(2,1)S(1)}, bf16[8,16,2048]{2,1,0:T(8,128)(2,1)S(1)}, u32[]{:S(2)}, u32[]{:S(2)}) collective-permute-start(bf16[8,16,2048]{2,1,0:T(8,128)(2,1)S(1)} %get-tuple-element.58), channel_id=1, source_target_pairs={{0,2},{2,0},{4,6},{6,4},{8,10},{10,8},{12,14},{14,12},{16,18},{18,... | collective-permute-start | bytes 1572872 | tf_op jit(solution)/shard_map/ppermute | solution.py:263
  51.8 9.7 %collective-permute-start.9 = (bf16[4,16,2048]{2,1,0:T(8,128)(2,1)S(1)}, bf16[4,16,2048]{2,1,0:T(8,128)(2,1)S(1)}, u32[]{:S(2)}, u32[]{:S(2)}) collective-permute-start(bf16[4,16,2048]{2,1,0:T(8,128)(2,1)S(1)} %get-tuple-element.60), channel_id=1, source_target_pairs={{0,4},{2,6},{4,0},{6,2},{8,12},{10,14},{12,8},{14,10},{16,20},{18,... | collective-permute-start | bytes 786440 | tf_op jit(solution)/shard_map/ppermute | solution.py:263
  53.6 5.3 %collective-permute-start.6 = (bf16[2,16,2048]{2,1,0:T(8,128)(2,1)S(1)}, bf16[2,16,2048]{2,1,0:T(8,128)(2,1)S(1)}, u32[]{:S(2)}, u32[]{:S(2)}) collective-permute-start(bf16[2,16,2048]{2,1,0:T(8,128)(2,1)S(1)} %get-tuple-element.54), channel_id=1, source_target_pairs={{0,8},{2,10},{4,12},{6,14},{8,0},{10,2},{12,4},{14,6},{16,24},{18,... | collective-permute-start | bytes 393224 | tf_op jit(solution)/shard_map/ppermute | solution.py:263
  58.9 9.3 %collective-permute-start.7 = (bf16[1,16,2048]{2,1,0:T(8,128)(2,1)S(1)}, bf16[1,16,2048]{2,1,0:T(8,128)(2,1)S(1)}, u32[]{:S(2)}, u32[]{:S(2)}) collective-permute-start(bf16[1,16,2048]{2,1,0:T(8,128)(2,1)S(1)} %get-tuple-element.56), channel_id=1, source_target_pairs={{0,16},{2,18},{4,20},{6,22},{8,24},{10,26},{12,28},{14,30},{16,0},... | collective-permute-start | bytes 196616 | tf_op jit(solution)/shard_map/ppermute | solution.py:263
  61.6 8.5 %collective-permute-start.10 = (bf16[1,16,2048]{2,1,0:T(8,128)(2,1)S(1)}, bf16[1,16,2048]{2,1,0:T(8,128)(2,1)S(1)}, u32[]{:S(2)}, u32[]{:S(2)}) collective-permute-start(bf16[1,16,2048]{2,1,0:T(8,128)(2,1)S(1)} %get-tuple-element.67), channel_id=1, source_target_pairs={{0,1},{1,0},{2,3},{3,2},{4,5},{5,4},{6,7},{7,6},{8,9},{9,8},{10,11... | collective-permute-start | bytes 196616 | tf_op jit(solution)/shard_map/ppermute | solution.py:263
  62.2 7.9 %collective-permute-start.11 = (bf16[1,16,2048]{2,1,0:T(8,128)(2,1)S(1)}, bf16[1,16,2048]{2,1,0:T(8,128)(2,1)S(1)}, u32[]{:S(2)}, u32[]{:S(2)}) collective-permute-start(bf16[1,16,2048]{2,1,0:T(8,128)(2,1)S(1)} %get-tuple-element.68), channel_id=1, source_target_pairs={{0,9},{1,8},{2,11},{3,10},{4,13},{5,12},{6,15},{7,14},{8,17},{9,16... | collective-permute-start | bytes 196616 | tf_op jit(solution)/shard_map/ppermute | solution.py:263
  63.5 7.7 %collective-permute-start.12 = (bf16[1,16,2048]{2,1,0:T(8,128)(2,1)S(1)}, bf16[1,16,2048]{2,1,0:T(8,128)(2,1)S(1)}, u32[]{:S(2)}, u32[]{:S(2)}) collective-permute-start(bf16[1,16,2048]{2,1,0:T(8,128)(2,1)S(1)} %get-tuple-element.69), channel_id=1, source_target_pairs={{0,17},{1,16},{2,19},{3,18},{4,21},{5,20},{6,23},{7,22},{8,25},{9,... | collective-permute-start | bytes 196616 | tf_op jit(solution)/shard_map/ppermute | solution.py:263
  66.0 5.6 %collective-permute-start.13 = (bf16[1,16,2048]{2,1,0:T(8,128)(2,1)S(1)}, bf16[1,16,2048]{2,1,0:T(8,128)(2,1)S(1)}, u32[]{:S(2)}, u32[]{:S(2)}) collective-permute-start(bf16[1,16,2048]{2,1,0:T(8,128)(2,1)S(1)} %get-tuple-element.70), channel_id=1, source_target_pairs={{0,25},{1,24},{2,27},{3,26},{4,29},{5,28},{6,31},{7,30},{8,1},{9,0... | collective-permute-start | bytes 196616 | tf_op jit(solution)/shard_map/ppermute | solution.py:263
  68.3 3.3 %copy-start.1 = (s32[2048]{0:T(1024)S(1)}, s32[2048]{0:T(1024)}, u32[]{:S(2)}) copy-start(s32[2048]{0:T(1024)} %param.11) | copy-start | bytes 24580
  68.3 3.3 %copy-start.2 = (s32[2048]{0:T(1024)S(1)}, s32[2048]{0:T(1024)}, u32[]{:S(2)}) copy-start(s32[2048]{0:T(1024)} %param.12) | copy-start | bytes 24580

commit v6 on v5

--- a/solution.py
+++ b/solution.py
@@ -30,26 +30,20 @@
     return pairs, [(row * 16, lane * LANES) for row, lane in spot]
 
 
-def lead_kernel(planes, rows_y, first, count, advect_count, *refs):
-    index_ref, pods_ref, wide = refs[0], refs[1], refs[-1]
-    ahead = refs[-2].shape == pods_ref.shape
-    out_ref = refs[-3] if ahead else refs[-2]
-    if ahead:
-        refs[-2][...] = pods_ref[...]
+def lead_kernel(planes, rows_y, r, advect_count, index_ref, pods_ref, out_ref, held_ref, wide):
+    held_ref[...] = pods_ref[...]
     comps, modes, cells, _ = pods_ref.shape
     base = lax.axis_index("mode") * modes
-    extra = out_ref.shape[0] - count
+    extra = out_ref.shape[0] - modes
     pairs, places = lead_places(comps, advect_count, out_ref.shape[1])
-    if extra:
-        out_ref[:extra, :] = jnp.zeros((extra, out_ref.shape[1]), BF16)
+    out_ref[:extra, :] = jnp.zeros((extra, out_ref.shape[1]), BF16)
     for c in range(comps):
         wide[...] = pods_ref[c].astype(F32).reshape(modes * cells, LANES)
-        for r in range(rows_y):
-            for p in range(planes):
-                value = wide[pl.ds(first * cells + p * rows_y + r, count, stride=cells), :]
-                at = ((r * comps + c) * planes + p) * LANES
-                out_ref[extra:, at : at + LANES] = value.astype(BF16)
-        for pair in range(pairs if extra else 0):
+        for p in range(planes):
+            value = wide[pl.ds(p * rows_y + r, modes, stride=cells), :]
+            at = (c * planes + p) * LANES
+            out_ref[extra:, at : at + LANES] = value.astype(BF16)
+        for pair in range(pairs):
             blocks = []
             for j in (2 * pair, 2 * pair + 1):
                 local = index_ref[min(j, advect_count - 1)] - base
@@ -60,24 +54,23 @@
             out_ref[row : row + 2 * cells, lane : lane + LANES] = jnp.concatenate(blocks, axis=0).astype(BF16)
 
 
-def lead(flat, advect_index, after, planes, rows_y, first, count, ahead):
+def lead(flat, advect_index, planes, rows_y, r):
     comps, modes, cells, width = flat.shape
-    lanes = comps * cells * width
-    extra = 0
-    if ahead:
-        _, places = lead_places(comps, advect_index.shape[0], lanes)
-        extra = places[-1][0] + 16
-    return pl.pallas_call(
-        functools.partial(lead_kernel, planes, rows_y, first, count, advect_index.shape[0]),
-        in_specs=[whole(pltpu.SMEM), whole()] + [whole(pl.ANY)] * len(after),
-        out_specs=[whole()] * (1 + ahead),
-        out_shape=[jax.ShapeDtypeStruct((extra + count, lanes), BF16)]
-        + [jax.ShapeDtypeStruct(flat.shape, BF16)] * ahead,
+    lanes = comps * planes * width
+    _, places = lead_places(comps, advect_index.shape[0], lanes)
+    return pl.pallas_call(
+        functools.partial(lead_kernel, planes, rows_y, r, advect_index.shape[0]),
+        in_specs=[whole(pltpu.SMEM), whole()],
+        out_specs=[whole()] * 2,
+        out_shape=[
+            jax.ShapeDtypeStruct((places[-1][0] + 16 + modes, lanes), BF16),
+            jax.ShapeDtypeStruct(flat.shape, BF16),
+        ],
         scratch_shapes=[pltpu.VMEM((modes * cells, width), F32)],
         compiler_params=params(8),
         cost_estimate=SHORT,
         name="lead",
-    )(advect_index, flat, *after)
+    )(advect_index, flat)
 
 
 def edge_kernel(planes, rows_y, r, pods_ref, after_ref, out_ref, wide):
@@ -193,49 +186,83 @@
     return [lax.rem(own + s, ways) for s in range(ways)]
 
 
-def contract_kernel(sizes, wide, rows_y, ahead_ref, rest_ref, *refs):
-    right_refs, outs, scratch = refs[:rows_y], refs[rows_y:-1], refs[-1]
+def begin_kernel(wide, left_ref, right_ref, out_ref):
+    extra = left_ref.shape[0] - out_ref.shape[0]
+    left = left_ref[extra:, :]
+    for n in range(right_ref.shape[0] // wide):
+        here = slice(n * wide, (n + 1) * wide)
+        out_ref[:, here] = lax.dot_general(
+            left, right_ref[here, :], (((1,), (1,)), ((), ())), preferred_element_type=F32
+        )
+
+
+def begin(left, right, rows):
+    columns = right.shape[0]
+    return pl.pallas_call(
+        functools.partial(begin_kernel, min(columns, 256)),
+        in_specs=[whole()] * 2,
+        out_specs=whole(),
+        out_shape=jax.ShapeDtypeStruct((rows, columns), F32),
+        compiler_params=params(8),
+        cost_estimate=SHORT,
+        name="begin",
+    )(left, right)
+
+
+def contract_kernel(sizes, wide, count, begun, pieces, *refs):
+    left_refs, right_refs = refs[:count], refs[count : 2 * count]
+    outs, scratch = refs[2 * count + begun : -1], refs[-1]
     columns = right_refs[0].shape[0]
-    extra = ahead_ref.shape[0] - rest_ref.shape[0]
-    left = jnp.concatenate([ahead_ref[extra:, :], rest_ref[...]], axis=0)
     places = digits(0, sizes)
+    left = jnp.concatenate([ref[...] for ref in left_refs], axis=1)
     for n in range(columns // wide):
         here = slice(n * wide, (n + 1) * wide)
         right = jnp.concatenate([ref[here, :] for ref in right_refs], axis=1)
         value = lax.dot_general(left, right, (((1,), (1,)), ((), ())), preferred_element_type=F32)
+        if begun:
+            value = value + refs[2 * count][:, here]
         scratch[n % 2] = value.reshape(scratch.shape[1:])
         for q in range(outs[0].shape[0]):
-            for out, place in zip(outs, places):
-                out[q, :, here] = scratch[n % 2, q * sizes[0] + place].astype(out.dtype)
-
-
-def contract(left, right, sizes):
+            outs[0][q, :, here] = scratch[n % 2, q * sizes[0] + places[0]]
+            for s, place in enumerate(places[1:]):
+                piece, at = divmod(n * wide, columns // pieces)
+                out = outs[1 + s * pieces + piece]
+                out[q, :, at : at + wide] = scratch[n % 2, q * sizes[0] + place].astype(BF16)
+
+
+def contract(left, right, sizes, pieces=1, begun=()):
     columns = right[0].shape[0]
-    rows = 2 * left[1].shape[0]
+    rows = left[0].shape[0]
     owners = math.prod(sizes)
     wide = min(columns, 256)
+    pieces = pieces if columns // wide % pieces == 0 else 1
     shape = (owners // sizes[0], rows // owners, columns)
-    return pl.pallas_call(
-        functools.partial(contract_kernel, sizes, wide, len(right)),
-        in_specs=[whole()] * (2 + len(right)),
-        out_specs=[whole()] * sizes[0],
-        out_shape=[jax.ShapeDtypeStruct(shape, BF16 if s else F32) for s in range(sizes[0])],
+    part = (*shape[:2], columns // pieces)
+    kept, *sent = pl.pallas_call(
+        functools.partial(contract_kernel, sizes, wide, len(left), len(begun), pieces),
+        in_specs=[whole()] * (2 * len(left) + len(begun)),
+        out_specs=[whole()] * (1 + (sizes[0] - 1) * pieces),
+        out_shape=[jax.ShapeDtypeStruct(shape, F32)]
+        + [jax.ShapeDtypeStruct(part, BF16)] * ((sizes[0] - 1) * pieces),
         scratch_shapes=[pltpu.VMEM((2, owners, rows // owners, wide), F32)],
         compiler_params=params(8),
         cost_estimate=SHORT,
         name="contract",
-    )(*left, *right)
-
-
-def fold_kernel(number, sizes, arrived, *refs):
-    kept_ref, arrived_refs, outs = refs[0], refs[1 : 1 + arrived], refs[1 + arrived :]
+    )(*left, *right, *begun)
+    return [kept] + [sent[s * pieces : (s + 1) * pieces] for s in range(sizes[0] - 1)]
+
+
+def fold_kernel(number, sizes, counts, *refs):
+    kept_ref, arrived_refs, outs = refs[0], iter(refs[1 : 1 + sum(counts)]), refs[1 + sum(counts) :]
+    arrived = [[next(arrived_refs) for _ in range(count)] for count in counts]
     places = [0] if number == len(sizes) else digits(number, sizes)
     ways = len(places)
     for q in range(kept_ref.shape[0] // ways):
         for out, place in zip(outs, places):
             total = kept_ref[q * ways + place]
-            for ref in arrived_refs:
-                total = total + ref[q * ways + place].astype(F32)
+            for pieces in arrived:
+                values = [ref[q * ways + place].astype(F32) for ref in pieces]
+                total = total + jnp.concatenate(values, axis=-1)
             out[q] = total.astype(out.dtype)
 
 
@@ -243,14 +270,14 @@
     ways = 1 if number == len(sizes) else sizes[number]
     shape = (kept.shape[0] // ways, *kept.shape[1:])
     return pl.pallas_call(
-        functools.partial(fold_kernel, number, sizes, len(arrived)),
-        in_specs=[whole()] * (1 + len(arrived)),
+        functools.partial(fold_kernel, number, sizes, [len(pieces) for pieces in arrived]),
+        in_specs=[whole()] * (1 + sum(len(pieces) for pieces in arrived)),
         out_specs=[whole()] * ways,
         out_shape=[jax.ShapeDtypeStruct(shape, BF16 if s or all_leave else F32) for s in range(ways)],
         compiler_params=params(8),
         cost_estimate=SHORT,
         name="fold",
-    )(kept, *arrived)
+    )(kept, *[piece for pieces in arrived for piece in pieces])
 
 
 def shifted(block, axis, distance, size, span, turn=0):
@@ -274,7 +301,10 @@
 
 def stage(parts, number, sizes, all_leave=False):
     span = math.prod(sizes[:number])
-    arrived = [shifted(part, "cell", s + 1, sizes[number], span) for s, part in enumerate(parts[1:])]
+    arrived = []
+    for s, part in enumerate(parts[1:]):
+        pieces = part if isinstance(part, list) else [part]
+        arrived.append([shifted(piece, "cell", s + 1, sizes[number], span) for piece in pieces])
     return fold(parts[0], arrived, number + 1, sizes, all_leave)
 
 
@@ -396,20 +426,19 @@
     rows_here = mode_block // cell_devs
 
     flat = pod_modes.reshape(comps, mode_block, planes * rows_y, width)
-    half = mode_block // 2
-    first, held = lead(flat, advect_index, (), planes, rows_y, 0, half, True)
-    own = [first]
-    rows, before = {}, own[0]
+    first, held = lead(flat, advect_index, planes, rows_y, rows_y - 1)
+    rows, before = {}, first
     for r in [rows_y - 1, *range(rows_y - 1)]:
         rows[r] = edge(held, before, planes, rows_y, r)
         before = rows[r]
-    own += lead(held, advect_index, (before,), planes, rows_y, half, mode_block - half, False)
-    weight = weights(slab_map, slab_volume, own[1])
-    arrived = [[shifted(block, "mode", s, mode_devs, 1) for block in own] for s in range(1, mode_devs)]
+    weight = weights(slab_map, slab_volume, before)
+    own = [rows[r] for r in range(rows_y)]
+    ahead = [shifted(first, "mode", s, mode_devs, 1) for s in range(1, mode_devs)]
+    arrived = [[shifted(block, "mode", s, mode_devs, 1) for block in own[:-1]] for s in range(1, mode_devs)]
     up = [(i, i + 1) for i in range(cell_devs - 1)]
     rows[-1] = lax.ppermute(rows[rows_y - 1], "cell", up)
     rows[rows_y] = lax.ppermute(rows[0], "cell", [(j, i) for i, j in up])
-    leads = [own[0]] + [block[0] for block in arrived]
+    leads = [first] + ahead
     right = []
     for r in range(rows_y):
         if right:
@@ -426,15 +455,21 @@
         return list(parts)
 
     pairwise = sizes[:-1] + [2, 2] if sizes[-1] == 4 else sizes
-    mine = summed(contract(own, right, pairwise), 0, early, pairwise)
+    mine = contract(own, right, pairwise)
+    mine[0], ahead = lax.optimization_barrier((mine[0], ahead))
+    begun = begin(ahead[0], right[-1], mode_block)
+    mine = summed(mine, 0, early, pairwise)
+    mine, begun = lax.optimization_barrier((mine, begun))
     mine[0], arrived = lax.optimization_barrier((mine[0], arrived))
     mine = summed(mine, early, early + 1, pairwise)
     result = []
     for s in range(1, mode_devs):
-        block = contract(arrived[s - 1], right, sizes)
+        begun = begun if s == 1 else begin(ahead[s - 1], right[-1], mode_block)
+        block = contract(arrived[s - 1], right[:-1], sizes, 4, [begun])
+        block = summed(block, 0, early, sizes)
         if s == 1:
             mine, block = lax.optimization_barrier((mine, block))
-        block = stage(summed(block, 0, last - 1, sizes), last - 1, sizes, True)
+        block = stage(summed(block, early, last - 1, sizes), last - 1, sizes, True)
         if s == 1:
             mine = summed(mine, early + 1, early + 2, pairwise)
             mine = summed(mine, early + 2, len(pairwise), pairwise)

time: 74.5 us -> 71.7 us (0.962)
  waiting for transfers between devices: 26.1 us -> 22.5 us
  starting transfers between devices: 22.7 us -> 24.5 us
  Pallas kernels: 22.6 us -> 21.6 us
    ppermute x12 -> x15, waiting for transfers between devices: 26.1 us -> 22.5 us  [shifted(): return lax.ppermute(block, (axis, 'mode') if turn else axis, route)]
    ppermute x12 -> x15, starting transfers between devices: 19.9 us -> 21.7 us  [shifted(): return lax.ppermute(block, (axis, 'mode') if turn else axis, route)]
    pallas_call x10, Pallas kernels: 10.3 us -> 9.29 us  [the longest x2 5.93 us: contract(): pl.pallas_call(functools.partial(contract_kernel, sizes, wide, len(left),...]
  transfers between devices with their start and end apart: 14 -> 17, of which waited for: 8 -> 9; matrix products, arithmetic and copies ran while one was open for 0% -> 0% of each run, Pallas kernels for 25% -> 25%
where the time goes in v6:
time: 71.7 us; the launch traced here: 71.5 us
  starting transfers between devices  24.5 us (34%)
  waiting for transfers between devices  22.5 us (31%)
  Pallas kernels  21.6 us (30%)
  local copies, waits for them, and re-layouts  2.09 us (3%)
  between operations  0.85 us (1%)
    ppermute x15, waiting for transfers between devices, shifted(): return lax.ppermute(block, (axis, 'mode') if turn else axis, route)  22.5 us
    ppermute x15, starting transfers between devices, shifted(): return lax.ppermute(block, (axis, 'mode') if turn else axis, route)  21.7 us
    pallas_call x2, Pallas kernels, advected(): pl.pallas_call(functools.partial(advected_kernel, comps, planes, rows_y,...  6.3 us
    pallas_call x2, Pallas kernels, contract(): pl.pallas_call(functools.partial(contract_kernel, sizes, wide, len(left),...  5.93 us
    pallas_call x1, Pallas kernels, finish(): pl.pallas_call(functools.partial(finish_kernel, advect_count, per_block,...  2.66 us
    unnamed x16, local copies, waits for them, and re-layouts  2.09 us
    pallas_call x1, Pallas kernels, begin(): pl.pallas_call(functools.partial(begin_kernel, min(columns, 256)), in_spe...  1.81 us
    pallas_call x1, Pallas kernels, prepare(): pl.pallas_call(prepare_kernel, in_specs=[whole(pltpu.HBM)], out_specs=[wh...  1.76 us
  transfers between devices with their start and end apart: 17, of which 9 were waited for; matrix products, arithmetic and copies ran while one was open for 0% of the time, Pallas kernels for 25%

profile of v6, /device:TPU:0, one launch (start us, length us, event | category | flops | bytes accessed | tf_op | source)
XLA Modules:
  0.0 71.5 jit_solution(2499221167789844590)
XLA Ops:
  0.6 0.0 copy-start.5
  0.6 0.0 copy-start
  0.7 1.4 %copy-done = bf16[3,256,4,2,128]{4,3,2,1,0:T(2,128)(2,1)S(1)} copy-done((bf16[3,256,4,2,128]{4,3,2,1,0:T(2,128)(2,1)S(1)}, bf16[3,256,4,2,128]{4,3,2,1,0:T(2,128)(2,1)}, u32[]{:S(2)}) %copy-start) | copy-done | bytes 1572888
  2.1 0.0 copy-start.4
  2.1 0.7 copy-done.4
  2.7 0.0 copy-start.3
  2.7 1.2 %lead.1 = (bf16[272,1536]{1,0:T(8,128)(2,1)S(1)}, bf16[3,256,8,128]{3,2,1,0:T(8,128)(2,1)S(1)}) custom-call(s32[8]{0:T(128)S(1)} %copy-done.4, bf16[3,256,8,128]{3,2,1,0:T(8,128)(2,1)S(1)} %bitcast.12), custom_call_target="tpu_custom_call" | custom-call | flops 1 | bytes 1 | tf_op jit(solution)/shard_map/lead/pallas_call | solution.py:61
  3.9 3.0 %collective-permute-start.1 = (bf16[272,1536]{1,0:T(8,128)(2,1)S(1)}, bf16[272,1536]{1,0:T(8,128)(2,1)S(1)}, u32[]{:S(2)}, u32[]{:S(2)}) collective-permute-start(bf16[272,1536]{1,0:T(8,128)(2,1)S(1)} %get-tuple-element.46.after_ref.refs_0_), channel_id=1, source_target_pairs={{0,1},{1,0},{2,3},{3,2},{4,5},{5,4},{6,7},{7,6},{8,9},{9,8},{10,11... | collective-permute-start | bytes 2506760 | tf_op jit(solution)/shard_map/ppermute | solution.py:290
  7.0 0.5 edge.2.after_ref.over_ref.here_ref.refs_1_
  7.5 1.5 %collective-permute-start = (bf16[256,1536]{1,0:T(8,128)(2,1)S(1)}, bf16[256,1536]{1,0:T(8,128)(2,1)S(1)}, u32[]{:S(2)}, u32[]{:S(2)}) collective-permute-start(bf16[256,1536]{1,0:T(8,128)(2,1)S(1)} %edge.2.after_ref.over_ref.here_ref.refs_1_), channel_id=1, source_target_pairs={{0,2},{2,4},{4,6},{6,8},{8,10},{10,12},{12,14},{14,16},{16,18},{18... | collective-permute-start | bytes 2359304 | tf_op jit(solution)/shard_map/ppermute | solution.py:439
  9.0 0.5 edge.3.after_ref.here_ref.under_ref.refs_0_
  9.5 1.3 %collective-permute-start.2 = (bf16[256,1536]{1,0:T(8,128)(2,1)S(1)}, bf16[256,1536]{1,0:T(8,128)(2,1)S(1)}, u32[]{:S(2)}, u32[]{:S(2)}) collective-permute-start(bf16[256,1536]{1,0:T(8,128)(2,1)S(1)} %edge.3.after_ref.here_ref.under_ref.refs_0_), channel_id=1, source_target_pairs={{2,0},{4,2},{6,4},{8,6},{10,8},{12,10},{14,12},{16,14},{18,16},{20... | collective-permute-start | bytes 2359304 | tf_op jit(solution)/shard_map/ppermute | solution.py:440
  10.8 0.4 collective-permute-start.4
  11.2 0.0 copy-done.5
  11.2 0.0 copy-done.3
  11.2 0.5 weights.1.weight_ref
  11.7 0.0 collective-permute-done.under_ref
  11.8 14.6 %collective-permute-done.1.refs_1_.left_ref = bf16[272,1536]{1,0:T(8,128)(2,1)S(1)} collective-permute-done((bf16[272,1536]{1,0:T(8,128)(2,1)S(1)}, bf16[272,1536]{1,0:T(8,128)(2,1)S(1)}, u32[]{:S(2)}, u32[]{:S(2)}) %collective-permute-start.1) | collective-permute-done | bytes 835616 | tf_op jit(solution)/shard_map/ppermute | solution.py:290
  26.4 3.1 %advected.2 = bf16[8,256,1536]{2,1,0:T(8,128)(2,1)S(1)} custom-call(f32[8,128]{1,0:T(8,128)S(1)} %weights.1.weight_ref, bf16[256,1536]{1,0:T(8,128)(2,1)S(1)} %edge.3.after_ref.here_ref.under_ref.refs_0_, bf16[256,1536]{1,0:T(8,128)(2,1)S(1)} %collective-permute-done.under_ref, bf16[256,1536]{1,0:T(8,128)(2,1)S(1)} %edge.2.after_ref.over_ref.here_ref.refs_1_, ...), custom_call_target="tpu_custom_call" | custom-call | flops 1 | bytes 1 | tf_op jit(solution)/shard_map/advected/pallas_call | solution.py:171
  29.5 0.0 collective-permute-done.2.over_ref
  29.6 3.2 %advected.3 = bf16[8,256,1536]{2,1,0:T(8,128)(2,1)S(1)} custom-call(f32[8,128]{1,0:T(8,128)S(1)} %weights.1.weight_ref, bf16[256,1536]{1,0:T(8,128)(2,1)S(1)} %edge.2.after_ref.over_ref.here_ref.refs_1_, bf16[256,1536]{1,0:T(8,128)(2,1)S(1)} %edge.3.after_ref.here_ref.under_ref.refs_0_, bf16[256,1536]{1,0:T(8,128)(2,1)S(1)} %collective-permute-done.2.over_ref, ...), custom_call_target="tpu_custom_call" | custom-call | flops 1 | bytes 1 | tf_op jit(solution)/shard_map/advected/pallas_call | solution.py:171
  32.7 3.8 %contract.2 = (f32[8,16,2048]{2,1,0:T(8,128)S(1)}, bf16[8,16,2048]{2,1,0:T(8,128)(2,1)S(1)}) custom-call(bf16[256,1536]{1,0:T(8,128)(2,1)S(1)} %edge.3.after_ref.here_ref.under_ref.refs_0_, bf16[256,1536]{1,0:T(8,128)(2,1)S(1)} %edge.2.after_ref.over_ref.here_ref.refs_1_, bf16[2048,1536]{1,0:T(8,128)(2,1)S(1)} %bitcast.6, bf16[2048,1536]{1,0:T(8,128)(2,1)S(1)} %bitcast.8), custom_call_target="tpu_custom_call" | custom-call | flops 1 | bytes 1 | tf_op jit(solution)/shard_map/contract/pallas_call | solution.py:241
  36.5 2.0 %collective-permute-start.3 = (bf16[8,16,2048]{2,1,0:T(8,128)(2,1)S(1)}, bf16[8,16,2048]{2,1,0:T(8,128)(2,1)S(1)}, u32[]{:S(2)}, u32[]{:S(2)}) collective-permute-start(bf16[8,16,2048]{2,1,0:T(8,128)(2,1)S(1)} %get-tuple-element.51), channel_id=1, source_target_pairs={{0,2},{2,0},{4,6},{6,4},{8,10},{10,8},{12,14},{14,12},{16,18},{18,... | collective-permute-start | bytes 1572872 | tf_op jit(solution)/shard_map/ppermute | solution.py:290
  38.5 0.0 slice-start
  38.5 1.8 %begin.1.refs_2_ = f32[256,2048]{1,0:T(8,128)S(1)} custom-call(bf16[272,1536]{1,0:T(8,128)(2,1)S(1)} %collective-permute-done.1.refs_1_.left_ref, bf16[2048,1536]{1,0:T(8,128)(2,1)S(1)} %bitcast.9), custom_call_target="tpu_custom_call" | custom-call | flops 1 | bytes 1 | tf_op jit(solution)/shard_map/begin/pallas_call | solution.py:201
  40.4 0.0 collective-permute-done.3.refs_1_
  40.4 0.1 fold.6
  40.5 0.0 slice-start.1
  40.5 2.5 %collective-permute-start.5 = (bf16[4,16,2048]{2,1,0:T(8,128)(2,1)S(1)}, bf16[4,16,2048]{2,1,0:T(8,128)(2,1)S(1)}, u32[]{:S(2)}, u32[]{:S(2)}) collective-permute-start(bf16[4,16,2048]{2,1,0:T(8,128)(2,1)S(1)} %get-tuple-element.57), channel_id=1, source_target_pairs={{0,4},{2,6},{4,0},{6,2},{8,12},{10,14},{12,8},{14,10},{16,20},{18,... | collective-permute-start | bytes 786440 | tf_op jit(solution)/shard_map/ppermute | solution.py:290
  43.0 0.0 collective-permute-done.4.refs_0_
  43.0 2.1 %contract.3 = (f32[8,16,2048]{2,1,0:T(8,128)S(1)}, bf16[8,16,512]{2,1,0:T(8,128)(2,1)S(1)}, bf16[8,16,512]{2,1,0:T(8,128)(2,1)S(1)}, bf16[8,16,512]{2,1,0:T(8,128)(2,1)S(1)}, bf16[8,16,512]{2,1,0:T(8,128)(2,1)S(1)}) custom-call(bf16[256,1536]{1,0:T(8,128)(2,1)S(1)} %collective-permute-done.4.refs_0_, bf16[2048,1536]{1,0:T(8,128)(2,1)S(1)} %bitcast.7, ...), custom_call_target="tpu_custom_call" | custom-call | flops 1 | bytes 1 | tf_op jit(solution)/shard_map/contract/pallas_call | solution.py:241
  45.1 0.2 collective-permute-start.6
  45.4 0.3 collective-permute-start.7
  45.7 0.2 collective-permute-start.8
  45.9 0.3 collective-permute-start.9
  46.2 0.3 collective-permute-done.6.refs_1_
  46.5 0.2 collective-permute-done.7.refs_2_
  46.7 0.3 collective-permute-done.8.refs_3_
  47.0 0.2 collective-permute-done.9.refs_4_
  47.2 0.1 fold.8
  47.3 2.6 %collective-permute-done.5.refs_1_ = bf16[4,16,2048]{2,1,0:T(8,128)(2,1)S(1)} collective-permute-done((bf16[4,16,2048]{2,1,0:T(8,128)(2,1)S(1)}, bf16[4,16,2048]{2,1,0:T(8,128)(2,1)S(1)}, u32[]{:S(2)}, u32[]{:S(2)}) %collective-permute-start.5) | collective-permute-done | bytes 262176 | tf_op jit(solution)/shard_map/ppermute | solution.py:290
  50.0 1.8 %collective-permute-start.12 = (bf16[4,16,2048]{2,1,0:T(8,128)(2,1)S(1)}, bf16[4,16,2048]{2,1,0:T(8,128)(2,1)S(1)}, u32[]{:S(2)}, u32[]{:S(2)}) collective-permute-start(bf16[4,16,2048]{2,1,0:T(8,128)(2,1)S(1)} %get-tuple-element.74), channel_id=1, source_target_pairs={{0,4},{2,6},{4,0},{6,2},{8,12},{10,14},{12,8},{14,10},{16,20},{18,... | collective-permute-start | bytes 786440 | tf_op jit(solution)/shard_map/ppermute | solution.py:290
  51.8 1.6 %collective-permute-start.10 = (bf16[2,16,2048]{2,1,0:T(8,128)(2,1)S(1)}, bf16[2,16,2048]{2,1,0:T(8,128)(2,1)S(1)}, u32[]{:S(2)}, u32[]{:S(2)}) collective-permute-start(bf16[2,16,2048]{2,1,0:T(8,128)(2,1)S(1)} %get-tuple-element.70), channel_id=1, source_target_pairs={{0,8},{2,10},{4,12},{6,14},{8,0},{10,2},{12,4},{14,6},{16,24},{18,... | collective-permute-start | bytes 393224 | tf_op jit(solution)/shard_map/ppermute | solution.py:290
  53.3 3.4 %collective-permute-done.10.refs_1_ = bf16[2,16,2048]{2,1,0:T(8,128)(2,1)S(1)} collective-permute-done((bf16[2,16,2048]{2,1,0:T(8,128)(2,1)S(1)}, bf16[2,16,2048]{2,1,0:T(8,128)(2,1)S(1)}, u32[]{:S(2)}, u32[]{:S(2)}) %collective-permute-start.10) | collective-permute-done | bytes 131104 | tf_op jit(solution)/shard_map/ppermute | solution.py:290
  56.8 2.7 %collective-permute-start.11 = (bf16[1,16,2048]{2,1,0:T(8,128)(2,1)S(1)}, bf16[1,16,2048]{2,1,0:T(8,128)(2,1)S(1)}, u32[]{:S(2)}, u32[]{:S(2)}) collective-permute-start(bf16[1,16,2048]{2,1,0:T(8,128)(2,1)S(1)} %get-tuple-element.72), channel_id=1, source_target_pairs={{0,16},{2,18},{4,20},{6,22},{8,24},{10,26},{12,28},{14,30},{16,0},... | collective-permute-start | bytes 196616 | tf_op jit(solution)/shard_map/ppermute | solution.py:290
  59.4 0.0 collective-permute-done.12.refs_1_
  59.5 0.6 collective-permute-start.13
  60.0 1.2 %collective-permute-start.14 = (bf16[1,16,2048]{2,1,0:T(8,128)(2,1)S(1)}, bf16[1,16,2048]{2,1,0:T(8,128)(2,1)S(1)}, u32[]{:S(2)}, u32[]{:S(2)}) collective-permute-start(bf16[1,16,2048]{2,1,0:T(8,128)(2,1)S(1)} %get-tuple-element.82), channel_id=1, source_target_pairs={{0,9},{1,8},{2,11},{3,10},{4,13},{5,12},{6,15},{7,14},{8,17},{9,16... | collective-permute-start | bytes 196616 | tf_op jit(solution)/shard_map/ppermute | solution.py:290
  61.3 1.6 %collective-permute-start.15 = (bf16[1,16,2048]{2,1,0:T(8,128)(2,1)S(1)}, bf16[1,16,2048]{2,1,0:T(8,128)(2,1)S(1)}, u32[]{:S(2)}, u32[]{:S(2)}) collective-permute-start(bf16[1,16,2048]{2,1,0:T(8,128)(2,1)S(1)} %get-tuple-element.83), channel_id=1, source_target_pairs={{0,17},{1,16},{2,19},{3,18},{4,21},{5,20},{6,23},{7,22},{8,25},{9,... | collective-permute-start | bytes 196616 | tf_op jit(solution)/shard_map/ppermute | solution.py:290
  62.8 3.3 %collective-permute-start.16 = (bf16[1,16,2048]{2,1,0:T(8,128)(2,1)S(1)}, bf16[1,16,2048]{2,1,0:T(8,128)(2,1)S(1)}, u32[]{:S(2)}, u32[]{:S(2)}) collective-permute-start(bf16[1,16,2048]{2,1,0:T(8,128)(2,1)S(1)} %get-tuple-element.84), channel_id=1, source_target_pairs={{0,25},{1,24},{2,27},{3,26},{4,29},{5,28},{6,31},{7,30},{8,1},{9,0... | collective-permute-start | bytes 196616 | tf_op jit(solution)/shard_map/ppermute | solution.py:290
  66.1 0.0 collective-permute-done.11.refs_1_
  66.1 0.0 slice-done
  66.1 0.0 slice-done.1
  66.2 0.0 copy-start.1
  66.2 0.0 copy-start.2
  66.2 1.8 %prepare.1 = (bf16[2048,1024]{1,0:T(8,128)(2,1)S(1)}, bf16[2048,1024]{1,0:T(8,128)(2,1)S(1)}) custom-call(f32[2048,1024]{1,0:T(8,128)S(1)} %bitcast.11), custom_call_target="tpu_custom_call" | custom-call | flops 8388608 | bytes 16777216 | tf_op jit(solution)/shard_map/prepare/pallas_call | solution.py:328
  67.9 0.0 collective-permute-done.13.refs_1_
  68.0 0.0 collective-permute-done.14.refs_2_
  68.0 0.8 %collective-permute-done.15.refs_3_ = bf16[1,16,2048]{2,1,0:T(8,128)(2,1)S(1)} collective-permute-done((bf16[1,16,2048]{2,1,0:T(8,128)(2,1)S(1)}, bf16[1,16,2048]{2,1,0:T(8,128)(2,1)S(1)}, u32[]{:S(2)}, u32[]{:S(2)}) %collective-permute-start.15) | collective-permute-done | bytes 65568 | tf_op jit(solution)/shard_map/ppermute | solution.py:290
  68.7 0.1 collective-permute-done.16.refs_4_
  68.8 0.0 copy-done.1
  68.8 0.0 copy-done.2
  68.8 2.7 %finish.1 = (f32[16,8,512]{2,1,0:T(8,128)}, f32[16,1024]{1,0:T(8,128)}) custom-call(s32[1,2048]{1,0:T(1,128)S(1)} %bitcast.13, s32[1,2048]{1,0:T(1,128)S(1)} %bitcast.14, f32[1,16,2048]{2,1,0:T(8,128)S(1)} %fold.10.refs_0_, bf16[1,16,2048]{2,1,0:T(8,128)(2,1)S(1)} %collective-permute-done.13.refs_1_, ...), custom_call_target="tpu_custom_call" | custom-call | flops 1 | bytes 1 | tf_op jit(solution)/shard_map/finish/pallas_call | solution.py:404
  (5 shorter events, 0.1 us)
Async XLA Ops:
  0.6 10.6 %copy-start.5 = (f32[8]{0:T(128)S(1)}, f32[8]{0:T(128)}, u32[]{:S(2)}) copy-start(f32[8]{0:T(128)} %volume_ref.1) | copy-start | bytes 100
  0.6 1.4 %copy-start = (bf16[3,256,4,2,128]{4,3,2,1,0:T(2,128)(2,1)S(1)}, bf16[3,256,4,2,128]{4,3,2,1,0:T(2,128)(2,1)}, u32[]{:S(2)}) copy-start(bf16[3,256,4,2,128]{4,3,2,1,0:T(2,128)(2,1)} %param.7) | copy-start | bytes 4718596
  2.1 0.7 copy-start.4
  2.7 8.5 %copy-start.3 = (s32[4,2,128]{2,1,0:T(2,128)S(1)}, s32[4,2,128]{2,1,0:T(2,128)}, u32[]{:S(2)}) copy-start(s32[4,2,128]{2,1,0:T(2,128)} %param.8) | copy-start | bytes 12292
  3.9 22.5 %collective-permute-start.1 = (bf16[272,1536]{1,0:T(8,128)(2,1)S(1)}, bf16[272,1536]{1,0:T(8,128)(2,1)S(1)}, u32[]{:S(2)}, u32[]{:S(2)}) collective-permute-start(bf16[272,1536]{1,0:T(8,128)(2,1)S(1)} %get-tuple-element.46.after_ref.refs_0_), channel_id=1, source_target_pairs={{0,1},{1,0},{2,3},{3,2},{4,5},{5,4},{6,7},{7,6},{8,9},{9,8},{10,11... | collective-permute-start | bytes 2506760 | tf_op jit(solution)/shard_map/ppermute | solution.py:290
  7.5 4.3 %collective-permute-start = (bf16[256,1536]{1,0:T(8,128)(2,1)S(1)}, bf16[256,1536]{1,0:T(8,128)(2,1)S(1)}, u32[]{:S(2)}, u32[]{:S(2)}) collective-permute-start(bf16[256,1536]{1,0:T(8,128)(2,1)S(1)} %edge.2.after_ref.over_ref.here_ref.refs_1_), channel_id=1, source_target_pairs={{0,2},{2,4},{4,6},{6,8},{8,10},{10,12},{12,14},{14,16},{16,18},{18... | collective-permute-start | bytes 2359304 | tf_op jit(solution)/shard_map/ppermute | solution.py:439
  9.5 20.0 %collective-permute-start.2 = (bf16[256,1536]{1,0:T(8,128)(2,1)S(1)}, bf16[256,1536]{1,0:T(8,128)(2,1)S(1)}, u32[]{:S(2)}, u32[]{:S(2)}) collective-permute-start(bf16[256,1536]{1,0:T(8,128)(2,1)S(1)} %edge.3.after_ref.here_ref.under_ref.refs_0_), channel_id=1, source_target_pairs={{2,0},{4,2},{6,4},{8,6},{10,8},{12,10},{14,12},{16,14},{18,16},{20... | collective-permute-start | bytes 2359304 | tf_op jit(solution)/shard_map/ppermute | solution.py:440
  10.8 32.2 %collective-permute-start.4 = (bf16[256,1536]{1,0:T(8,128)(2,1)S(1)}, bf16[256,1536]{1,0:T(8,128)(2,1)S(1)}, u32[]{:S(2)}, u32[]{:S(2)}) collective-permute-start(bf16[256,1536]{1,0:T(8,128)(2,1)S(1)} %edge.3.after_ref.here_ref.under_ref.refs_0_), channel_id=1, source_target_pairs={{0,1},{1,0},{2,3},{3,2},{4,5},{5,4},{6,7},{7,6},{8,9},{9,8},{10,11... | collective-permute-start | bytes 2359304 | tf_op jit(solution)/shard_map/ppermute | solution.py:290
  36.5 3.9 %collective-permute-start.3 = (bf16[8,16,2048]{2,1,0:T(8,128)(2,1)S(1)}, bf16[8,16,2048]{2,1,0:T(8,128)(2,1)S(1)}, u32[]{:S(2)}, u32[]{:S(2)}) collective-permute-start(bf16[8,16,2048]{2,1,0:T(8,128)(2,1)S(1)} %get-tuple-element.51), channel_id=1, source_target_pairs={{0,2},{2,0},{4,6},{6,4},{8,10},{10,8},{12,14},{14,12},{16,18},{18,... | collective-permute-start | bytes 1572872 | tf_op jit(solution)/shard_map/ppermute | solution.py:290
  38.5 27.6 %slice-start = ((s8[8388608]{0:T(1024)(128)(4,1)}), s8[4194304]{0:T(1024)(128)(4,1)S(1)}, s32[]{:S(2)}) async-start(s8[8388608]{0:T(1024)(128)(4,1)} %bitcast.10), calls=%async_computation | async-start | bytes 8388608
  40.5 25.7 %slice-start.1 = ((s8[8388608]{0:T(1024)(128)(4,1)}), s8[4194304]{0:T(1024)(128)(4,1)S(1)}, s32[]{:S(2)}) async-start(s8[8388608]{0:T(1024)(128)(4,1)} %bitcast.10), calls=%async_computation.1 | async-start | bytes 8388608
  40.5 9.4 %collective-permute-start.5 = (bf16[4,16,2048]{2,1,0:T(8,128)(2,1)S(1)}, bf16[4,16,2048]{2,1,0:T(8,128)(2,1)S(1)}, u32[]{:S(2)}, u32[]{:S(2)}) collective-permute-start(bf16[4,16,2048]{2,1,0:T(8,128)(2,1)S(1)} %get-tuple-element.57), channel_id=1, source_target_pairs={{0,4},{2,6},{4,0},{6,2},{8,12},{10,14},{12,8},{14,10},{16,20},{18,... | collective-permute-start | bytes 786440 | tf_op jit(solution)/shard_map/ppermute | solution.py:290
  45.1 1.4 %collective-permute-start.6 = (bf16[8,16,512]{2,1,0:T(8,128)(2,1)S(1)}, bf16[8,16,512]{2,1,0:T(8,128)(2,1)S(1)}, u32[]{:S(2)}, u32[]{:S(2)}) collective-permute-start(bf16[8,16,512]{2,1,0:T(8,128)(2,1)S(1)} %get-tuple-element.63), channel_id=1, source_target_pairs={{0,2},{2,0},{4,6},{6,4},{8,10},{10,8},{12,14},{14,12},{16,18},{18,... | collective-permute-start | bytes 393224 | tf_op jit(solution)/shard_map/ppermute | solution.py:290
  45.4 1.4 %collective-permute-start.7 = (bf16[8,16,512]{2,1,0:T(8,128)(2,1)S(1)}, bf16[8,16,512]{2,1,0:T(8,128)(2,1)S(1)}, u32[]{:S(2)}, u32[]{:S(2)}) collective-permute-start(bf16[8,16,512]{2,1,0:T(8,128)(2,1)S(1)} %get-tuple-element.64), channel_id=1, source_target_pairs={{0,2},{2,0},{4,6},{6,4},{8,10},{10,8},{12,14},{14,12},{16,18},{18,... | collective-permute-start | bytes 393224 | tf_op jit(solution)/shard_map/ppermute | solution.py:290
  45.7 1.3 %collective-permute-start.8 = (bf16[8,16,512]{2,1,0:T(8,128)(2,1)S(1)}, bf16[8,16,512]{2,1,0:T(8,128)(2,1)S(1)}, u32[]{:S(2)}, u32[]{:S(2)}) collective-permute-start(bf16[8,16,512]{2,1,0:T(8,128)(2,1)S(1)} %get-tuple-element.65), channel_id=1, source_target_pairs={{0,2},{2,0},{4,6},{6,4},{8,10},{10,8},{12,14},{14,12},{16,18},{18,... | collective-permute-start | bytes 393224 | tf_op jit(solution)/shard_map/ppermute | solution.py:290
  45.9 1.4 %collective-permute-start.9 = (bf16[8,16,512]{2,1,0:T(8,128)(2,1)S(1)}, bf16[8,16,512]{2,1,0:T(8,128)(2,1)S(1)}, u32[]{:S(2)}, u32[]{:S(2)}) collective-permute-start(bf16[8,16,512]{2,1,0:T(8,128)(2,1)S(1)} %get-tuple-element.66), channel_id=1, source_target_pairs={{0,2},{2,0},{4,6},{6,4},{8,10},{10,8},{12,14},{14,12},{16,18},{18,... | collective-permute-start | bytes 393224 | tf_op jit(solution)/shard_map/ppermute | solution.py:290
  50.0 9.5 %collective-permute-start.12 = (bf16[4,16,2048]{2,1,0:T(8,128)(2,1)S(1)}, bf16[4,16,2048]{2,1,0:T(8,128)(2,1)S(1)}, u32[]{:S(2)}, u32[]{:S(2)}) collective-permute-start(bf16[4,16,2048]{2,1,0:T(8,128)(2,1)S(1)} %get-tuple-element.74), channel_id=1, source_target_pairs={{0,4},{2,6},{4,0},{6,2},{8,12},{10,14},{12,8},{14,10},{16,20},{18,... | collective-permute-start | bytes 786440 | tf_op jit(solution)/shard_map/ppermute | solution.py:290
  51.8 5.0 %collective-permute-start.10 = (bf16[2,16,2048]{2,1,0:T(8,128)(2,1)S(1)}, bf16[2,16,2048]{2,1,0:T(8,128)(2,1)S(1)}, u32[]{:S(2)}, u32[]{:S(2)}) collective-permute-start(bf16[2,16,2048]{2,1,0:T(8,128)(2,1)S(1)} %get-tuple-element.70), channel_id=1, source_target_pairs={{0,8},{2,10},{4,12},{6,14},{8,0},{10,2},{12,4},{14,6},{16,24},{18,... | collective-permute-start | bytes 393224 | tf_op jit(solution)/shard_map/ppermute | solution.py:290
  56.8 9.4 %collective-permute-start.11 = (bf16[1,16,2048]{2,1,0:T(8,128)(2,1)S(1)}, bf16[1,16,2048]{2,1,0:T(8,128)(2,1)S(1)}, u32[]{:S(2)}, u32[]{:S(2)}) collective-permute-start(bf16[1,16,2048]{2,1,0:T(8,128)(2,1)S(1)} %get-tuple-element.72), channel_id=1, source_target_pairs={{0,16},{2,18},{4,20},{6,22},{8,24},{10,26},{12,28},{14,30},{16,0},... | collective-permute-start | bytes 196616 | tf_op jit(solution)/shard_map/ppermute | solution.py:290
  59.5 8.5 %collective-permute-start.13 = (bf16[1,16,2048]{2,1,0:T(8,128)(2,1)S(1)}, bf16[1,16,2048]{2,1,0:T(8,128)(2,1)S(1)}, u32[]{:S(2)}, u32[]{:S(2)}) collective-permute-start(bf16[1,16,2048]{2,1,0:T(8,128)(2,1)S(1)} %get-tuple-element.81), channel_id=1, source_target_pairs={{0,1},{1,0},{2,3},{3,2},{4,5},{5,4},{6,7},{7,6},{8,9},{9,8},{10,11... | collective-permute-start | bytes 196616 | tf_op jit(solution)/shard_map/ppermute | solution.py:290
  60.0 7.9 %collective-permute-start.14 = (bf16[1,16,2048]{2,1,0:T(8,128)(2,1)S(1)}, bf16[1,16,2048]{2,1,0:T(8,128)(2,1)S(1)}, u32[]{:S(2)}, u32[]{:S(2)}) collective-permute-start(bf16[1,16,2048]{2,1,0:T(8,128)(2,1)S(1)} %get-tuple-element.82), channel_id=1, source_target_pairs={{0,9},{1,8},{2,11},{3,10},{4,13},{5,12},{6,15},{7,14},{8,17},{9,16... | collective-permute-start | bytes 196616 | tf_op jit(solution)/shard_map/ppermute | solution.py:290
  61.3 7.5 %collective-permute-start.15 = (bf16[1,16,2048]{2,1,0:T(8,128)(2,1)S(1)}, bf16[1,16,2048]{2,1,0:T(8,128)(2,1)S(1)}, u32[]{:S(2)}, u32[]{:S(2)}) collective-permute-start(bf16[1,16,2048]{2,1,0:T(8,128)(2,1)S(1)} %get-tuple-element.83), channel_id=1, source_target_pairs={{0,17},{1,16},{2,19},{3,18},{4,21},{5,20},{6,23},{7,22},{8,25},{9,... | collective-permute-start | bytes 196616 | tf_op jit(solution)/shard_map/ppermute | solution.py:290
  62.8 6.0 %collective-permute-start.16 = (bf16[1,16,2048]{2,1,0:T(8,128)(2,1)S(1)}, bf16[1,16,2048]{2,1,0:T(8,128)(2,1)S(1)}, u32[]{:S(2)}, u32[]{:S(2)}) collective-permute-start(bf16[1,16,2048]{2,1,0:T(8,128)(2,1)S(1)} %get-tuple-element.84), channel_id=1, source_target_pairs={{0,25},{1,24},{2,27},{3,26},{4,29},{5,28},{6,31},{7,30},{8,1},{9,0... | collective-permute-start | bytes 196616 | tf_op jit(solution)/shard_map/ppermute | solution.py:290
  66.2 2.7 %copy-start.1 = (s32[2048]{0:T(1024)S(1)}, s32[2048]{0:T(1024)}, u32[]{:S(2)}) copy-start(s32[2048]{0:T(1024)} %param.11) | copy-start | bytes 24580
  66.2 2.7 %copy-start.2 = (s32[2048]{0:T(1024)S(1)}, s32[2048]{0:T(1024)}, u32[]{:S(2)}) copy-start(s32[2048]{0:T(1024)} %param.12) | copy-start | bytes 24580

commit v7 on v6

--- a/solution.py
+++ b/solution.py
@@ -138,7 +138,7 @@
     def difference(x, y):
         return (x - y).astype(F32)
 
-    @pl.loop(0, modes // tall)
+    @pl.loop(0, modes // tall, unroll=2)
     def _(b):
         here = pl.ds(pl.multiple_of(b * tall, tall), tall)
 
@@ -308,12 +308,33 @@
     return fold(parts[0], arrived, number + 1, sizes, all_leave)
 
 
-def prepare_kernel(amp_ref, high_ref, low_ref, amps, sems):
+def columns_of(flat, first, blocks, total, found, adv, mode, me, advect_count, per_block):
+    rows, groups = found.shape[0], flat.shape[2] // LANES
+    part = lax.rem(mode // per_block - me + total, total)
+    slot = (part * advect_count + adv) * per_block + lax.rem(mode, per_block)
+    lane = jnp.broadcast_to(lax.rem(slot, LANES), (rows, LANES))
+    group = jnp.broadcast_to(slot // LANES, (rows, LANES))
+    for b in range(blocks):
+        for s in range(groups):
+            source = flat[b, :, s * LANES : (s + 1) * LANES]
+            taken = jnp.take_along_axis(source, lane, axis=1)
+            found = jnp.where(group == (first + b) * groups + s, taken, found)
+    return found
+
+
+def prepare_kernel(blocks, advect_count, per_block, scale_factor, adv_ref, mode_ref, own_ref, amp_ref, high_ref, low_ref, found_ref, flat, amps, sems):
     steps, tall, _ = amps.shape
     copies = []
     for i in range(steps):
         copies.append(pltpu.make_async_copy(amp_ref.at[pl.ds(i * tall, tall)], amps.at[i], sems.at[i]))
         copies[-1].start()
+    flat[0] = own_ref[0] * scale_factor
+    for g in range(found_ref.shape[1] // LANES):
+        here = slice(g * LANES, (g + 1) * LANES)
+        found = jnp.zeros((found_ref.shape[0], LANES), F32)
+        me = lax.axis_index("mode")
+        pairs = adv_ref[:, here], mode_ref[:, here]
+        found_ref[:, here] = columns_of(flat, 0, 1, blocks, found, *pairs, me, advect_count, per_block)
     for i in range(steps):
         copies[i].wait()
         amp = amps[i]
@@ -322,26 +343,29 @@
         low_ref[i * tall : (i + 1) * tall, :] = (amp - high.astype(F32)).astype(BF16)
 
 
-def prepare(amp):
+def prepare(pair_adv, pair_mode, own, amp, blocks, advect_count, scale_factor):
     pairs, snaps = amp.shape
+    _, rows, columns = own.shape
     tall = 256 if pairs % 256 == 0 else pairs
-    return pl.pallas_call(
-        prepare_kernel,
-        in_specs=[whole(pltpu.HBM)],
-        out_specs=[whole()] * 2,
-        out_shape=[jax.ShapeDtypeStruct(amp.shape, BF16)] * 2,
+    per_block = columns // advect_count
+    return pl.pallas_call(
+        functools.partial(prepare_kernel, blocks, advect_count, per_block, scale_factor),
+        in_specs=[whole()] * 3 + [whole(pltpu.HBM)],
+        out_specs=[whole()] * 3,
+        out_shape=[jax.ShapeDtypeStruct(amp.shape, BF16)] * 2 + [jax.ShapeDtypeStruct((rows, pairs), F32)],
         scratch_shapes=[
+            pltpu.VMEM((1, rows, columns), F32),
             pltpu.VMEM((pairs // tall, tall, snaps), F32),
             pltpu.SemaphoreType.DMA((pairs // tall,)),
         ],
         compiler_params=params(24),
         cost_estimate=pl.CostEstimate(flops=4 * amp.size, bytes_accessed=8 * amp.size, transcendentals=0),
         name="prepare",
-    )(amp)
+    )(pair_adv.reshape(1, pairs), pair_mode.reshape(1, pairs), own, amp)
 
 
 def finish_kernel(advect_count, per_block, scale_factor, counts, adv_ref, mode_ref, *refs):
-    *part_refs, high_ref, low_ref, tensor_ref, out_ref, flat = refs
+    *part_refs, high_ref, low_ref, found_ref, tensor_ref, out_ref, flat = refs
     blocks, rows = flat.shape[0], flat.shape[1]
     me = lax.axis_index("mode")
     tall = 512 if high_ref.shape[0] % 512 == 0 else high_ref.shape[0]
@@ -360,23 +384,14 @@
                 value = jnp.where(lax.rem(me + s, blocks) == b, flat[s, :, at], value)
             tensor_ref[:, j, b * per_block : (b + 1) * per_block] = value
 
-    groups = flat.shape[2] // LANES
-
     def columns(i):
         high, low = [], []
         for g in range(i * tall // LANES, (i + 1) * tall // LANES):
             here = slice(g * LANES, (g + 1) * LANES)
-            mode = mode_ref[:, here]
-            part = lax.rem(mode // per_block - me + blocks, blocks)
-            slot = (part * advect_count + adv_ref[:, here]) * per_block + lax.rem(mode, per_block)
-            lane = jnp.broadcast_to(lax.rem(slot, LANES), (rows, LANES))
-            group = jnp.broadcast_to(slot // LANES, (rows, LANES))
-            found = jnp.zeros((rows, LANES), F32)
-            for b in range(blocks):
-                for s in range(groups):
-                    source = flat[b, :, s * LANES : (s + 1) * LANES]
-                    taken = jnp.take_along_axis(source, lane, axis=1)
-                    found = jnp.where(group == b * groups + s, taken, found)
+            pairs = adv_ref[:, here], mode_ref[:, here]
+            found = columns_of(
+                flat.at[1:], 1, blocks - 1, blocks, found_ref[:, here], *pairs, me, advect_count, per_block
+            )
             high.append(found.astype(BF16).astype(F32))
             low.append(found - high[-1])
         both = [jnp.concatenate(high, axis=1), jnp.concatenate(low, axis=1)]
@@ -394,7 +409,7 @@
     out_ref[...] = total
 
 
-def finish(pair_adv, pair_mode, parts, high, low, advect_count, scale_factor):
+def finish(pair_adv, pair_mode, parts, high, low, found, advect_count, scale_factor):
     pairs, snaps = high.shape
     _, rows, columns = parts[0][0].shape
     blocks = len(parts)
@@ -403,7 +418,7 @@
     per_block = columns // advect_count
     return pl.pallas_call(
         functools.partial(finish_kernel, advect_count, per_block, scale_factor, counts),
-        in_specs=[whole()] * (4 + len(terms)),
+        in_specs=[whole()] * (5 + len(terms)),
         out_specs=[whole(), whole()],
         out_shape=[
             jax.ShapeDtypeStruct((rows, advect_count, blocks * per_block), F32),
@@ -413,7 +428,7 @@
         compiler_params=params(8),
         cost_estimate=SHORT,
         name="finish",
-    )(pair_adv.reshape(1, pairs), pair_mode.reshape(1, pairs), *terms, high, low)
+    )(pair_adv.reshape(1, pairs), pair_mode.reshape(1, pairs), *terms, high, low, found)
 
 
 def shards(pod_modes, slab_map, slab_volume, advect_index, pair_adv, pair_mode, pair_amp):
@@ -478,8 +493,10 @@
             result.append(mine)
         span = math.prod(sizes[:last])
         result.append([shifted(b, "cell", n, sizes[last], span, mode_devs - s) for n, b in enumerate(block)])
-    high, low = prepare(pair_amp)
-    tensor, response = finish(pair_adv, pair_mode, result, high, low, advect_count, scale_factor)
+    high, low, found = prepare(
+        pair_adv, pair_mode, result[0][0], pair_amp, mode_devs, advect_count, scale_factor
+    )
+    tensor, response = finish(pair_adv, pair_mode, result, high, low, found, advect_count, scale_factor)
     return (tensor, response)
 
 

time: 71.7 us -> 71.2 us (level)
  no operation moved by 1% of the time
where the time goes in v7:
time: 71.2 us; the launch traced here: 71.1 us
  starting transfers between devices  24.5 us (34%)
  Pallas kernels  21.8 us (31%)
  waiting for transfers between devices  21.8 us (31%)
  local copies, waits for them, and re-layouts  2.09 us (3%)
  between operations  0.87 us (1%)
    ppermute x15, waiting for transfers between devices, shifted(): return lax.ppermute(block, (axis, 'mode') if turn else axis, route)  21.8 us
    ppermute x15, starting transfers between devices, shifted(): return lax.ppermute(block, (axis, 'mode') if turn else axis, route)  21.7 us
    pallas_call x2, Pallas kernels, advected(): pl.pallas_call(functools.partial(advected_kernel, comps, planes, rows_y,...  6.09 us
    pallas_call x2, Pallas kernels, contract(): pl.pallas_call(functools.partial(contract_kernel, sizes, wide, len(left),...  5.93 us
    pallas_call x1, Pallas kernels, prepare(): pl.pallas_call(functools.partial(prepare_kernel, blocks, advect_count, pe...  2.44 us
    pallas_call x1, Pallas kernels, finish(): pl.pallas_call(functools.partial(finish_kernel, advect_count, per_block,...  2.42 us
    unnamed x16, local copies, waits for them, and re-layouts  2.09 us
    pallas_call x1, Pallas kernels, begin(): pl.pallas_call(functools.partial(begin_kernel, min(columns, 256)), in_spe...  1.81 us
  transfers between devices with their start and end apart: 17, of which 9 were waited for; matrix products, arithmetic and copies ran while one was open for 0% of the time, Pallas kernels for 25%

profile of v7, /device:TPU:0, one launch (start us, length us, event | category | flops | bytes accessed | tf_op | source)
XLA Modules:
  0.0 71.1 jit_solution(15521307357406516571)
XLA Ops:
  0.6 0.0 copy-start.5
  0.6 0.0 copy-start
  0.7 1.4 %copy-done = bf16[3,256,4,2,128]{4,3,2,1,0:T(2,128)(2,1)S(1)} copy-done((bf16[3,256,4,2,128]{4,3,2,1,0:T(2,128)(2,1)S(1)}, bf16[3,256,4,2,128]{4,3,2,1,0:T(2,128)(2,1)}, u32[]{:S(2)}) %copy-start) | copy-done | bytes 1572888
  2.1 0.0 copy-start.4
  2.1 0.7 copy-done.4
  2.7 0.0 copy-start.3
  2.7 1.2 %lead.1 = (bf16[272,1536]{1,0:T(8,128)(2,1)S(1)}, bf16[3,256,8,128]{3,2,1,0:T(8,128)(2,1)S(1)}) custom-call(s32[8]{0:T(128)S(1)} %copy-done.4, bf16[3,256,8,128]{3,2,1,0:T(8,128)(2,1)S(1)} %bitcast.12), custom_call_target="tpu_custom_call" | custom-call | flops 1 | bytes 1 | tf_op jit(solution)/shard_map/lead/pallas_call | solution.py:61
  3.9 3.0 %collective-permute-start.1 = (bf16[272,1536]{1,0:T(8,128)(2,1)S(1)}, bf16[272,1536]{1,0:T(8,128)(2,1)S(1)}, u32[]{:S(2)}, u32[]{:S(2)}) collective-permute-start(bf16[272,1536]{1,0:T(8,128)(2,1)S(1)} %get-tuple-element.47.after_ref.refs_0_), channel_id=1, source_target_pairs={{0,1},{1,0},{2,3},{3,2},{4,5},{5,4},{6,7},{7,6},{8,9},{9,8},{10,11... | collective-permute-start | bytes 2506760 | tf_op jit(solution)/shard_map/ppermute | solution.py:290
  7.0 0.5 edge.2.after_ref.over_ref.here_ref.refs_1_
  7.5 1.5 %collective-permute-start = (bf16[256,1536]{1,0:T(8,128)(2,1)S(1)}, bf16[256,1536]{1,0:T(8,128)(2,1)S(1)}, u32[]{:S(2)}, u32[]{:S(2)}) collective-permute-start(bf16[256,1536]{1,0:T(8,128)(2,1)S(1)} %edge.2.after_ref.over_ref.here_ref.refs_1_), channel_id=1, source_target_pairs={{0,2},{2,4},{4,6},{6,8},{8,10},{10,12},{12,14},{14,16},{16,18},{18... | collective-permute-start | bytes 2359304 | tf_op jit(solution)/shard_map/ppermute | solution.py:454
  9.0 0.5 edge.3.after_ref.here_ref.under_ref.refs_0_
  9.5 1.3 %collective-permute-start.2 = (bf16[256,1536]{1,0:T(8,128)(2,1)S(1)}, bf16[256,1536]{1,0:T(8,128)(2,1)S(1)}, u32[]{:S(2)}, u32[]{:S(2)}) collective-permute-start(bf16[256,1536]{1,0:T(8,128)(2,1)S(1)} %edge.3.after_ref.here_ref.under_ref.refs_0_), channel_id=1, source_target_pairs={{2,0},{4,2},{6,4},{8,6},{10,8},{12,10},{14,12},{16,14},{18,16},{20... | collective-permute-start | bytes 2359304 | tf_op jit(solution)/shard_map/ppermute | solution.py:455
  10.8 0.4 collective-permute-start.4
  11.2 0.0 copy-done.5
  11.2 0.0 copy-done.3
  11.2 0.5 weights.1.weight_ref
  11.7 0.0 collective-permute-done.under_ref
  11.8 14.6 %collective-permute-done.1.refs_1_.left_ref = bf16[272,1536]{1,0:T(8,128)(2,1)S(1)} collective-permute-done((bf16[272,1536]{1,0:T(8,128)(2,1)S(1)}, bf16[272,1536]{1,0:T(8,128)(2,1)S(1)}, u32[]{:S(2)}, u32[]{:S(2)}) %collective-permute-start.1) | collective-permute-done | bytes 835616 | tf_op jit(solution)/shard_map/ppermute | solution.py:290
  26.4 3.0 %advected.2 = bf16[8,256,1536]{2,1,0:T(8,128)(2,1)S(1)} custom-call(f32[8,128]{1,0:T(8,128)S(1)} %weights.1.weight_ref, bf16[256,1536]{1,0:T(8,128)(2,1)S(1)} %edge.3.after_ref.here_ref.under_ref.refs_0_, bf16[256,1536]{1,0:T(8,128)(2,1)S(1)} %collective-permute-done.under_ref, bf16[256,1536]{1,0:T(8,128)(2,1)S(1)} %edge.2.after_ref.over_ref.here_ref.refs_1_, ...), custom_call_target="tpu_custom_call" | custom-call | flops 1 | bytes 1 | tf_op jit(solution)/shard_map/advected/pallas_call | solution.py:171
  29.4 0.0 collective-permute-done.2.over_ref
  29.5 3.0 %advected.3 = bf16[8,256,1536]{2,1,0:T(8,128)(2,1)S(1)} custom-call(f32[8,128]{1,0:T(8,128)S(1)} %weights.1.weight_ref, bf16[256,1536]{1,0:T(8,128)(2,1)S(1)} %edge.2.after_ref.over_ref.here_ref.refs_1_, bf16[256,1536]{1,0:T(8,128)(2,1)S(1)} %edge.3.after_ref.here_ref.under_ref.refs_0_, bf16[256,1536]{1,0:T(8,128)(2,1)S(1)} %collective-permute-done.2.over_ref, ...), custom_call_target="tpu_custom_call" | custom-call | flops 1 | bytes 1 | tf_op jit(solution)/shard_map/advected/pallas_call | solution.py:171
  32.5 3.8 %contract.2 = (f32[8,16,2048]{2,1,0:T(8,128)S(1)}, bf16[8,16,2048]{2,1,0:T(8,128)(2,1)S(1)}) custom-call(bf16[256,1536]{1,0:T(8,128)(2,1)S(1)} %edge.3.after_ref.here_ref.under_ref.refs_0_, bf16[256,1536]{1,0:T(8,128)(2,1)S(1)} %edge.2.after_ref.over_ref.here_ref.refs_1_, bf16[2048,1536]{1,0:T(8,128)(2,1)S(1)} %bitcast.6, bf16[2048,1536]{1,0:T(8,128)(2,1)S(1)} %bitcast.8), custom_call_target="tpu_custom_call" | custom-call | flops 1 | bytes 1 | tf_op jit(solution)/shard_map/contract/pallas_call | solution.py:241
  36.3 2.0 %collective-permute-start.3 = (bf16[8,16,2048]{2,1,0:T(8,128)(2,1)S(1)}, bf16[8,16,2048]{2,1,0:T(8,128)(2,1)S(1)}, u32[]{:S(2)}, u32[]{:S(2)}) collective-permute-start(bf16[8,16,2048]{2,1,0:T(8,128)(2,1)S(1)} %get-tuple-element.52), channel_id=1, source_target_pairs={{0,2},{2,0},{4,6},{6,4},{8,10},{10,8},{12,14},{14,12},{16,18},{18,... | collective-permute-start | bytes 1572872 | tf_op jit(solution)/shard_map/ppermute | solution.py:290
  38.3 0.0 slice-start
  38.3 1.8 %begin.1.refs_2_ = f32[256,2048]{1,0:T(8,128)S(1)} custom-call(bf16[272,1536]{1,0:T(8,128)(2,1)S(1)} %collective-permute-done.1.refs_1_.left_ref, bf16[2048,1536]{1,0:T(8,128)(2,1)S(1)} %bitcast.9), custom_call_target="tpu_custom_call" | custom-call | flops 1 | bytes 1 | tf_op jit(solution)/shard_map/begin/pallas_call | solution.py:201
  40.1 0.0 collective-permute-done.3.refs_1_
  40.2 0.1 fold.6
  40.3 0.0 slice-start.1
  40.3 0.0 copy-start.1
  40.3 0.0 copy-start.2
  40.3 2.5 %collective-permute-start.5 = (bf16[4,16,2048]{2,1,0:T(8,128)(2,1)S(1)}, bf16[4,16,2048]{2,1,0:T(8,128)(2,1)S(1)}, u32[]{:S(2)}, u32[]{:S(2)}) collective-permute-start(bf16[4,16,2048]{2,1,0:T(8,128)(2,1)S(1)} %get-tuple-element.58), channel_id=1, source_target_pairs={{0,4},{2,6},{4,0},{6,2},{8,12},{10,14},{12,8},{14,10},{16,20},{18,... | collective-permute-start | bytes 786440 | tf_op jit(solution)/shard_map/ppermute | solution.py:290
  42.8 0.0 collective-permute-done.4.refs_0_
  42.8 2.1 %contract.3 = (f32[8,16,2048]{2,1,0:T(8,128)S(1)}, bf16[8,16,512]{2,1,0:T(8,128)(2,1)S(1)}, bf16[8,16,512]{2,1,0:T(8,128)(2,1)S(1)}, bf16[8,16,512]{2,1,0:T(8,128)(2,1)S(1)}, bf16[8,16,512]{2,1,0:T(8,128)(2,1)S(1)}) custom-call(bf16[256,1536]{1,0:T(8,128)(2,1)S(1)} %collective-permute-done.4.refs_0_, bf16[2048,1536]{1,0:T(8,128)(2,1)S(1)} %bitcast.7, ...), custom_call_target="tpu_custom_call" | custom-call | flops 1 | bytes 1 | tf_op jit(solution)/shard_map/contract/pallas_call | solution.py:241
  44.9 0.2 collective-permute-start.6
  45.2 0.3 collective-permute-start.7
  45.5 0.2 collective-permute-start.8
  45.7 0.3 collective-permute-start.9
  46.0 0.3 collective-permute-done.6.refs_1_
  46.4 0.2 collective-permute-done.7.refs_2_
  46.5 0.3 collective-permute-done.8.refs_3_
  46.9 0.2 collective-permute-done.9.refs_4_
  47.0 0.1 fold.8
  47.1 2.6 %collective-permute-done.5.refs_1_ = bf16[4,16,2048]{2,1,0:T(8,128)(2,1)S(1)} collective-permute-done((bf16[4,16,2048]{2,1,0:T(8,128)(2,1)S(1)}, bf16[4,16,2048]{2,1,0:T(8,128)(2,1)S(1)}, u32[]{:S(2)}, u32[]{:S(2)}) %collective-permute-start.5) | collective-permute-done | bytes 262176 | tf_op jit(solution)/shard_map/ppermute | solution.py:290
  49.8 1.8 %collective-permute-start.12 = (bf16[4,16,2048]{2,1,0:T(8,128)(2,1)S(1)}, bf16[4,16,2048]{2,1,0:T(8,128)(2,1)S(1)}, u32[]{:S(2)}, u32[]{:S(2)}) collective-permute-start(bf16[4,16,2048]{2,1,0:T(8,128)(2,1)S(1)} %get-tuple-element.75), channel_id=1, source_target_pairs={{0,4},{2,6},{4,0},{6,2},{8,12},{10,14},{12,8},{14,10},{16,20},{18,... | collective-permute-start | bytes 786440 | tf_op jit(solution)/shard_map/ppermute | solution.py:290
  51.6 1.6 %collective-permute-start.10 = (bf16[2,16,2048]{2,1,0:T(8,128)(2,1)S(1)}, bf16[2,16,2048]{2,1,0:T(8,128)(2,1)S(1)}, u32[]{:S(2)}, u32[]{:S(2)}) collective-permute-start(bf16[2,16,2048]{2,1,0:T(8,128)(2,1)S(1)} %get-tuple-element.71), channel_id=1, source_target_pairs={{0,8},{2,10},{4,12},{6,14},{8,0},{10,2},{12,4},{14,6},{16,24},{18,... | collective-permute-start | bytes 393224 | tf_op jit(solution)/shard_map/ppermute | solution.py:290
  53.1 3.4 %collective-permute-done.10.refs_1_ = bf16[2,16,2048]{2,1,0:T(8,128)(2,1)S(1)} collective-permute-done((bf16[2,16,2048]{2,1,0:T(8,128)(2,1)S(1)}, bf16[2,16,2048]{2,1,0:T(8,128)(2,1)S(1)}, u32[]{:S(2)}, u32[]{:S(2)}) %collective-permute-start.10) | collective-permute-done | bytes 131104 | tf_op jit(solution)/shard_map/ppermute | solution.py:290
  56.6 2.7 %collective-permute-start.11 = (bf16[1,16,2048]{2,1,0:T(8,128)(2,1)S(1)}, bf16[1,16,2048]{2,1,0:T(8,128)(2,1)S(1)}, u32[]{:S(2)}, u32[]{:S(2)}) collective-permute-start(bf16[1,16,2048]{2,1,0:T(8,128)(2,1)S(1)} %get-tuple-element.73), channel_id=1, source_target_pairs={{0,16},{2,18},{4,20},{6,22},{8,24},{10,26},{12,28},{14,30},{16,0},... | collective-permute-start | bytes 196616 | tf_op jit(solution)/shard_map/ppermute | solution.py:290
  59.2 0.0 collective-permute-done.12.refs_1_
  59.3 0.6 collective-permute-start.13
  59.9 1.2 %collective-permute-start.14 = (bf16[1,16,2048]{2,1,0:T(8,128)(2,1)S(1)}, bf16[1,16,2048]{2,1,0:T(8,128)(2,1)S(1)}, u32[]{:S(2)}, u32[]{:S(2)}) collective-permute-start(bf16[1,16,2048]{2,1,0:T(8,128)(2,1)S(1)} %get-tuple-element.83), channel_id=1, source_target_pairs={{0,9},{1,8},{2,11},{3,10},{4,13},{5,12},{6,15},{7,14},{8,17},{9,16... | collective-permute-start | bytes 196616 | tf_op jit(solution)/shard_map/ppermute | solution.py:290
  61.1 1.6 %collective-permute-start.15 = (bf16[1,16,2048]{2,1,0:T(8,128)(2,1)S(1)}, bf16[1,16,2048]{2,1,0:T(8,128)(2,1)S(1)}, u32[]{:S(2)}, u32[]{:S(2)}) collective-permute-start(bf16[1,16,2048]{2,1,0:T(8,128)(2,1)S(1)} %get-tuple-element.84), channel_id=1, source_target_pairs={{0,17},{1,16},{2,19},{3,18},{4,21},{5,20},{6,23},{7,22},{8,25},{9,... | collective-permute-start | bytes 196616 | tf_op jit(solution)/shard_map/ppermute | solution.py:290
  62.7 3.3 %collective-permute-start.16 = (bf16[1,16,2048]{2,1,0:T(8,128)(2,1)S(1)}, bf16[1,16,2048]{2,1,0:T(8,128)(2,1)S(1)}, u32[]{:S(2)}, u32[]{:S(2)}) collective-permute-start(bf16[1,16,2048]{2,1,0:T(8,128)(2,1)S(1)} %get-tuple-element.85), channel_id=1, source_target_pairs={{0,25},{1,24},{2,27},{3,26},{4,29},{5,28},{6,31},{7,30},{8,1},{9,0... | collective-permute-start | bytes 196616 | tf_op jit(solution)/shard_map/ppermute | solution.py:290
  65.9 0.0 collective-permute-done.11.refs_1_
  65.9 0.0 slice-done
  66.0 0.0 slice-done.1
  66.0 0.0 copy-done.1
  66.0 0.0 copy-done.2
  66.0 2.4 %prepare.1 = (bf16[2048,1024]{1,0:T(8,128)(2,1)S(1)}, bf16[2048,1024]{1,0:T(8,128)(2,1)S(1)}, f32[16,2048]{1,0:T(8,128)S(1)}) custom-call(s32[1,2048]{1,0:T(1,128)S(1)} %bitcast.13, s32[1,2048]{1,0:T(1,128)S(1)} %bitcast.15, f32[1,16,2048]{2,1,0:T(8,128)S(1)} %fold.10.own_ref.refs_0_, f32[2048,1024]{1,0:T(8,128)S(1)} %bitcast.11), custom_call_target="tpu_custom_call" | custom-call | flops 8388608 | bytes 16777216 | tf_op jit(solution)/shard_map/prepare/pallas_call | solution.py:351
  68.4 0.0 collective-permute-done.13.refs_1_
  68.5 0.0 collective-permute-done.14.refs_2_
  68.5 0.1 collective-permute-done.15.refs_3_
  68.6 0.1 collective-permute-done.16.refs_4_
  68.6 2.4 %finish.1 = (f32[16,8,512]{2,1,0:T(8,128)}, f32[16,1024]{1,0:T(8,128)}) custom-call(s32[1,2048]{1,0:T(1,128)S(1)} %bitcast.14, s32[1,2048]{1,0:T(1,128)S(1)} %bitcast.16, f32[1,16,2048]{2,1,0:T(8,128)S(1)} %fold.10.own_ref.refs_0_, bf16[1,16,2048]{2,1,0:T(8,128)(2,1)S(1)} %collective-permute-done.13.refs_1_, ...), custom_call_target="tpu_custom_call" | custom-call | flops 1 | bytes 1 | tf_op jit(solution)/shard_map/finish/pallas_call | solution.py:419
  (5 shorter events, 0.1 us)
Async XLA Ops:
  0.6 10.6 %copy-start.5 = (f32[8]{0:T(128)S(1)}, f32[8]{0:T(128)}, u32[]{:S(2)}) copy-start(f32[8]{0:T(128)} %volume_ref.1) | copy-start | bytes 100
  0.6 1.4 %copy-start = (bf16[3,256,4,2,128]{4,3,2,1,0:T(2,128)(2,1)S(1)}, bf16[3,256,4,2,128]{4,3,2,1,0:T(2,128)(2,1)}, u32[]{:S(2)}) copy-start(bf16[3,256,4,2,128]{4,3,2,1,0:T(2,128)(2,1)} %param.7) | copy-start | bytes 4718596
  2.1 0.7 copy-start.4
  2.7 8.5 %copy-start.3 = (s32[4,2,128]{2,1,0:T(2,128)S(1)}, s32[4,2,128]{2,1,0:T(2,128)}, u32[]{:S(2)}) copy-start(s32[4,2,128]{2,1,0:T(2,128)} %param.8) | copy-start | bytes 12292
  3.9 22.5 %collective-permute-start.1 = (bf16[272,1536]{1,0:T(8,128)(2,1)S(1)}, bf16[272,1536]{1,0:T(8,128)(2,1)S(1)}, u32[]{:S(2)}, u32[]{:S(2)}) collective-permute-start(bf16[272,1536]{1,0:T(8,128)(2,1)S(1)} %get-tuple-element.47.after_ref.refs_0_), channel_id=1, source_target_pairs={{0,1},{1,0},{2,3},{3,2},{4,5},{5,4},{6,7},{7,6},{8,9},{9,8},{10,11... | collective-permute-start | bytes 2506760 | tf_op jit(solution)/shard_map/ppermute | solution.py:290
  7.5 4.3 %collective-permute-start = (bf16[256,1536]{1,0:T(8,128)(2,1)S(1)}, bf16[256,1536]{1,0:T(8,128)(2,1)S(1)}, u32[]{:S(2)}, u32[]{:S(2)}) collective-permute-start(bf16[256,1536]{1,0:T(8,128)(2,1)S(1)} %edge.2.after_ref.over_ref.here_ref.refs_1_), channel_id=1, source_target_pairs={{0,2},{2,4},{4,6},{6,8},{8,10},{10,12},{12,14},{14,16},{16,18},{18... | collective-permute-start | bytes 2359304 | tf_op jit(solution)/shard_map/ppermute | solution.py:454
  9.5 19.9 %collective-permute-start.2 = (bf16[256,1536]{1,0:T(8,128)(2,1)S(1)}, bf16[256,1536]{1,0:T(8,128)(2,1)S(1)}, u32[]{:S(2)}, u32[]{:S(2)}) collective-permute-start(bf16[256,1536]{1,0:T(8,128)(2,1)S(1)} %edge.3.after_ref.here_ref.under_ref.refs_0_), channel_id=1, source_target_pairs={{2,0},{4,2},{6,4},{8,6},{10,8},{12,10},{14,12},{16,14},{18,16},{20... | collective-permute-start | bytes 2359304 | tf_op jit(solution)/shard_map/ppermute | solution.py:455
  10.8 32.0 %collective-permute-start.4 = (bf16[256,1536]{1,0:T(8,128)(2,1)S(1)}, bf16[256,1536]{1,0:T(8,128)(2,1)S(1)}, u32[]{:S(2)}, u32[]{:S(2)}) collective-permute-start(bf16[256,1536]{1,0:T(8,128)(2,1)S(1)} %edge.3.after_ref.here_ref.under_ref.refs_0_), channel_id=1, source_target_pairs={{0,1},{1,0},{2,3},{3,2},{4,5},{5,4},{6,7},{7,6},{8,9},{9,8},{10,11... | collective-permute-start | bytes 2359304 | tf_op jit(solution)/shard_map/ppermute | solution.py:290
  36.3 3.9 %collective-permute-start.3 = (bf16[8,16,2048]{2,1,0:T(8,128)(2,1)S(1)}, bf16[8,16,2048]{2,1,0:T(8,128)(2,1)S(1)}, u32[]{:S(2)}, u32[]{:S(2)}) collective-permute-start(bf16[8,16,2048]{2,1,0:T(8,128)(2,1)S(1)} %get-tuple-element.52), channel_id=1, source_target_pairs={{0,2},{2,0},{4,6},{6,4},{8,10},{10,8},{12,14},{14,12},{16,18},{18,... | collective-permute-start | bytes 1572872 | tf_op jit(solution)/shard_map/ppermute | solution.py:290
  38.3 27.6 %slice-start = ((s8[8388608]{0:T(1024)(128)(4,1)}), s8[4194304]{0:T(1024)(128)(4,1)S(1)}, s32[]{:S(2)}) async-start(s8[8388608]{0:T(1024)(128)(4,1)} %bitcast.10), calls=%async_computation | async-start | bytes 8388608
  40.3 25.7 %slice-start.1 = ((s8[8388608]{0:T(1024)(128)(4,1)}), s8[4194304]{0:T(1024)(128)(4,1)S(1)}, s32[]{:S(2)}) async-start(s8[8388608]{0:T(1024)(128)(4,1)} %bitcast.10), calls=%async_computation.1 | async-start | bytes 8388608
  40.3 25.7 %copy-start.1 = (s32[2048]{0:T(1024)S(1)}, s32[2048]{0:T(1024)}, u32[]{:S(2)}) copy-start(s32[2048]{0:T(1024)} %param.11) | copy-start | bytes 24580
  40.3 25.7 %copy-start.2 = (s32[2048]{0:T(1024)S(1)}, s32[2048]{0:T(1024)}, u32[]{:S(2)}) copy-start(s32[2048]{0:T(1024)} %param.12) | copy-start | bytes 24580
  40.3 9.4 %collective-permute-start.5 = (bf16[4,16,2048]{2,1,0:T(8,128)(2,1)S(1)}, bf16[4,16,2048]{2,1,0:T(8,128)(2,1)S(1)}, u32[]{:S(2)}, u32[]{:S(2)}) collective-permute-start(bf16[4,16,2048]{2,1,0:T(8,128)(2,1)S(1)} %get-tuple-element.58), channel_id=1, source_target_pairs={{0,4},{2,6},{4,0},{6,2},{8,12},{10,14},{12,8},{14,10},{16,20},{18,... | collective-permute-start | bytes 786440 | tf_op jit(solution)/shard_map/ppermute | solution.py:290
  44.9 1.4 %collective-permute-start.6 = (bf16[8,16,512]{2,1,0:T(8,128)(2,1)S(1)}, bf16[8,16,512]{2,1,0:T(8,128)(2,1)S(1)}, u32[]{:S(2)}, u32[]{:S(2)}) collective-permute-start(bf16[8,16,512]{2,1,0:T(8,128)(2,1)S(1)} %get-tuple-element.64), channel_id=1, source_target_pairs={{0,2},{2,0},{4,6},{6,4},{8,10},{10,8},{12,14},{14,12},{16,18},{18,... | collective-permute-start | bytes 393224 | tf_op jit(solution)/shard_map/ppermute | solution.py:290
  45.2 1.4 %collective-permute-start.7 = (bf16[8,16,512]{2,1,0:T(8,128)(2,1)S(1)}, bf16[8,16,512]{2,1,0:T(8,128)(2,1)S(1)}, u32[]{:S(2)}, u32[]{:S(2)}) collective-permute-start(bf16[8,16,512]{2,1,0:T(8,128)(2,1)S(1)} %get-tuple-element.65), channel_id=1, source_target_pairs={{0,2},{2,0},{4,6},{6,4},{8,10},{10,8},{12,14},{14,12},{16,18},{18,... | collective-permute-start | bytes 393224 | tf_op jit(solution)/shard_map/ppermute | solution.py:290
  45.5 1.3 %collective-permute-start.8 = (bf16[8,16,512]{2,1,0:T(8,128)(2,1)S(1)}, bf16[8,16,512]{2,1,0:T(8,128)(2,1)S(1)}, u32[]{:S(2)}, u32[]{:S(2)}) collective-permute-start(bf16[8,16,512]{2,1,0:T(8,128)(2,1)S(1)} %get-tuple-element.66), channel_id=1, source_target_pairs={{0,2},{2,0},{4,6},{6,4},{8,10},{10,8},{12,14},{14,12},{16,18},{18,... | collective-permute-start | bytes 393224 | tf_op jit(solution)/shard_map/ppermute | solution.py:290
  45.7 1.4 %collective-permute-start.9 = (bf16[8,16,512]{2,1,0:T(8,128)(2,1)S(1)}, bf16[8,16,512]{2,1,0:T(8,128)(2,1)S(1)}, u32[]{:S(2)}, u32[]{:S(2)}) collective-permute-start(bf16[8,16,512]{2,1,0:T(8,128)(2,1)S(1)} %get-tuple-element.67), channel_id=1, source_target_pairs={{0,2},{2,0},{4,6},{6,4},{8,10},{10,8},{12,14},{14,12},{16,18},{18,... | collective-permute-start | bytes 393224 | tf_op jit(solution)/shard_map/ppermute | solution.py:290
  49.8 9.5 %collective-permute-start.12 = (bf16[4,16,2048]{2,1,0:T(8,128)(2,1)S(1)}, bf16[4,16,2048]{2,1,0:T(8,128)(2,1)S(1)}, u32[]{:S(2)}, u32[]{:S(2)}) collective-permute-start(bf16[4,16,2048]{2,1,0:T(8,128)(2,1)S(1)} %get-tuple-element.75), channel_id=1, source_target_pairs={{0,4},{2,6},{4,0},{6,2},{8,12},{10,14},{12,8},{14,10},{16,20},{18,... | collective-permute-start | bytes 786440 | tf_op jit(solution)/shard_map/ppermute | solution.py:290
  51.6 5.0 %collective-permute-start.10 = (bf16[2,16,2048]{2,1,0:T(8,128)(2,1)S(1)}, bf16[2,16,2048]{2,1,0:T(8,128)(2,1)S(1)}, u32[]{:S(2)}, u32[]{:S(2)}) collective-permute-start(bf16[2,16,2048]{2,1,0:T(8,128)(2,1)S(1)} %get-tuple-element.71), channel_id=1, source_target_pairs={{0,8},{2,10},{4,12},{6,14},{8,0},{10,2},{12,4},{14,6},{16,24},{18,... | collective-permute-start | bytes 393224 | tf_op jit(solution)/shard_map/ppermute | solution.py:290
  56.6 9.4 %collective-permute-start.11 = (bf16[1,16,2048]{2,1,0:T(8,128)(2,1)S(1)}, bf16[1,16,2048]{2,1,0:T(8,128)(2,1)S(1)}, u32[]{:S(2)}, u32[]{:S(2)}) collective-permute-start(bf16[1,16,2048]{2,1,0:T(8,128)(2,1)S(1)} %get-tuple-element.73), channel_id=1, source_target_pairs={{0,16},{2,18},{4,20},{6,22},{8,24},{10,26},{12,28},{14,30},{16,0},... | collective-permute-start | bytes 196616 | tf_op jit(solution)/shard_map/ppermute | solution.py:290
  59.3 9.2 %collective-permute-start.13 = (bf16[1,16,2048]{2,1,0:T(8,128)(2,1)S(1)}, bf16[1,16,2048]{2,1,0:T(8,128)(2,1)S(1)}, u32[]{:S(2)}, u32[]{:S(2)}) collective-permute-start(bf16[1,16,2048]{2,1,0:T(8,128)(2,1)S(1)} %get-tuple-element.82), channel_id=1, source_target_pairs={{0,1},{1,0},{2,3},{3,2},{4,5},{5,4},{6,7},{7,6},{8,9},{9,8},{10,11... | collective-permute-start | bytes 196616 | tf_op jit(solution)/shard_map/ppermute | solution.py:290
  59.9 8.6 %collective-permute-start.14 = (bf16[1,16,2048]{2,1,0:T(8,128)(2,1)S(1)}, bf16[1,16,2048]{2,1,0:T(8,128)(2,1)S(1)}, u32[]{:S(2)}, u32[]{:S(2)}) collective-permute-start(bf16[1,16,2048]{2,1,0:T(8,128)(2,1)S(1)} %get-tuple-element.83), channel_id=1, source_target_pairs={{0,9},{1,8},{2,11},{3,10},{4,13},{5,12},{6,15},{7,14},{8,17},{9,16... | collective-permute-start | bytes 196616 | tf_op jit(solution)/shard_map/ppermute | solution.py:290
  61.1 7.5 %collective-permute-start.15 = (bf16[1,16,2048]{2,1,0:T(8,128)(2,1)S(1)}, bf16[1,16,2048]{2,1,0:T(8,128)(2,1)S(1)}, u32[]{:S(2)}, u32[]{:S(2)}) collective-permute-start(bf16[1,16,2048]{2,1,0:T(8,128)(2,1)S(1)} %get-tuple-element.84), channel_id=1, source_target_pairs={{0,17},{1,16},{2,19},{3,18},{4,21},{5,20},{6,23},{7,22},{8,25},{9,... | collective-permute-start | bytes 196616 | tf_op jit(solution)/shard_map/ppermute | solution.py:290
  62.7 6.0 %collective-permute-start.16 = (bf16[1,16,2048]{2,1,0:T(8,128)(2,1)S(1)}, bf16[1,16,2048]{2,1,0:T(8,128)(2,1)S(1)}, u32[]{:S(2)}, u32[]{:S(2)}) collective-permute-start(bf16[1,16,2048]{2,1,0:T(8,128)(2,1)S(1)} %get-tuple-element.85), channel_id=1, source_target_pairs={{0,25},{1,24},{2,27},{3,26},{4,29},{5,28},{6,31},{7,30},{8,1},{9,0... | collective-permute-start | bytes 196616 | tf_op jit(solution)/shard_map/ppermute | solution.py:290

commit v8 on v7

--- a/solution.py
+++ b/solution.py
@@ -474,7 +474,6 @@
     mine[0], ahead = lax.optimization_barrier((mine[0], ahead))
     begun = begin(ahead[0], right[-1], mode_block)
     mine = summed(mine, 0, early, pairwise)
-    mine, begun = lax.optimization_barrier((mine, begun))
     mine[0], arrived = lax.optimization_barrier((mine[0], arrived))
     mine = summed(mine, early, early + 1, pairwise)
     result = []

time: 71.2 us -> 71 us (level)
  transfers between devices with their start and end apart: 17 -> 17, of which waited for: 9 -> 9; matrix products, arithmetic and copies ran while one was open for 0% -> 0% of each run, Pallas kernels for 25% -> 26%
where the time goes in v8:
time: 71 us; the launch traced here: 70.8 us
  starting transfers between devices  24.9 us (35%)
  Pallas kernels  21.8 us (31%)
  waiting for transfers between devices  21.2 us (30%)
  local copies, waits for them, and re-layouts  2.09 us (3%)
  between operations  0.87 us (1%)
    ppermute x15, starting transfers between devices, shifted(): return lax.ppermute(block, (axis, 'mode') if turn else axis, route)  22.1 us
    ppermute x15, waiting for transfers between devices, shifted(): return lax.ppermute(block, (axis, 'mode') if turn else axis, route)  21.2 us
    pallas_call x2, Pallas kernels, advected(): pl.pallas_call(functools.partial(advected_kernel, comps, planes, rows_y,...  6.09 us
    pallas_call x2, Pallas kernels, contract(): pl.pallas_call(functools.partial(contract_kernel, sizes, wide, len(left),...  5.94 us
    pallas_call x1, Pallas kernels, prepare(): pl.pallas_call(functools.partial(prepare_kernel, blocks, advect_count, pe...  2.44 us
    pallas_call x1, Pallas kernels, finish(): pl.pallas_call(functools.partial(finish_kernel, advect_count, per_block,...  2.42 us
    unnamed x16, local copies, waits for them, and re-layouts  2.09 us
    pallas_call x1, Pallas kernels, begin(): pl.pallas_call(functools.partial(begin_kernel, min(columns, 256)), in_spe...  1.81 us
  transfers between devices with their start and end apart: 17, of which 9 were waited for; matrix products, arithmetic and copies ran while one was open for 0% of the time, Pallas kernels for 26%

profile of v8, /device:TPU:0, one launch (start us, length us, event | category | flops | bytes accessed | tf_op | source)
XLA Modules:
  0.0 70.8 jit_solution(8096992572024361581)
XLA Ops:
  0.6 0.0 copy-start.5
  0.6 0.0 copy-start
  0.7 1.4 %copy-done = bf16[3,256,4,2,128]{4,3,2,1,0:T(2,128)(2,1)S(1)} copy-done((bf16[3,256,4,2,128]{4,3,2,1,0:T(2,128)(2,1)S(1)}, bf16[3,256,4,2,128]{4,3,2,1,0:T(2,128)(2,1)}, u32[]{:S(2)}) %copy-start) | copy-done | bytes 1572888
  2.1 0.0 copy-start.4
  2.1 0.7 copy-done.4
  2.7 0.0 copy-start.3
  2.7 1.2 %lead.1 = (bf16[272,1536]{1,0:T(8,128)(2,1)S(1)}, bf16[3,256,8,128]{3,2,1,0:T(8,128)(2,1)S(1)}) custom-call(s32[8]{0:T(128)S(1)} %copy-done.4, bf16[3,256,8,128]{3,2,1,0:T(8,128)(2,1)S(1)} %bitcast.12), custom_call_target="tpu_custom_call" | custom-call | flops 1 | bytes 1 | tf_op jit(solution)/shard_map/lead/pallas_call | solution.py:61
  3.9 3.0 %collective-permute-start.1 = (bf16[272,1536]{1,0:T(8,128)(2,1)S(1)}, bf16[272,1536]{1,0:T(8,128)(2,1)S(1)}, u32[]{:S(2)}, u32[]{:S(2)}) collective-permute-start(bf16[272,1536]{1,0:T(8,128)(2,1)S(1)} %get-tuple-element.44.after_ref.refs_0_), channel_id=1, source_target_pairs={{0,1},{1,0},{2,3},{3,2},{4,5},{5,4},{6,7},{7,6},{8,9},{9,8},{10,11... | collective-permute-start | bytes 2506760 | tf_op jit(solution)/shard_map/ppermute | solution.py:290
  7.0 0.5 edge.2.after_ref.over_ref.here_ref.refs_1_
  7.5 1.5 %collective-permute-start = (bf16[256,1536]{1,0:T(8,128)(2,1)S(1)}, bf16[256,1536]{1,0:T(8,128)(2,1)S(1)}, u32[]{:S(2)}, u32[]{:S(2)}) collective-permute-start(bf16[256,1536]{1,0:T(8,128)(2,1)S(1)} %edge.2.after_ref.over_ref.here_ref.refs_1_), channel_id=1, source_target_pairs={{0,2},{2,4},{4,6},{6,8},{8,10},{10,12},{12,14},{14,16},{16,18},{18... | collective-permute-start | bytes 2359304 | tf_op jit(solution)/shard_map/ppermute | solution.py:454
  9.0 0.5 edge.3.after_ref.here_ref.under_ref.refs_0_
  9.5 1.3 %collective-permute-start.2 = (bf16[256,1536]{1,0:T(8,128)(2,1)S(1)}, bf16[256,1536]{1,0:T(8,128)(2,1)S(1)}, u32[]{:S(2)}, u32[]{:S(2)}) collective-permute-start(bf16[256,1536]{1,0:T(8,128)(2,1)S(1)} %edge.3.after_ref.here_ref.under_ref.refs_0_), channel_id=1, source_target_pairs={{2,0},{4,2},{6,4},{8,6},{10,8},{12,10},{14,12},{16,14},{18,16},{20... | collective-permute-start | bytes 2359304 | tf_op jit(solution)/shard_map/ppermute | solution.py:455
  10.8 0.4 collective-permute-start.4
  11.2 0.0 copy-done.5
  11.2 0.0 copy-done.3
  11.2 0.5 weights.1.weight_ref
  11.7 0.0 collective-permute-done.under_ref
  11.8 14.6 %collective-permute-done.1.refs_1_.left_ref = bf16[272,1536]{1,0:T(8,128)(2,1)S(1)} collective-permute-done((bf16[272,1536]{1,0:T(8,128)(2,1)S(1)}, bf16[272,1536]{1,0:T(8,128)(2,1)S(1)}, u32[]{:S(2)}, u32[]{:S(2)}) %collective-permute-start.1) | collective-permute-done | bytes 835616 | tf_op jit(solution)/shard_map/ppermute | solution.py:290
  26.4 3.0 %advected.2 = bf16[8,256,1536]{2,1,0:T(8,128)(2,1)S(1)} custom-call(f32[8,128]{1,0:T(8,128)S(1)} %weights.1.weight_ref, bf16[256,1536]{1,0:T(8,128)(2,1)S(1)} %edge.3.after_ref.here_ref.under_ref.refs_0_, bf16[256,1536]{1,0:T(8,128)(2,1)S(1)} %collective-permute-done.under_ref, bf16[256,1536]{1,0:T(8,128)(2,1)S(1)} %edge.2.after_ref.over_ref.here_ref.refs_1_, ...), custom_call_target="tpu_custom_call" | custom-call | flops 1 | bytes 1 | tf_op jit(solution)/shard_map/advected/pallas_call | solution.py:171
  29.4 0.0 collective-permute-done.2.over_ref
  29.5 3.0 %advected.3 = bf16[8,256,1536]{2,1,0:T(8,128)(2,1)S(1)} custom-call(f32[8,128]{1,0:T(8,128)S(1)} %weights.1.weight_ref, bf16[256,1536]{1,0:T(8,128)(2,1)S(1)} %edge.2.after_ref.over_ref.here_ref.refs_1_, bf16[256,1536]{1,0:T(8,128)(2,1)S(1)} %edge.3.after_ref.here_ref.under_ref.refs_0_, bf16[256,1536]{1,0:T(8,128)(2,1)S(1)} %collective-permute-done.2.over_ref, ...), custom_call_target="tpu_custom_call" | custom-call | flops 1 | bytes 1 | tf_op jit(solution)/shard_map/advected/pallas_call | solution.py:171
  32.5 3.8 %contract.2 = (f32[8,16,2048]{2,1,0:T(8,128)S(1)}, bf16[8,16,2048]{2,1,0:T(8,128)(2,1)S(1)}) custom-call(bf16[256,1536]{1,0:T(8,128)(2,1)S(1)} %edge.3.after_ref.here_ref.under_ref.refs_0_, bf16[256,1536]{1,0:T(8,128)(2,1)S(1)} %edge.2.after_ref.over_ref.here_ref.refs_1_, bf16[2048,1536]{1,0:T(8,128)(2,1)S(1)} %bitcast.6, bf16[2048,1536]{1,0:T(8,128)(2,1)S(1)} %bitcast.8), custom_call_target="tpu_custom_call" | custom-call | flops 1 | bytes 1 | tf_op jit(solution)/shard_map/contract/pallas_call | solution.py:241
  36.3 2.0 %collective-permute-start.3 = (bf16[8,16,2048]{2,1,0:T(8,128)(2,1)S(1)}, bf16[8,16,2048]{2,1,0:T(8,128)(2,1)S(1)}, u32[]{:S(2)}, u32[]{:S(2)}) collective-permute-start(bf16[8,16,2048]{2,1,0:T(8,128)(2,1)S(1)} %get-tuple-element.49), channel_id=1, source_target_pairs={{0,2},{2,0},{4,6},{6,4},{8,10},{10,8},{12,14},{14,12},{16,18},{18,... | collective-permute-start | bytes 1572872 | tf_op jit(solution)/shard_map/ppermute | solution.py:290
  38.3 1.5 %collective-permute-done.3.refs_1_ = bf16[8,16,2048]{2,1,0:T(8,128)(2,1)S(1)} collective-permute-done((bf16[8,16,2048]{2,1,0:T(8,128)(2,1)S(1)}, bf16[8,16,2048]{2,1,0:T(8,128)(2,1)S(1)}, u32[]{:S(2)}, u32[]{:S(2)}) %collective-permute-start.3) | collective-permute-done | bytes 524320 | tf_op jit(solution)/shard_map/ppermute | solution.py:290
  39.9 0.1 fold.6
  40.0 2.8 %collective-permute-start.5 = (bf16[4,16,2048]{2,1,0:T(8,128)(2,1)S(1)}, bf16[4,16,2048]{2,1,0:T(8,128)(2,1)S(1)}, u32[]{:S(2)}, u32[]{:S(2)}) collective-permute-start(bf16[4,16,2048]{2,1,0:T(8,128)(2,1)S(1)} %get-tuple-element.52), channel_id=1, source_target_pairs={{0,4},{2,6},{4,0},{6,2},{8,12},{10,14},{12,8},{14,10},{16,20},{18,... | collective-permute-start | bytes 786440 | tf_op jit(solution)/shard_map/ppermute | solution.py:290
  42.8 0.0 slice-start
  42.8 1.8 %begin.1.refs_2_ = f32[256,2048]{1,0:T(8,128)S(1)} custom-call(bf16[272,1536]{1,0:T(8,128)(2,1)S(1)} %collective-permute-done.1.refs_1_.left_ref, bf16[2048,1536]{1,0:T(8,128)(2,1)S(1)} %bitcast.9), custom_call_target="tpu_custom_call" | custom-call | flops 1 | bytes 1 | tf_op jit(solution)/shard_map/begin/pallas_call | solution.py:201
  44.6 0.0 collective-permute-done.4.refs_0_
  44.6 0.0 slice-start.1
  44.6 0.0 copy-start.1
  44.6 0.0 copy-start.2
  44.6 2.2 %contract.3 = (f32[8,16,2048]{2,1,0:T(8,128)S(1)}, bf16[8,16,512]{2,1,0:T(8,128)(2,1)S(1)}, bf16[8,16,512]{2,1,0:T(8,128)(2,1)S(1)}, bf16[8,16,512]{2,1,0:T(8,128)(2,1)S(1)}, bf16[8,16,512]{2,1,0:T(8,128)(2,1)S(1)}) custom-call(bf16[256,1536]{1,0:T(8,128)(2,1)S(1)} %collective-permute-done.4.refs_0_, bf16[2048,1536]{1,0:T(8,128)(2,1)S(1)} %bitcast.7, ...), custom_call_target="tpu_custom_call" | custom-call | flops 1 | bytes 1 | tf_op jit(solution)/shard_map/contract/pallas_call | solution.py:241
  46.8 0.1 collective-permute-start.6
  46.9 0.5 collective-permute-start.7
  47.4 0.1 collective-permute-start.8
  47.4 0.4 collective-permute-start.9
  47.9 0.3 collective-permute-done.6.refs_1_
  48.2 0.2 collective-permute-done.7.refs_2_
  48.4 0.3 collective-permute-done.8.refs_3_
  48.7 0.2 collective-permute-done.9.refs_4_
  48.9 0.1 fold.8
  49.0 0.4 collective-permute-done.5.refs_1_
  49.4 0.1 fold.7
  49.4 1.8 %collective-permute-start.12 = (bf16[4,16,2048]{2,1,0:T(8,128)(2,1)S(1)}, bf16[4,16,2048]{2,1,0:T(8,128)(2,1)S(1)}, u32[]{:S(2)}, u32[]{:S(2)}) collective-permute-start(bf16[4,16,2048]{2,1,0:T(8,128)(2,1)S(1)} %get-tuple-element.69), channel_id=1, source_target_pairs={{0,4},{2,6},{4,0},{6,2},{8,12},{10,14},{12,8},{14,10},{16,20},{18,... | collective-permute-start | bytes 786440 | tf_op jit(solution)/shard_map/ppermute | solution.py:290
  51.2 1.6 %collective-permute-start.10 = (bf16[2,16,2048]{2,1,0:T(8,128)(2,1)S(1)}, bf16[2,16,2048]{2,1,0:T(8,128)(2,1)S(1)}, u32[]{:S(2)}, u32[]{:S(2)}) collective-permute-start(bf16[2,16,2048]{2,1,0:T(8,128)(2,1)S(1)} %get-tuple-element.65), channel_id=1, source_target_pairs={{0,8},{2,10},{4,12},{6,14},{8,0},{10,2},{12,4},{14,6},{16,24},{18,... | collective-permute-start | bytes 393224 | tf_op jit(solution)/shard_map/ppermute | solution.py:290
  52.8 3.4 %collective-permute-done.10.refs_1_ = bf16[2,16,2048]{2,1,0:T(8,128)(2,1)S(1)} collective-permute-done((bf16[2,16,2048]{2,1,0:T(8,128)(2,1)S(1)}, bf16[2,16,2048]{2,1,0:T(8,128)(2,1)S(1)}, u32[]{:S(2)}, u32[]{:S(2)}) %collective-permute-start.10) | collective-permute-done | bytes 131104 | tf_op jit(solution)/shard_map/ppermute | solution.py:290
  56.2 2.7 %collective-permute-start.11 = (bf16[1,16,2048]{2,1,0:T(8,128)(2,1)S(1)}, bf16[1,16,2048]{2,1,0:T(8,128)(2,1)S(1)}, u32[]{:S(2)}, u32[]{:S(2)}) collective-permute-start(bf16[1,16,2048]{2,1,0:T(8,128)(2,1)S(1)} %get-tuple-element.67), channel_id=1, source_target_pairs={{0,16},{2,18},{4,20},{6,22},{8,24},{10,26},{12,28},{14,30},{16,0},... | collective-permute-start | bytes 196616 | tf_op jit(solution)/shard_map/ppermute | solution.py:290
  58.9 0.0 collective-permute-done.12.refs_1_
  58.9 0.6 collective-permute-start.13
  59.5 1.3 %collective-permute-start.14 = (bf16[1,16,2048]{2,1,0:T(8,128)(2,1)S(1)}, bf16[1,16,2048]{2,1,0:T(8,128)(2,1)S(1)}, u32[]{:S(2)}, u32[]{:S(2)}) collective-permute-start(bf16[1,16,2048]{2,1,0:T(8,128)(2,1)S(1)} %get-tuple-element.77), channel_id=1, source_target_pairs={{0,9},{1,8},{2,11},{3,10},{4,13},{5,12},{6,15},{7,14},{8,17},{9,16... | collective-permute-start | bytes 196616 | tf_op jit(solution)/shard_map/ppermute | solution.py:290
  60.8 1.6 %collective-permute-start.15 = (bf16[1,16,2048]{2,1,0:T(8,128)(2,1)S(1)}, bf16[1,16,2048]{2,1,0:T(8,128)(2,1)S(1)}, u32[]{:S(2)}, u32[]{:S(2)}) collective-permute-start(bf16[1,16,2048]{2,1,0:T(8,128)(2,1)S(1)} %get-tuple-element.78), channel_id=1, source_target_pairs={{0,17},{1,16},{2,19},{3,18},{4,21},{5,20},{6,23},{7,22},{8,25},{9,... | collective-permute-start | bytes 196616 | tf_op jit(solution)/shard_map/ppermute | solution.py:290
  62.4 3.3 %collective-permute-start.16 = (bf16[1,16,2048]{2,1,0:T(8,128)(2,1)S(1)}, bf16[1,16,2048]{2,1,0:T(8,128)(2,1)S(1)}, u32[]{:S(2)}, u32[]{:S(2)}) collective-permute-start(bf16[1,16,2048]{2,1,0:T(8,128)(2,1)S(1)} %get-tuple-element.79), channel_id=1, source_target_pairs={{0,25},{1,24},{2,27},{3,26},{4,29},{5,28},{6,31},{7,30},{8,1},{9,0... | collective-permute-start | bytes 196616 | tf_op jit(solution)/shard_map/ppermute | solution.py:290
  65.7 0.0 collective-permute-done.11.refs_1_
  65.7 0.0 slice-done
  65.7 0.0 slice-done.1
  65.7 0.0 copy-done.1
  65.7 0.0 copy-done.2
  65.7 2.4 %prepare.1 = (bf16[2048,1024]{1,0:T(8,128)(2,1)S(1)}, bf16[2048,1024]{1,0:T(8,128)(2,1)S(1)}, f32[16,2048]{1,0:T(8,128)S(1)}) custom-call(s32[1,2048]{1,0:T(1,128)S(1)} %bitcast.13, s32[1,2048]{1,0:T(1,128)S(1)} %bitcast.15, f32[1,16,2048]{2,1,0:T(8,128)S(1)} %fold.10.own_ref.refs_0_, f32[2048,1024]{1,0:T(8,128)S(1)} %bitcast.11), custom_call_target="tpu_custom_call" | custom-call | flops 8388608 | bytes 16777216 | tf_op jit(solution)/shard_map/prepare/pallas_call | solution.py:351
  68.2 0.0 collective-permute-done.13.refs_1_
  68.2 0.0 collective-permute-done.14.refs_2_
  68.2 0.2 collective-permute-done.15.refs_3_
  68.4 0.0 collective-permute-done.16.refs_4_
  68.4 2.4 %finish.1 = (f32[16,8,512]{2,1,0:T(8,128)}, f32[16,1024]{1,0:T(8,128)}) custom-call(s32[1,2048]{1,0:T(1,128)S(1)} %bitcast.14, s32[1,2048]{1,0:T(1,128)S(1)} %bitcast.16, f32[1,16,2048]{2,1,0:T(8,128)S(1)} %fold.10.own_ref.refs_0_, bf16[1,16,2048]{2,1,0:T(8,128)(2,1)S(1)} %collective-permute-done.13.refs_1_, ...), custom_call_target="tpu_custom_call" | custom-call | flops 1 | bytes 1 | tf_op jit(solution)/shard_map/finish/pallas_call | solution.py:419
  (4 shorter events, 0.1 us)
Async XLA Ops:
  0.6 10.6 %copy-start.5 = (f32[8]{0:T(128)S(1)}, f32[8]{0:T(128)}, u32[]{:S(2)}) copy-start(f32[8]{0:T(128)} %volume_ref.1) | copy-start | bytes 100
  0.6 1.4 %copy-start = (bf16[3,256,4,2,128]{4,3,2,1,0:T(2,128)(2,1)S(1)}, bf16[3,256,4,2,128]{4,3,2,1,0:T(2,128)(2,1)}, u32[]{:S(2)}) copy-start(bf16[3,256,4,2,128]{4,3,2,1,0:T(2,128)(2,1)} %param.7) | copy-start | bytes 4718596
  2.1 0.7 copy-start.4
  2.7 8.5 %copy-start.3 = (s32[4,2,128]{2,1,0:T(2,128)S(1)}, s32[4,2,128]{2,1,0:T(2,128)}, u32[]{:S(2)}) copy-start(s32[4,2,128]{2,1,0:T(2,128)} %param.8) | copy-start | bytes 12292
  3.9 22.5 %collective-permute-start.1 = (bf16[272,1536]{1,0:T(8,128)(2,1)S(1)}, bf16[272,1536]{1,0:T(8,128)(2,1)S(1)}, u32[]{:S(2)}, u32[]{:S(2)}) collective-permute-start(bf16[272,1536]{1,0:T(8,128)(2,1)S(1)} %get-tuple-element.44.after_ref.refs_0_), channel_id=1, source_target_pairs={{0,1},{1,0},{2,3},{3,2},{4,5},{5,4},{6,7},{7,6},{8,9},{9,8},{10,11... | collective-permute-start | bytes 2506760 | tf_op jit(solution)/shard_map/ppermute | solution.py:290
  7.5 4.3 %collective-permute-start = (bf16[256,1536]{1,0:T(8,128)(2,1)S(1)}, bf16[256,1536]{1,0:T(8,128)(2,1)S(1)}, u32[]{:S(2)}, u32[]{:S(2)}) collective-permute-start(bf16[256,1536]{1,0:T(8,128)(2,1)S(1)} %edge.2.after_ref.over_ref.here_ref.refs_1_), channel_id=1, source_target_pairs={{0,2},{2,4},{4,6},{6,8},{8,10},{10,12},{12,14},{14,16},{16,18},{18... | collective-permute-start | bytes 2359304 | tf_op jit(solution)/shard_map/ppermute | solution.py:454
  9.5 19.9 %collective-permute-start.2 = (bf16[256,1536]{1,0:T(8,128)(2,1)S(1)}, bf16[256,1536]{1,0:T(8,128)(2,1)S(1)}, u32[]{:S(2)}, u32[]{:S(2)}) collective-permute-start(bf16[256,1536]{1,0:T(8,128)(2,1)S(1)} %edge.3.after_ref.here_ref.under_ref.refs_0_), channel_id=1, source_target_pairs={{2,0},{4,2},{6,4},{8,6},{10,8},{12,10},{14,12},{16,14},{18,16},{20... | collective-permute-start | bytes 2359304 | tf_op jit(solution)/shard_map/ppermute | solution.py:455
  10.8 33.8 %collective-permute-start.4 = (bf16[256,1536]{1,0:T(8,128)(2,1)S(1)}, bf16[256,1536]{1,0:T(8,128)(2,1)S(1)}, u32[]{:S(2)}, u32[]{:S(2)}) collective-permute-start(bf16[256,1536]{1,0:T(8,128)(2,1)S(1)} %edge.3.after_ref.here_ref.under_ref.refs_0_), channel_id=1, source_target_pairs={{0,1},{1,0},{2,3},{3,2},{4,5},{5,4},{6,7},{7,6},{8,9},{9,8},{10,11... | collective-permute-start | bytes 2359304 | tf_op jit(solution)/shard_map/ppermute | solution.py:290
  36.3 3.6 %collective-permute-start.3 = (bf16[8,16,2048]{2,1,0:T(8,128)(2,1)S(1)}, bf16[8,16,2048]{2,1,0:T(8,128)(2,1)S(1)}, u32[]{:S(2)}, u32[]{:S(2)}) collective-permute-start(bf16[8,16,2048]{2,1,0:T(8,128)(2,1)S(1)} %get-tuple-element.49), channel_id=1, source_target_pairs={{0,2},{2,0},{4,6},{6,4},{8,10},{10,8},{12,14},{14,12},{16,18},{18,... | collective-permute-start | bytes 1572872 | tf_op jit(solution)/shard_map/ppermute | solution.py:290
  40.0 9.4 %collective-permute-start.5 = (bf16[4,16,2048]{2,1,0:T(8,128)(2,1)S(1)}, bf16[4,16,2048]{2,1,0:T(8,128)(2,1)S(1)}, u32[]{:S(2)}, u32[]{:S(2)}) collective-permute-start(bf16[4,16,2048]{2,1,0:T(8,128)(2,1)S(1)} %get-tuple-element.52), channel_id=1, source_target_pairs={{0,4},{2,6},{4,0},{6,2},{8,12},{10,14},{12,8},{14,10},{16,20},{18,... | collective-permute-start | bytes 786440 | tf_op jit(solution)/shard_map/ppermute | solution.py:290
  42.8 22.9 %slice-start = ((s8[8388608]{0:T(1024)(128)(4,1)}), s8[4194304]{0:T(1024)(128)(4,1)S(1)}, s32[]{:S(2)}) async-start(s8[8388608]{0:T(1024)(128)(4,1)} %bitcast.10), calls=%async_computation | async-start | bytes 8388608
  44.6 21.1 %slice-start.1 = ((s8[8388608]{0:T(1024)(128)(4,1)}), s8[4194304]{0:T(1024)(128)(4,1)S(1)}, s32[]{:S(2)}) async-start(s8[8388608]{0:T(1024)(128)(4,1)} %bitcast.10), calls=%async_computation.1 | async-start | bytes 8388608
  44.6 21.1 %copy-start.1 = (s32[2048]{0:T(1024)S(1)}, s32[2048]{0:T(1024)}, u32[]{:S(2)}) copy-start(s32[2048]{0:T(1024)} %param.11) | copy-start | bytes 24580
  44.6 21.1 %copy-start.2 = (s32[2048]{0:T(1024)S(1)}, s32[2048]{0:T(1024)}, u32[]{:S(2)}) copy-start(s32[2048]{0:T(1024)} %param.12) | copy-start | bytes 24580
  46.8 1.4 %collective-permute-start.6 = (bf16[8,16,512]{2,1,0:T(8,128)(2,1)S(1)}, bf16[8,16,512]{2,1,0:T(8,128)(2,1)S(1)}, u32[]{:S(2)}, u32[]{:S(2)}) collective-permute-start(bf16[8,16,512]{2,1,0:T(8,128)(2,1)S(1)} %get-tuple-element.58), channel_id=1, source_target_pairs={{0,2},{2,0},{4,6},{6,4},{8,10},{10,8},{12,14},{14,12},{16,18},{18,... | collective-permute-start | bytes 393224 | tf_op jit(solution)/shard_map/ppermute | solution.py:290
  46.9 1.5 %collective-permute-start.7 = (bf16[8,16,512]{2,1,0:T(8,128)(2,1)S(1)}, bf16[8,16,512]{2,1,0:T(8,128)(2,1)S(1)}, u32[]{:S(2)}, u32[]{:S(2)}) collective-permute-start(bf16[8,16,512]{2,1,0:T(8,128)(2,1)S(1)} %get-tuple-element.59), channel_id=1, source_target_pairs={{0,2},{2,0},{4,6},{6,4},{8,10},{10,8},{12,14},{14,12},{16,18},{18,... | collective-permute-start | bytes 393224 | tf_op jit(solution)/shard_map/ppermute | solution.py:290
  47.4 1.3 %collective-permute-start.8 = (bf16[8,16,512]{2,1,0:T(8,128)(2,1)S(1)}, bf16[8,16,512]{2,1,0:T(8,128)(2,1)S(1)}, u32[]{:S(2)}, u32[]{:S(2)}) collective-permute-start(bf16[8,16,512]{2,1,0:T(8,128)(2,1)S(1)} %get-tuple-element.60), channel_id=1, source_target_pairs={{0,2},{2,0},{4,6},{6,4},{8,10},{10,8},{12,14},{14,12},{16,18},{18,... | collective-permute-start | bytes 393224 | tf_op jit(solution)/shard_map/ppermute | solution.py:290
  47.4 1.5 %collective-permute-start.9 = (bf16[8,16,512]{2,1,0:T(8,128)(2,1)S(1)}, bf16[8,16,512]{2,1,0:T(8,128)(2,1)S(1)}, u32[]{:S(2)}, u32[]{:S(2)}) collective-permute-start(bf16[8,16,512]{2,1,0:T(8,128)(2,1)S(1)} %get-tuple-element.61), channel_id=1, source_target_pairs={{0,2},{2,0},{4,6},{6,4},{8,10},{10,8},{12,14},{14,12},{16,18},{18,... | collective-permute-start | bytes 393224 | tf_op jit(solution)/shard_map/ppermute | solution.py:290
  49.4 9.5 %collective-permute-start.12 = (bf16[4,16,2048]{2,1,0:T(8,128)(2,1)S(1)}, bf16[4,16,2048]{2,1,0:T(8,128)(2,1)S(1)}, u32[]{:S(2)}, u32[]{:S(2)}) collective-permute-start(bf16[4,16,2048]{2,1,0:T(8,128)(2,1)S(1)} %get-tuple-element.69), channel_id=1, source_target_pairs={{0,4},{2,6},{4,0},{6,2},{8,12},{10,14},{12,8},{14,10},{16,20},{18,... | collective-permute-start | bytes 786440 | tf_op jit(solution)/shard_map/ppermute | solution.py:290
  51.2 5.0 %collective-permute-start.10 = (bf16[2,16,2048]{2,1,0:T(8,128)(2,1)S(1)}, bf16[2,16,2048]{2,1,0:T(8,128)(2,1)S(1)}, u32[]{:S(2)}, u32[]{:S(2)}) collective-permute-start(bf16[2,16,2048]{2,1,0:T(8,128)(2,1)S(1)} %get-tuple-element.65), channel_id=1, source_target_pairs={{0,8},{2,10},{4,12},{6,14},{8,0},{10,2},{12,4},{14,6},{16,24},{18,... | collective-permute-start | bytes 393224 | tf_op jit(solution)/shard_map/ppermute | solution.py:290
  56.2 9.5 %collective-permute-start.11 = (bf16[1,16,2048]{2,1,0:T(8,128)(2,1)S(1)}, bf16[1,16,2048]{2,1,0:T(8,128)(2,1)S(1)}, u32[]{:S(2)}, u32[]{:S(2)}) collective-permute-start(bf16[1,16,2048]{2,1,0:T(8,128)(2,1)S(1)} %get-tuple-element.67), channel_id=1, source_target_pairs={{0,16},{2,18},{4,20},{6,22},{8,24},{10,26},{12,28},{14,30},{16,0},... | collective-permute-start | bytes 196616 | tf_op jit(solution)/shard_map/ppermute | solution.py:290
  58.9 9.3 %collective-permute-start.13 = (bf16[1,16,2048]{2,1,0:T(8,128)(2,1)S(1)}, bf16[1,16,2048]{2,1,0:T(8,128)(2,1)S(1)}, u32[]{:S(2)}, u32[]{:S(2)}) collective-permute-start(bf16[1,16,2048]{2,1,0:T(8,128)(2,1)S(1)} %get-tuple-element.76), channel_id=1, source_target_pairs={{0,1},{1,0},{2,3},{3,2},{4,5},{5,4},{6,7},{7,6},{8,9},{9,8},{10,11... | collective-permute-start | bytes 196616 | tf_op jit(solution)/shard_map/ppermute | solution.py:290
  59.5 8.7 %collective-permute-start.14 = (bf16[1,16,2048]{2,1,0:T(8,128)(2,1)S(1)}, bf16[1,16,2048]{2,1,0:T(8,128)(2,1)S(1)}, u32[]{:S(2)}, u32[]{:S(2)}) collective-permute-start(bf16[1,16,2048]{2,1,0:T(8,128)(2,1)S(1)} %get-tuple-element.77), channel_id=1, source_target_pairs={{0,9},{1,8},{2,11},{3,10},{4,13},{5,12},{6,15},{7,14},{8,17},{9,16... | collective-permute-start | bytes 196616 | tf_op jit(solution)/shard_map/ppermute | solution.py:290
  60.8 7.6 %collective-permute-start.15 = (bf16[1,16,2048]{2,1,0:T(8,128)(2,1)S(1)}, bf16[1,16,2048]{2,1,0:T(8,128)(2,1)S(1)}, u32[]{:S(2)}, u32[]{:S(2)}) collective-permute-start(bf16[1,16,2048]{2,1,0:T(8,128)(2,1)S(1)} %get-tuple-element.78), channel_id=1, source_target_pairs={{0,17},{1,16},{2,19},{3,18},{4,21},{5,20},{6,23},{7,22},{8,25},{9,... | collective-permute-start | bytes 196616 | tf_op jit(solution)/shard_map/ppermute | solution.py:290
  62.4 6.0 %collective-permute-start.16 = (bf16[1,16,2048]{2,1,0:T(8,128)(2,1)S(1)}, bf16[1,16,2048]{2,1,0:T(8,128)(2,1)S(1)}, u32[]{:S(2)}, u32[]{:S(2)}) collective-permute-start(bf16[1,16,2048]{2,1,0:T(8,128)(2,1)S(1)} %get-tuple-element.79), channel_id=1, source_target_pairs={{0,25},{1,24},{2,27},{3,26},{4,29},{5,28},{6,31},{7,30},{8,1},{9,0... | collective-permute-start | bytes 196616 | tf_op jit(solution)/shard_map/ppermute | solution.py:290
